TPU v7x, 32 devices: a whole 2x2x4 slice. The times are simulated.
32 devices in a mesh: groups: 2 (over y), row: 4 (over x, core), col: 4 (over z).
Axes of the slice: x: 2, y: 2, z: 4, core: 2. Of those that a mesh axis runs over, the one named last changes fastest.
Arguments:
- object_slab: float32 [2, 2, 2048, 2048], P(None, None, ('groups', 'row'), 'col'), parts along dimension 2, may hold values from -5 to 5
- probe_field: float32 [4, 256, 256], P('groups'), parts along dimension 0, may hold values from -6 to 6
- prop_phase: float32 [256, 256], replicated, may hold values from -3.140625 to 3.140625
- intensities: float32 [16, 1024, 256], P(('groups', 'row'), 'col'), parts along dimension 0, may hold values from 0.1 to 3
- corners: int32 [32, 4, 2], P(('groups', 'row'), 'col'), parts along dimension 0, may hold values from 0 to 256, as said below
- slot_source: int32 [16, 4], P(('groups', 'row'), 'col'), parts along dimension 0, may hold values from 0 to 3, as said below
Outputs:
- updated_slab: float32 [2, 2, 2048, 2048], P(None, None, ('groups', 'row'), 'col'), parts along dimension 2
- updated_probe: float32 [4, 256, 256], P('groups'), parts along dimension 0
There are 2 independent parts, one for each index of `groups`. A program takes and returns all parts, laid end to end along the dimension named above; an argument that names none is the same for every part. Nothing has to cross between parts.
Inputs may be any that keep to these rules, and one draw needn't show every extreme that they name: `corners`: entry [t * 4 + d, c] gives the row and column, within tile (t, c), of the patch that scan owner d of column c may take from that tile; the row is below 256, the column at most 256. `slot_source`: entry [d * 2 + k, c] is the tile row of column c that holds slot k of scan owner (d, c); one owner's 2 entries differ; in each column no tile row is named more than 4 times, and some tile row exactly 4 times.
All inputs are finite; a program needn't handle non-finite values.
Results may differ from a plain program's by a relative error of at most 0.015.
The roundings to bfloat16 on the way count: a program that leaves them out, or rounds other values in their place, can miss the bound.
Values may be sent and summed in bfloat16 or wider, within the bound.
No kernel may reach another device: no remote copies, remote signals or barrier semaphores. Data moves between devices by JAX's collectives and lax.ppermute only.
A program may use at most 128 MiB of HBM per device.

v0:
```python
import functools

import jax
import jax.numpy as jnp
import ml_dtypes
import numpy as np
from jax import lax
from jax.experimental import pallas as pl
from jax.experimental.pallas import tpu as pltpu
from jax.sharding import PartitionSpec as P

step_object = 0.05
step_probe = 0.5
SMALL_FLOPS = 2000000000
SMALL_VMEM = 8 * 1024 * 1024
LARGE_VMEM = 24 * 1024 * 1024
POSITIONS_AT_ONCE = 4


def permute_pairs(block, axis, partner):
    return lax.ppermute(block, axis, [(i, partner(i)) for i in range(lax.axis_size(axis))])


def from_behind(block, axis, distance):
    devices = range(lax.axis_size(axis))
    route = [(i - distance, i) for i in devices if i - distance in devices]
    return lax.ppermute(block, axis, route)


def dft_table(length):
    index = np.arange(length)
    angles = (index[:, None] * index[None, :] % length) * (2.0 * np.pi / length)
    scale_factor = 1.0 / np.sqrt(length)
    table_re = (np.cos(angles) * scale_factor).astype(np.float32).astype(ml_dtypes.bfloat16)
    table_im = (-np.sin(angles) * scale_factor).astype(np.float32).astype(ml_dtypes.bfloat16)
    return jnp.asarray(np.block([[table_re, -table_im], [table_im, table_re]]))


def product(a, b):
    return jnp.dot(a, b, preferred_element_type=jnp.float32)


def transform(table_ref, field_ref, middle_ref, out_ref, positions):
    n = field_ref.shape[1] // 2
    for p in positions:
        middle = product(table_ref[...], field_ref[p])
        middle_ref[p, :, n:] = middle[:n].astype(jnp.bfloat16)
        middle_ref[p, :, :n] = middle[n:].astype(jnp.bfloat16)
        out_ref[p] = product(middle_ref[p], table_ref[...])


def chunks(n):
    size = min(32, n)
    return [slice(a, a + size) for a in range(0, n, size)]


def put_forward(field_ref, p, rows, re, im):
    n = field_ref.shape[1] // 2
    field_ref[p, rows] = re.astype(jnp.bfloat16)
    field_ref[p, slice(n + rows.start, n + rows.stop)] = im.astype(jnp.bfloat16)


def put_backward(field_ref, p, rows, re, im):
    put_forward(field_ref, p, rows, im, re)


def get_forward(out_ref, p, rows):
    n = out_ref.shape[1]
    return out_ref[p, rows, n:], out_ref[p, rows, :n]


def get_backward(out_ref, p, rows):
    n = out_ref.shape[1]
    return out_ref[p, rows, :n], out_ref[p, rows, n:]


def one_hot_rows(shape, offset):
    rows = lax.broadcasted_iota(jnp.int32, shape, 0)
    columns = lax.broadcasted_iota(jnp.int32, shape, 1)
    return (columns == rows + offset).astype(jnp.bfloat16)


def one_hot_columns(shape, offset):
    rows = lax.broadcasted_iota(jnp.int32, shape, 0)
    columns = lax.broadcasted_iota(jnp.int32, shape, 1)
    return (rows == columns + offset).astype(jnp.bfloat16)


def spot(corner_ref, position):
    return corner_ref[position, 0, :1, :1], corner_ref[position, 1, :1, :1]


def cut(own_ref, rim_ref, patch_ref, corner_ref, base, count):
    n = patch_ref.shape[2]
    height = own_ref.shape[1] + rim_ref.shape[1]
    width = own_ref.shape[2]
    planes = jnp.concatenate([jnp.concatenate([own_ref[c], rim_ref[c]], 0) for c in range(2)], 1)
    for p in range(count):
        corner_y, corner_x = spot(corner_ref, base + p)
        rows = product(one_hot_rows((n, height), corner_y), planes).astype(jnp.bfloat16)
        rows = jnp.concatenate([rows[:, :width], rows[:, width:]], 0)
        both = product(rows, one_hot_columns((width, n), corner_x)).astype(jnp.bfloat16)
        patch_ref[p, 0] = both[:n]
        patch_ref[p, 1] = both[n:]


def pair(ref, p, rows):
    return ref[p, 0, rows].astype(jnp.float32), ref[p, 1, rows].astype(jnp.float32)


def first_prep_kernel(slab_ref, own_ref, wide_ref, sems):
    planes = own_ref.shape[0]
    copies = [pltpu.make_async_copy(slab_ref.at[c], wide_ref.at[c], sems.at[c]) for c in range(planes)]
    for copy in copies:
        copy.start()
    for c, copy in enumerate(copies):
        copy.wait()
        own_ref[c] = wide_ref[c].astype(jnp.bfloat16)


def second_prep_kernel(source_ref, slab_hbm, intensity_ref, own_ref, *rest):
    message_refs, wide_ref, sem = rest[:-2], rest[-2], rest[-1]
    copy = pltpu.make_async_copy(slab_hbm.at[pl.ds(own_ref.shape[0], own_ref.shape[0])], wide_ref, sem)
    copy.start()
    for s, message_ref in enumerate(message_refs):
        target = lax.axis_index("row") ^ s
        slot = jnp.int32(-1)
        for k in range(intensity_ref.shape[0]):
            slot = jnp.where(source_ref[k] == target, k, slot)
        chosen = intensity_ref[jnp.maximum(slot, 0)]
        message_ref[...] = jnp.where(slot >= 0, chosen, -1.0).astype(jnp.bfloat16)
    copy.wait()
    own_ref[...] = wide_ref[...].astype(jnp.bfloat16)


def third_prep_kernel(corner_ref, phase_ref, table_hbm, table_ref, kernel_ref, spot_ref, sem):
    copy = pltpu.make_async_copy(table_hbm, table_ref, sem)
    copy.start()
    for p in range(spot_ref.shape[0]):
        owner = lax.axis_index("row") ^ p
        for k in range(2):
            spot_ref[p, k] = jnp.full(spot_ref.shape[2:], corner_ref[owner, k], jnp.int32)
    for rows in chunks(phase_ref.shape[0]):
        kernel_ref[0, rows] = jnp.cos(phase_ref[rows])
        kernel_ref[1, rows] = jnp.sin(phase_ref[rows])
    copy.wait()


def first_kernel(
    corner_ref, own_ref, rim_ref, probe_ref, kernel_ref, table_ref, patch_ref, moved_ref,
    field_ref, middle_ref, out_ref,
):
    count, _, n, _ = patch_ref.shape
    cut(own_ref, rim_ref, patch_ref, corner_ref, pl.program_id(0) * count, count)
    for p in range(count):
        for rows in chunks(n):
            q_re, q_im = probe_ref[0, rows], probe_ref[1, rows]
            o_re, o_im = pair(patch_ref, p, rows)
            put_forward(field_ref, p, rows, q_re * o_re - q_im * o_im, q_re * o_im + q_im * o_re)
    transform(table_ref, field_ref, middle_ref, out_ref, range(count))
    for p in range(count):
        for rows in chunks(n):
            k_re, k_im = kernel_ref[0, rows], kernel_ref[1, rows]
            r, i = get_forward(out_ref, p, rows)
            put_backward(field_ref, p, rows, k_re * r - k_im * i, k_re * i + k_im * r)
    transform(table_ref, field_ref, middle_ref, moved_ref, range(count))


def second_kernel(
    corner_ref, own_ref, rim_ref, moved_ref, table_ref, patch_ref, far_ref, field_ref, middle_ref
):
    count, _, n, _ = patch_ref.shape
    cut(own_ref, rim_ref, patch_ref, corner_ref, pl.program_id(0) * count, count)
    for p in range(count):
        for rows in chunks(n):
            m_re, m_im = get_backward(moved_ref, p, rows)
            o_re, o_im = pair(patch_ref, p, rows)
            put_forward(field_ref, p, rows, m_re * o_re - m_im * o_im, m_re * o_im + m_im * o_re)
    transform(table_ref, field_ref, middle_ref, far_ref, range(count))


def third_kernel(corner_ref, probe_ref, kernel_ref, table_ref, zero_ref, one_ref, moved_ref, far_ref, *rest):
    measured_refs = rest[:-9]
    grad_ref, rim_ref, keep_ref, send_ref, probe_grad_ref, measured_ref = rest[-9:-3]
    field_ref, middle_ref, out_ref = rest[-3:]
    count, _, n, _ = zero_ref.shape
    planes = grad_ref.shape[0]
    base = pl.program_id(0) * count
    last = pl.program_id(0) == pl.num_programs(0) - 1

    @pl.when(pl.program_id(0) == 0)
    def _():
        for s, ref in enumerate(measured_refs):
            measured_ref[s] = ref[...]
        probe_grad_ref[...] = jnp.zeros_like(probe_grad_ref)

    for p in range(count):
        for rows in chunks(n):
            f_re, f_im = get_forward(far_ref, p, rows)
            measured = measured_ref[base + p, rows].astype(jnp.float32)
            misfit = jnp.where(measured < 0.0, 0.0, f_re * f_re + f_im * f_im - measured)
            put_backward(field_ref, p, rows, misfit * f_re, misfit * f_im)
    transform(table_ref, field_ref, middle_ref, out_ref, range(count))
    for p in range(count):
        for rows in chunks(n):
            b_re, b_im = get_backward(out_ref, p, rows)
            m_re, m_im = get_backward(moved_ref, p, rows)
            o_re, o_im = pair(one_ref, p, rows)
            grad_ref[2, base + p, rows] = (m_re * b_re + m_im * b_im).astype(jnp.bfloat16)
            grad_ref[3, base + p, rows] = (m_re * b_im - m_im * b_re).astype(jnp.bfloat16)
            put_forward(field_ref, p, rows, o_re * b_re + o_im * b_im, o_re * b_im - o_im * b_re)
    transform(table_ref, field_ref, middle_ref, out_ref, range(count))
    for p in range(count):
        for rows in chunks(n):
            k_re, k_im = kernel_ref[0, rows], kernel_ref[1, rows]
            r, i = get_forward(out_ref, p, rows)
            put_backward(field_ref, p, rows, k_re * r + k_im * i, k_re * i - k_im * r)
    transform(table_ref, field_ref, middle_ref, out_ref, range(count))
    for rows in chunks(n):
        total_re, total_im = probe_grad_ref[0, rows], probe_grad_ref[1, rows]
        q_re, q_im = probe_ref[0, rows], probe_ref[1, rows]
        for p in range(count):
            b_re, b_im = get_backward(out_ref, p, rows)
            o_re, o_im = pair(zero_ref, p, rows)
            grad_ref[0, base + p, rows] = (q_re * b_re + q_im * b_im).astype(jnp.bfloat16)
            grad_ref[1, base + p, rows] = (q_re * b_im - q_im * b_re).astype(jnp.bfloat16)
            total_re += o_re * b_re + o_im * b_im
            total_im += o_re * b_im - o_im * b_re
        probe_grad_ref[0, rows] = total_re
        probe_grad_ref[1, rows] = total_im

    @pl.when(last)
    def _():
        core = lax.axis_index("row") % 2
        keep_ref[...] = probe_grad_ref[core]
        send_ref[...] = probe_grad_ref[1 - core].astype(jnp.bfloat16)
        rows, width = rim_ref.shape[1:]
        moves, tall = placements(corner_ref, grad_ref.shape[1], n, width, rows, rows)
        for plane in range(planes):
            rim_ref[plane] = placed(grad_ref, plane, moves, tall).astype(jnp.bfloat16)


def placements(corner_ref, positions, n, width, rows, first_row):
    moves, tall = [], []
    for p in range(positions):
        corner_y, corner_x = spot(corner_ref, p)
        moves.append(one_hot_rows((n, width), corner_x))
        tall.append(one_hot_columns((rows, n), corner_y - first_row))
    return moves, jnp.concatenate(tall, 1)


def placed(grad_ref, plane, moves, tall):
    wide = [product(grad_ref[plane, p], move).astype(jnp.bfloat16) for p, move in enumerate(moves)]
    return product(tall, jnp.concatenate(wide, 0))


def place_kernel(corner_ref, grad_ref, slab_ref, part_ref):
    rows, width = part_ref.shape[1:]
    moves, tall = placements(corner_ref, grad_ref.shape[1], grad_ref.shape[2], width, rows, 0)
    for plane in range(grad_ref.shape[0]):
        part_ref[plane] = slab_ref[plane] - step_object * placed(grad_ref, plane, moves, tall)


def in_hbm(array):
    return pltpu.with_memory_space_constraint(array, pltpu.HBM)


def finish_kernel(part_ref, rim_ref, out_ref):
    rows = rim_ref.shape[1]
    out_ref[:, :rows] = part_ref[:, :rows] - step_object * rim_ref[...].astype(jnp.float32)
    if rows < part_ref.shape[1]:
        out_ref[:, rows:] = part_ref[:, rows:]


def whole(shape):
    return pl.BlockSpec(shape, lambda *_: (0,) * len(shape))


def per_position(shape):
    return pl.BlockSpec(shape, lambda i, *_: (i,) + (0,) * (len(shape) - 1))


def half_sum_kernel(keep_ref, other_ref, mine_ref, *rest):
    send_refs, total_ref = rest[:-1], rest[-1]
    chip = lax.axis_index("row") // 2
    piece = mine_ref.shape[0]
    total_ref[...] = keep_ref[...] + other_ref[...].astype(jnp.float32)
    mine_ref[...] = total_ref[pl.ds(pl.multiple_of(chip * piece, piece), piece)]
    for s, send_ref in enumerate(send_refs, 1):
        rows = pl.ds(pl.multiple_of((chip ^ s) * piece, piece), piece)
        send_ref[...] = total_ref[rows].astype(jnp.bfloat16)


def row_sum_kernel(mine_ref, *rest):
    other_refs, total_ref, send_ref = rest[:-2], rest[-2], rest[-1]
    total = mine_ref[...]
    for other_ref in other_refs:
        total += other_ref[...].astype(jnp.float32)
    total_ref[...] = total
    send_ref[...] = total.astype(jnp.bfloat16)


def full_sum_kernel(mine_ref, *rest):
    other_refs, total_ref = rest[:-1], rest[-1]
    total = mine_ref[...]
    for other_ref in other_refs:
        total += other_ref[...].astype(jnp.float32)
    total_ref[...] = total.astype(jnp.bfloat16)


def gather_kernel(mine_ref, *rest):
    other_refs, half_ref = rest[:-1], rest[-1]
    chip = lax.axis_index("row") // 2
    piece = mine_ref.shape[0]
    for s, ref in enumerate((mine_ref,) + other_refs):
        half_ref[pl.ds(pl.multiple_of((chip ^ s) * piece, piece), piece)] = ref[...]


def probe_kernel(probe_ref, mine_ref, other_ref, out_ref, *, scale):
    core = lax.axis_index("row") % 2
    out_ref[core] = probe_ref[core] - scale * mine_ref[...].astype(jnp.float32)
    out_ref[1 - core] = probe_ref[1 - core] - scale * other_ref[...].astype(jnp.float32)


def small_call(body, arrays, out_shape, name, scratch=()):
    return pl.pallas_call(
        body,
        in_specs=[pl.BlockSpec(memory_space=pltpu.VMEM)] * len(arrays),
        out_specs=[pl.BlockSpec(memory_space=pltpu.VMEM)] * len(out_shape),
        out_shape=out_shape,
        scratch_shapes=scratch,
        compiler_params=pltpu.CompilerParams(vmem_limit_bytes=SMALL_VMEM),
        cost_estimate=pl.CostEstimate(flops=SMALL_FLOPS, bytes_accessed=2**18, transcendentals=0),
        name=name,
    )(*arrays)


def probe_sum(keep, send, part):
    n = keep.shape[0]
    row_count, col_count = lax.axis_size("row"), lax.axis_size("col")
    chips = row_count // 2
    shape = (n // chips, n)
    wide, narrow = jax.ShapeDtypeStruct(shape, jnp.float32), jax.ShapeDtypeStruct(shape, jnp.bfloat16)
    other = permute_pairs(send, "row", lambda i: i ^ 1)
    mine, *sends = small_call(
        half_sum_kernel, [keep, other], [wide] + [narrow] * (chips - 1), "half_sum", [pltpu.VMEM((n, n), jnp.float32)]
    )
    others = [permute_pairs(sends[s - 1], "row", lambda i: i ^ (2 * s)) for s in range(1, chips)]
    total, send = small_call(row_sum_kernel, [mine, *others], [wide, narrow], "row_sum")
    others = [permute_pairs(send, "col", lambda i: i ^ s) for s in range(col_count - 1, 0, -1)]
    others, part = lax.optimization_barrier((others, part))
    (total,) = small_call(full_sum_kernel, [total, *others], [narrow], "full_sum")
    others = [permute_pairs(total, "row", lambda i: i ^ (2 * s)) for s in range(1, chips)]
    half = jax.ShapeDtypeStruct((n, n), jnp.bfloat16)
    (mine,) = small_call(gather_kernel, [total, *others], [half], "gather_half")
    return mine, permute_pairs(mine, "row", lambda i: i ^ 1), part


def per_device(object_slab, probe_field, prop_phase, intensities, corners, slot_source):
    slice_count, pair_count, height, width = object_slab.shape
    n = probe_field.shape[-1]
    row_count = lax.axis_size("row")
    col_count = lax.axis_size("col")
    slot_count = intensities.shape[0]
    me = lax.axis_index("row")

    planes = slice_count * pair_count
    slab = object_slab.reshape(planes, height, width)
    sources = slot_source.reshape(slot_count)
    smem = pl.BlockSpec(memory_space=pltpu.SMEM)
    hbm = pl.BlockSpec(memory_space=pltpu.HBM)
    vmem = pl.BlockSpec(memory_space=pltpu.VMEM)
    small = row_count <= POSITIONS_AT_ONCE

    def kept(shape, kind):
        return pltpu.VMEM(shape, kind) if small else jax.ShapeDtypeStruct(shape, kind)

    def near(array):
        return pltpu.with_memory_space_constraint(array, pltpu.VMEM) if small else array

    tile = (pair_count, height, width)
    own_zero = pl.pallas_call(
        first_prep_kernel,
        in_specs=[hbm],
        out_specs=vmem,
        out_shape=kept(tile, jnp.bfloat16),
        scratch_shapes=[pltpu.VMEM(tile, jnp.float32), pltpu.SemaphoreType.DMA((pair_count,))],
        compiler_params=pltpu.CompilerParams(vmem_limit_bytes=SMALL_VMEM),
        name="prepare_zero",
    )(in_hbm(slab))
    rim_zero = from_behind(own_zero[:, :n], "row", -1)
    own_one, *messages = pl.pallas_call(
        second_prep_kernel,
        in_specs=[smem, hbm, vmem],
        out_specs=[vmem] * (1 + row_count),
        out_shape=[kept(tile, jnp.bfloat16)] + [kept((n, n), jnp.bfloat16)] * row_count,
        scratch_shapes=[pltpu.VMEM(tile, jnp.float32), pltpu.SemaphoreType.DMA],
        compiler_params=pltpu.CompilerParams(vmem_limit_bytes=SMALL_VMEM),
        name="prepare_one",
    )(sources, in_hbm(slab), intensities)
    table, kernel, spots = pl.pallas_call(
        third_prep_kernel,
        in_specs=[smem, vmem, hbm],
        out_specs=[vmem] * 3,
        out_shape=[
            kept((2 * n, 2 * n), jnp.bfloat16),
            kept((2, n, n), jnp.float32),
            kept((row_count, 2, 8, 128), jnp.int32),
        ],
        scratch_shapes=[pltpu.SemaphoreType.DMA],
        compiler_params=pltpu.CompilerParams(vmem_limit_bytes=SMALL_VMEM),
        name="prepare_two",
    )(corners.reshape(row_count, 2), prop_phase, in_hbm(dft_table(n)))
    rim_one = from_behind(own_one[:, :n], "row", -1)
    measured = [messages[0]]
    for s in range(1, row_count):
        measured.append(permute_pairs(messages[s], "row", lambda i: i ^ s))

    count = min(POSITIONS_AT_ONCE, row_count)
    plane = (2, n, n)
    positions = (row_count, 2, n, n)
    block = per_position((count, 2, n, n))
    own_block, rim_block, tables = whole(tile), whole((pair_count, n, width)), whole((2 * n, 2 * n))
    wide = (row_count, n, 2 * n)
    wide_block = per_position((count, n, 2 * n))
    work = [
        pltpu.VMEM((count, 2 * n, n), jnp.bfloat16),
        pltpu.VMEM((count, n, 2 * n), jnp.bfloat16),
        pltpu.VMEM((count, n, 2 * n), jnp.float32),
    ]
    unit = 2 * n * n * n

    def call(body, in_specs, out_specs, out_shape, units, name, scratch=(), steps=row_count // count):
        return pl.pallas_call(
            body,
            grid=(steps,),
            in_specs=[whole((row_count, 2, 8, 128))] + in_specs,
            out_specs=out_specs,
            scratch_shapes=scratch,
            out_shape=out_shape,
            compiler_params=pltpu.CompilerParams(vmem_limit_bytes=LARGE_VMEM),
            cost_estimate=pl.CostEstimate(
                flops=row_count * units * unit, bytes_accessed=2**21, transcendentals=0
            ),
            name=name,
        )

    patch_zero, moved = call(
        first_kernel,
        [own_block, rim_block, whole(plane), whole(plane), tables],
        [block, wide_block],
        [kept(positions, jnp.bfloat16), kept(wide, jnp.float32)],
        28,
        "moved",
        scratch=work,
    )(near(spots), near(own_zero), near(rim_zero), probe_field, near(kernel), near(table))
    patch_one, far = call(
        second_kernel,
        [own_block, rim_block, wide_block, tables],
        [block, wide_block],
        [kept(positions, jnp.bfloat16), kept(wide, jnp.float32)],
        20,
        "far",
        scratch=work[:2],
    )(near(spots), near(own_one), near(rim_one), near(moved), near(table))
    grad_shape = (planes, row_count, n, n)
    grads, rim_grad, keep, send = call(
        third_kernel,
        [whole(plane), whole(plane), tables, block, block, wide_block, wide_block] + [whole((n, n))] * row_count,
        [whole(grad_shape), whole((planes, n, width)), whole((n, n)), whole((n, n))],
        [
            kept(grad_shape, jnp.bfloat16),
            kept((planes, n, width), jnp.bfloat16),
            kept((n, n), jnp.float32),
            kept((n, n), jnp.bfloat16),
        ],
        40,
        "gradients",
        scratch=[pltpu.VMEM(plane, jnp.float32), pltpu.VMEM((row_count, n, n), jnp.bfloat16)] + work,
    )(
        near(spots), probe_field, near(kernel), near(table), near(patch_zero), near(patch_one), near(moved), near(far),
        *[near(array) for array in measured],
    )
    (part,) = call(
        place_kernel,
        [whole(grad_shape), whole((planes, height, width))],
        [whole((planes, height, width))],
        [kept((planes, height, width), jnp.float32)],
        16,
        "place",
        steps=1,
    )(near(spots), near(grads), slab)

    rim_grad = from_behind(rim_grad, "row", 1)
    mine, other, part = probe_sum(keep, send, part)
    updated_slab = pl.pallas_call(
        finish_kernel,
        grid=(planes,),
        in_specs=[
            pl.BlockSpec((1, height, width), lambda i: (i, 0, 0)),
            pl.BlockSpec((1, n, width), lambda i: (i, 0, 0)),
        ],
        out_specs=pl.BlockSpec((1, height, width), lambda i: (i, 0, 0)),
        out_shape=jax.ShapeDtypeStruct((planes, height, width), jnp.float32),
        compiler_params=pltpu.CompilerParams(vmem_limit_bytes=SMALL_VMEM),
        name="finish",
    )(near(part), near(rim_grad)).reshape(object_slab.shape)
    (updated_probe,) = small_call(
        functools.partial(probe_kernel, scale=step_probe / (row_count * col_count * slot_count)),
        [probe_field, mine, other],
        [jax.ShapeDtypeStruct(probe_field.shape, jnp.float32)],
        "update_probe",
    )
    return (updated_slab, updated_probe)


def solution(mesh):
    placed = (
        P(None, None, ("groups", "row"), "col"),
        P("groups", None, None),
        P(),
        P(("groups", "row"), "col", None),
        P(("groups", "row"), "col", None),
        P(("groups", "row"), "col"),
    )
    return jax.shard_map(
        per_device,
        mesh=mesh,
        in_specs=placed,
        out_specs=(P(None, None, ("groups", "row"), "col"), P("groups", None, None)),
        check_vma=False,
    )
```

profile of v0, /device:TPU:0, one launch (start us, length us, event | category | flops | bytes accessed | tf_op | source)
XLA Modules:
  0.0 58.6 jit_solution(15836570039226303579)
XLA Ops:
  0.6 0.0 copy-start.3
  0.6 0.0 copy-start.1
  0.7 0.0 copy-start.5
  0.7 0.0 copy-start.2
  0.7 1.3 %prepare_zero.1.own_ref = bf16[2,256,512]{2,1,0:T(8,128)(2,1)S(1)} custom-call(f32[4,256,512]{2,1,0:T(8,128)} %bitcast.4), custom_call_target="tpu_custom_call" | custom-call | tf_op jit(solution)/shard_map/prepare_zero/pallas_call | solution.py:382
  2.0 0.0 copy-start.4
  2.0 1.4 %collective-permute-start = (bf16[2,256,512]{2,1,0:T(8,128)(2,1)S(1)}, bf16[2,256,512]{2,1,0:T(8,128)(2,1)S(1)}, u32[]{:S(2)}, u32[]{:S(2)}) collective-permute-start(bf16[2,256,512]{2,1,0:T(8,128)(2,1)S(1)} %prepare_zero.1.own_ref), channel_id=1, source_target_pairs={{4,0},{8,4},{12,8},{5,1},{9,5},{13,9},{6,2},{10,6},{14,10},{7,3},{... | collective-permute-start | bytes 1572872 | tf_op jit(solution)/shard_map/ppermute | solution.py:27
  3.4 0.0 copy-done.3
  3.4 0.0 copy-done.1
  3.5 2.4 %prepare_one.1 = (bf16[2,256,512]{2,1,0:T(8,128)(2,1)S(1)}, bf16[256,256]{1,0:T(8,128)(2,1)S(1)}, bf16[256,256]{1,0:T(8,128)(2,1)}, bf16[256,256]{1,0:T(8,128)(2,1)S(1)}, bf16[256,256]{1,0:T(8,128)(2,1)S(1)}) custom-call(s32[2]{0:T(128)S(1)} %bitcast.7, f32[4,256,512]{2,1,0:T(8,128)} %bitcast.5, f32[2,256,256]{2,1,0:T(8,128)S(1)} %copy-done.1), custom_call_target="tpu_custom_call" | custom-call | tf_op jit(solution)/shard_map/prepare_one/pallas_call | solution.py:392
  5.9 1.3 %collective-permute-start.1 = (bf16[2,256,512]{2,1,0:T(8,128)(2,1)S(1)}, bf16[2,256,512]{2,1,0:T(8,128)(2,1)S(1)}, u32[]{:S(2)}, u32[]{:S(2)}) collective-permute-start(bf16[2,256,512]{2,1,0:T(8,128)(2,1)S(1)} %get-tuple-element.30.own_ref), channel_id=1, source_target_pairs={{4,0},{8,4},{12,8},{5,1},{9,5},{13,9},{6,2},{10,6},{14,10},{7,3},{... | collective-permute-start | bytes 1572872 | tf_op jit(solution)/shard_map/ppermute | solution.py:27
  7.2 1.8 %collective-permute-start.2 = (bf16[256,256]{1,0:T(8,128)(2,1)}, bf16[256,256]{1,0:T(8,128)(2,1)S(1)}, u32[]{:S(2)}, u32[]{:S(2)}) collective-permute-start(bf16[256,256]{1,0:T(8,128)(2,1)} %get-tuple-element.35), channel_id=1, source_target_pairs={{0,4},{4,0},{8,12},{12,8},{1,5},{5,1},{9,13},{13,9},{2,6},{6,2},{1... | collective-permute-start | bytes 393224 | tf_op jit(solution)/shard_map/ppermute | solution.py:21
  9.0 3.0 %collective-permute-start.3 = (bf16[256,256]{1,0:T(8,128)(2,1)S(1)}, bf16[256,256]{1,0:T(8,128)(2,1)S(1)}, u32[]{:S(2)}, u32[]{:S(2)}) collective-permute-start(bf16[256,256]{1,0:T(8,128)(2,1)S(1)} %get-tuple-element.36), channel_id=1, source_target_pairs={{0,8},{4,12},{8,0},{12,4},{1,9},{5,13},{9,1},{13,5},{2,10},{6,14},... | collective-permute-start | bytes 393224 | tf_op jit(solution)/shard_map/ppermute | solution.py:21
  12.0 0.0 collective-permute-start.4
  12.0 0.0 copy-done.5
  12.0 0.1 copy.9.corner_ref
  12.1 0.0 copy-done.2
  12.1 2.2 %prepare_two.1 = (bf16[512,512]{1,0:T(8,128)(2,1)S(1)}, f32[2,256,256]{2,1,0:T(8,128)S(1)}, s32[4,2,8,128]{3,2,1,0:T(8,128)S(1)}) custom-call(s32[4,2]{1,0:T(4,128)S(1)} %copy.9.corner_ref, f32[256,256]{1,0:T(8,128)S(1)} %copy-done.2, bf16[512,512]{1,0:T(8,128)(2,1)} %constant.2.clone.table_hbm), custom_call_target="tpu_custom_call" | custom-call | tf_op jit(solution)/shard_map/prepare_two/pallas_call | solution.py:401
  14.3 0.0 collective-permute-done.rim_ref
  14.3 0.0 copy-done.4
  14.4 4.9 %moved.1 = (bf16[4,2,256,256]{3,2,1,0:T(8,128)(2,1)S(1)}, f32[4,256,512]{2,1,0:T(8,128)S(1)}) custom-call(s32[4,2,8,128]{3,2,1,0:T(8,128)S(1)} %get-tuple-element.26.corner_ref, bf16[2,256,512]{2,1,0:T(8,128)(2,1)S(1)} %prepare_zero.1.own_ref, bf16[2,256,512]{2,1,0:T(8,128)(2,1)S(1)} %collective-permute-done.rim_ref, f32[2,256,256]{2,1,0:T(8,128)S(1)} %copy-done.4, ...), custom_call_target="tpu_custom_call" | custom-call | flops 3758096384 | bytes 2097152 | tf_op jit(solution)/shard_map/moved/pallas_call | solution.py:448
  19.2 0.0 collective-permute-done.1.rim_ref
  19.2 3.6 %far.1 = (bf16[4,2,256,256]{3,2,1,0:T(8,128)(2,1)S(1)}, f32[4,256,512]{2,1,0:T(8,128)S(1)}) custom-call(s32[4,2,8,128]{3,2,1,0:T(8,128)S(1)} %get-tuple-element.26.corner_ref, bf16[2,256,512]{2,1,0:T(8,128)(2,1)S(1)} %get-tuple-element.30.own_ref, bf16[2,256,512]{2,1,0:T(8,128)(2,1)S(1)} %collective-permute-done.1.rim_ref, ...), custom_call_target="tpu_custom_call" | custom-call | flops 2684354560 | bytes 2097152 | tf_op jit(solution)/shard_map/far/pallas_call | solution.py:457
  22.9 0.0 collective-permute-done.2.rest_1_
  22.9 1.1 %collective-permute-done.3.rest_2_ = bf16[256,256]{1,0:T(8,128)(2,1)S(1)} collective-permute-done((bf16[256,256]{1,0:T(8,128)(2,1)S(1)}, bf16[256,256]{1,0:T(8,128)(2,1)S(1)}, u32[]{:S(2)}, u32[]{:S(2)}) %collective-permute-start.3) | collective-permute-done | bytes 131104 | tf_op jit(solution)/shard_map/ppermute | solution.py:21
  24.0 0.0 collective-permute-done.4.rest_3_
  24.0 8.2 %gradients.1 = (bf16[4,4,256,256]{3,2,1,0:T(8,128)(2,1)S(1)}, bf16[4,256,512]{2,1,0:T(8,128)(2,1)S(1)}, f32[256,256]{1,0:T(8,128)S(1)}, bf16[256,256]{1,0:T(8,128)(2,1)S(1)}) custom-call(s32[4,2,8,128]{3,2,1,0:T(8,128)S(1)} %get-tuple-element.26.corner_ref, f32[2,256,256]{2,1,0:T(8,128)S(1)} %copy-done.4, f32[2,256,256]{2,1,0:T(8,128)S(1)} %get-tuple-element.27.kernel_ref, ...), custom_call_target="tpu_custom_call" | custom-call | flops 5368709120 | bytes 2097152 | tf_op jit(solution)/shard_map/gradients/pallas_call | solution.py:467
  32.2 2.2 %collective-permute-start.5 = (bf16[256,256]{1,0:T(8,128)(2,1)S(1)}, bf16[256,256]{1,0:T(8,128)(2,1)S(1)}, u32[]{:S(2)}, u32[]{:S(2)}) collective-permute-start(bf16[256,256]{1,0:T(8,128)(2,1)S(1)} %get-tuple-element.39), channel_id=1, source_target_pairs={{0,4},{4,0},{8,12},{12,8},{1,5},{5,1},{9,13},{13,9},{2,6},{6,2},{1... | collective-permute-start | bytes 393224 | tf_op jit(solution)/shard_map/ppermute | solution.py:21
  34.3 1.0 %collective-permute-done.5.other_ref = bf16[256,256]{1,0:T(8,128)(2,1)S(1)} collective-permute-done((bf16[256,256]{1,0:T(8,128)(2,1)S(1)}, bf16[256,256]{1,0:T(8,128)(2,1)S(1)}, u32[]{:S(2)}, u32[]{:S(2)}) %collective-permute-start.5) | collective-permute-done | bytes 131104 | tf_op jit(solution)/shard_map/ppermute | solution.py:21
  35.4 0.1 collective-permute-start.6
  35.5 2.3 %collective-permute-start.10 = (bf16[4,256,512]{2,1,0:T(8,128)(2,1)S(1)}, bf16[4,256,512]{2,1,0:T(8,128)(2,1)S(1)}, u32[]{:S(2)}, u32[]{:S(2)}) collective-permute-start(bf16[4,256,512]{2,1,0:T(8,128)(2,1)S(1)} %get-tuple-element.45), channel_id=1, source_target_pairs={{0,4},{4,8},{8,12},{1,5},{5,9},{9,13},{2,6},{6,10},{10,14},{3,7},{... | collective-permute-start | bytes 3145736 | tf_op jit(solution)/shard_map/ppermute | solution.py:27
  37.8 2.0 %collective-permute-done.6.rest_0_ = bf16[128,256]{1,0:T(8,128)(2,1)S(1)} collective-permute-done((bf16[128,256]{1,0:T(8,128)(2,1)S(1)}, bf16[128,256]{1,0:T(8,128)(2,1)S(1)}, u32[]{:S(2)}, u32[]{:S(2)}) %collective-permute-start.6) | collective-permute-done | bytes 65568 | tf_op jit(solution)/shard_map/ppermute | solution.py:21
  39.8 0.0 copy-start
  39.8 1.6 %collective-permute-start.9 = (bf16[128,256]{1,0:T(8,128)(2,1)S(1)}, bf16[128,256]{1,0:T(8,128)(2,1)S(1)}, u32[]{:S(2)}, u32[]{:S(2)}) collective-permute-start(bf16[128,256]{1,0:T(8,128)(2,1)S(1)} %get-tuple-element.42), channel_id=1, source_target_pairs={{0,1},{1,0},{2,3},{3,2},{4,5},{5,4},{6,7},{7,6},{8,9},{9,8},{10,11... | collective-permute-start | bytes 196616 | tf_op jit(solution)/shard_map/ppermute | solution.py:21
  41.5 2.6 %collective-permute-start.8 = (bf16[128,256]{1,0:T(8,128)(2,1)S(1)}, bf16[128,256]{1,0:T(8,128)(2,1)S(1)}, u32[]{:S(2)}, u32[]{:S(2)}) collective-permute-start(bf16[128,256]{1,0:T(8,128)(2,1)S(1)} %get-tuple-element.42), channel_id=1, source_target_pairs={{0,2},{1,3},{2,0},{3,1},{4,6},{5,7},{6,4},{7,5},{8,10},{9,11},{10,... | collective-permute-start | bytes 196616 | tf_op jit(solution)/shard_map/ppermute | solution.py:21
  44.0 0.2 collective-permute-start.7
  44.3 0.0 copy-done
  44.3 2.5 %place.1.part_ref = f32[4,256,512]{2,1,0:T(8,128)S(1)} custom-call(s32[4,2,8,128]{3,2,1,0:T(8,128)S(1)} %get-tuple-element.26.corner_ref, bf16[4,4,256,256]{3,2,1,0:T(8,128)(2,1)S(1)} %get-tuple-element.43.grad_ref, f32[4,256,512]{2,1,0:T(8,128)S(1)} %bitcast.6), custom_call_target="tpu_custom_call" | custom-call | flops 2147483648 | bytes 2097152 | tf_op jit(solution)/shard_map/place/pallas_call | solution.py:484
  46.7 0.0 collective-permute-done.9.rest_2_
  46.7 1.9 %collective-permute-done.8.rest_1_ = bf16[128,256]{1,0:T(8,128)(2,1)S(1)} collective-permute-done((bf16[128,256]{1,0:T(8,128)(2,1)S(1)}, bf16[128,256]{1,0:T(8,128)(2,1)S(1)}, u32[]{:S(2)}, u32[]{:S(2)}) %collective-permute-start.8) | collective-permute-done | bytes 65568 | tf_op jit(solution)/shard_map/ppermute | solution.py:21
  48.6 1.5 %collective-permute-done.7.rest_0_ = bf16[128,256]{1,0:T(8,128)(2,1)S(1)} collective-permute-done((bf16[128,256]{1,0:T(8,128)(2,1)S(1)}, bf16[128,256]{1,0:T(8,128)(2,1)S(1)}, u32[]{:S(2)}, u32[]{:S(2)}) %collective-permute-start.7) | collective-permute-done | bytes 65568 | tf_op jit(solution)/shard_map/ppermute | solution.py:21
  50.1 0.4 collective-permute-start.11
  50.5 4.0 %collective-permute-done.11.rest_0_ = bf16[128,256]{1,0:T(8,128)(2,1)S(1)} collective-permute-done((bf16[128,256]{1,0:T(8,128)(2,1)S(1)}, bf16[128,256]{1,0:T(8,128)(2,1)S(1)}, u32[]{:S(2)}, u32[]{:S(2)}) %collective-permute-start.11) | collective-permute-done | bytes 65568 | tf_op jit(solution)/shard_map/ppermute | solution.py:21
  54.5 0.1 collective-permute-start.12
  54.6 1.3 %collective-permute-done.12.other_ref = bf16[256,256]{1,0:T(8,128)(2,1)S(1)} collective-permute-done((bf16[256,256]{1,0:T(8,128)(2,1)S(1)}, bf16[256,256]{1,0:T(8,128)(2,1)S(1)}, u32[]{:S(2)}, u32[]{:S(2)}) %collective-permute-start.12) | collective-permute-done | bytes 131104 | tf_op jit(solution)/shard_map/ppermute | solution.py:21
  55.9 0.9 %update_probe.1 = f32[2,256,256]{2,1,0:T(8,128)} custom-call(f32[2,256,256]{2,1,0:T(8,128)S(1)} %copy-done.4, bf16[256,256]{1,0:T(8,128)(2,1)S(1)} %gather_half.1.mine_ref, bf16[256,256]{1,0:T(8,128)(2,1)S(1)} %collective-permute-done.12.other_ref), custom_call_target="tpu_custom_call" | custom-call | flops 2000000000 | bytes 262144 | tf_op jit(solution)/shard_map/update_probe/pallas_call | solution.py:326
  56.8 0.0 collective-permute-done.10.rim_ref
  56.8 1.9 %finish.1 = f32[4,256,512]{2,1,0:T(8,128)} custom-call(f32[4,256,512]{2,1,0:T(8,128)S(1)} %place.1.part_ref, bf16[4,256,512]{2,1,0:T(8,128)(2,1)S(1)} %collective-permute-done.10.rim_ref), custom_call_target="tpu_custom_call" | custom-call | tf_op jit(solution)/shard_map/finish/pallas_call | solution.py:496
  (4 shorter events, 0.1 us)
Async XLA Ops:
  0.6 2.8 %copy-start.3 = (s32[2,1]{0,1:T(1,128)S(1)}, s32[2,1]{0,1:T(1,128)}, u32[]{:S(2)}) copy-start(s32[2,1]{0,1:T(1,128)} %param.12) | copy-start | bytes 28
  0.6 2.8 %copy-start.1 = (f32[2,256,256]{2,1,0:T(8,128)S(1)}, f32[2,256,256]{2,1,0:T(8,128)}, u32[]{:S(2)}) copy-start(f32[2,256,256]{2,1,0:T(8,128)} %intensity_ref.1) | copy-start | bytes 1572868
  0.7 11.3 %copy-start.5 = (s32[4,1,2]{0,2,1:T(2,128)S(1)}, s32[4,1,2]{0,2,1:T(2,128)}, u32[]{:S(2)}) copy-start(s32[4,1,2]{0,2,1:T(2,128)} %param.11) | copy-start | bytes 100
  0.7 11.4 %copy-start.2 = (f32[256,256]{1,0:T(8,128)S(1)}, f32[256,256]{1,0:T(8,128)}, u32[]{:S(2)}) copy-start(f32[256,256]{1,0:T(8,128)} %phase_ref.1) | copy-start | bytes 786436
  2.0 12.4 %copy-start.4 = (f32[2,256,256]{2,1,0:T(8,128)S(1)}, f32[2,256,256]{2,1,0:T(8,128)}, u32[]{:S(2)}) copy-start(f32[2,256,256]{2,1,0:T(8,128)} %probe_ref.5) | copy-start | bytes 1572868
  2.0 12.3 %collective-permute-start = (bf16[2,256,512]{2,1,0:T(8,128)(2,1)S(1)}, bf16[2,256,512]{2,1,0:T(8,128)(2,1)S(1)}, u32[]{:S(2)}, u32[]{:S(2)}) collective-permute-start(bf16[2,256,512]{2,1,0:T(8,128)(2,1)S(1)} %prepare_zero.1.own_ref), channel_id=1, source_target_pairs={{4,0},{8,4},{12,8},{5,1},{9,5},{13,9},{6,2},{10,6},{14,10},{7,3},{... | collective-permute-start | bytes 1572872 | tf_op jit(solution)/shard_map/ppermute | solution.py:27
  5.9 13.3 %collective-permute-start.1 = (bf16[2,256,512]{2,1,0:T(8,128)(2,1)S(1)}, bf16[2,256,512]{2,1,0:T(8,128)(2,1)S(1)}, u32[]{:S(2)}, u32[]{:S(2)}) collective-permute-start(bf16[2,256,512]{2,1,0:T(8,128)(2,1)S(1)} %get-tuple-element.30.own_ref), channel_id=1, source_target_pairs={{4,0},{8,4},{12,8},{5,1},{9,5},{13,9},{6,2},{10,6},{14,10},{7,3},{... | collective-permute-start | bytes 1572872 | tf_op jit(solution)/shard_map/ppermute | solution.py:27
  7.2 15.7 %collective-permute-start.2 = (bf16[256,256]{1,0:T(8,128)(2,1)}, bf16[256,256]{1,0:T(8,128)(2,1)S(1)}, u32[]{:S(2)}, u32[]{:S(2)}) collective-permute-start(bf16[256,256]{1,0:T(8,128)(2,1)} %get-tuple-element.35), channel_id=1, source_target_pairs={{0,4},{4,0},{8,12},{12,8},{1,5},{5,1},{9,13},{13,9},{2,6},{6,2},{1... | collective-permute-start | bytes 393224 | tf_op jit(solution)/shard_map/ppermute | solution.py:21
  9.0 15.0 %collective-permute-start.3 = (bf16[256,256]{1,0:T(8,128)(2,1)S(1)}, bf16[256,256]{1,0:T(8,128)(2,1)S(1)}, u32[]{:S(2)}, u32[]{:S(2)}) collective-permute-start(bf16[256,256]{1,0:T(8,128)(2,1)S(1)} %get-tuple-element.36), channel_id=1, source_target_pairs={{0,8},{4,12},{8,0},{12,4},{1,9},{5,13},{9,1},{13,5},{2,10},{6,14},... | collective-permute-start | bytes 393224 | tf_op jit(solution)/shard_map/ppermute | solution.py:21
  12.0 12.0 %collective-permute-start.4 = (bf16[256,256]{1,0:T(8,128)(2,1)S(1)}, bf16[256,256]{1,0:T(8,128)(2,1)}, u32[]{:S(2)}, u32[]{:S(2)}) collective-permute-start(bf16[256,256]{1,0:T(8,128)(2,1)S(1)} %get-tuple-element.37), channel_id=1, source_target_pairs={{0,12},{4,8},{8,4},{12,0},{1,13},{5,9},{9,5},{13,1},{2,14},{6,10},... | collective-permute-start | bytes 393224 | tf_op jit(solution)/shard_map/ppermute | solution.py:21
  32.2 3.2 %collective-permute-start.5 = (bf16[256,256]{1,0:T(8,128)(2,1)S(1)}, bf16[256,256]{1,0:T(8,128)(2,1)S(1)}, u32[]{:S(2)}, u32[]{:S(2)}) collective-permute-start(bf16[256,256]{1,0:T(8,128)(2,1)S(1)} %get-tuple-element.39), channel_id=1, source_target_pairs={{0,4},{4,0},{8,12},{12,8},{1,5},{5,1},{9,13},{13,9},{2,6},{6,2},{1... | collective-permute-start | bytes 393224 | tf_op jit(solution)/shard_map/ppermute | solution.py:21
  35.4 4.4 %collective-permute-start.6 = (bf16[128,256]{1,0:T(8,128)(2,1)S(1)}, bf16[128,256]{1,0:T(8,128)(2,1)S(1)}, u32[]{:S(2)}, u32[]{:S(2)}) collective-permute-start(bf16[128,256]{1,0:T(8,128)(2,1)S(1)} %get-tuple-element.41), channel_id=1, source_target_pairs={{0,8},{4,12},{8,0},{12,4},{1,9},{5,13},{9,1},{13,5},{2,10},{6,14},... | collective-permute-start | bytes 196616 | tf_op jit(solution)/shard_map/ppermute | solution.py:21
  35.5 21.3 %collective-permute-start.10 = (bf16[4,256,512]{2,1,0:T(8,128)(2,1)S(1)}, bf16[4,256,512]{2,1,0:T(8,128)(2,1)S(1)}, u32[]{:S(2)}, u32[]{:S(2)}) collective-permute-start(bf16[4,256,512]{2,1,0:T(8,128)(2,1)S(1)} %get-tuple-element.45), channel_id=1, source_target_pairs={{0,4},{4,8},{8,12},{1,5},{5,9},{9,13},{2,6},{6,10},{10,14},{3,7},{... | collective-permute-start | bytes 3145736 | tf_op jit(solution)/shard_map/ppermute | solution.py:27
  39.8 4.5 %copy-start = (f32[2,2,256,512]{3,2,1,0:T(8,128)S(1)}, f32[2,2,256,512]{3,2,1,0:T(8,128)}, u32[]{:S(2)}) copy-start(f32[2,2,256,512]{3,2,1,0:T(8,128)} %param.7) | copy-start | bytes 6291460
  39.8 6.9 %collective-permute-start.9 = (bf16[128,256]{1,0:T(8,128)(2,1)S(1)}, bf16[128,256]{1,0:T(8,128)(2,1)S(1)}, u32[]{:S(2)}, u32[]{:S(2)}) collective-permute-start(bf16[128,256]{1,0:T(8,128)(2,1)S(1)} %get-tuple-element.42), channel_id=1, source_target_pairs={{0,1},{1,0},{2,3},{3,2},{4,5},{5,4},{6,7},{7,6},{8,9},{9,8},{10,11... | collective-permute-start | bytes 196616 | tf_op jit(solution)/shard_map/ppermute | solution.py:21
  41.5 7.2 %collective-permute-start.8 = (bf16[128,256]{1,0:T(8,128)(2,1)S(1)}, bf16[128,256]{1,0:T(8,128)(2,1)S(1)}, u32[]{:S(2)}, u32[]{:S(2)}) collective-permute-start(bf16[128,256]{1,0:T(8,128)(2,1)S(1)} %get-tuple-element.42), channel_id=1, source_target_pairs={{0,2},{1,3},{2,0},{3,1},{4,6},{5,7},{6,4},{7,5},{8,10},{9,11},{10,... | collective-permute-start | bytes 196616 | tf_op jit(solution)/shard_map/ppermute | solution.py:21
  44.0 6.1 %collective-permute-start.7 = (bf16[128,256]{1,0:T(8,128)(2,1)S(1)}, bf16[128,256]{1,0:T(8,128)(2,1)S(1)}, u32[]{:S(2)}, u32[]{:S(2)}) collective-permute-start(bf16[128,256]{1,0:T(8,128)(2,1)S(1)} %get-tuple-element.42), channel_id=1, source_target_pairs={{0,3},{1,2},{2,1},{3,0},{4,7},{5,6},{6,5},{7,4},{8,11},{9,10},{10,... | collective-permute-start | bytes 196616 | tf_op jit(solution)/shard_map/ppermute | solution.py:21
  50.1 4.3 %collective-permute-start.11 = (bf16[128,256]{1,0:T(8,128)(2,1)S(1)}, bf16[128,256]{1,0:T(8,128)(2,1)S(1)}, u32[]{:S(2)}, u32[]{:S(2)}) collective-permute-start(bf16[128,256]{1,0:T(8,128)(2,1)S(1)} %full_sum.1.mine_ref), channel_id=1, source_target_pairs={{0,8},{4,12},{8,0},{12,4},{1,9},{5,13},{9,1},{13,5},{2,10},{6,14},... | collective-permute-start | bytes 196616 | tf_op jit(solution)/shard_map/ppermute | solution.py:21
  54.5 1.4 %collective-permute-start.12 = (bf16[256,256]{1,0:T(8,128)(2,1)S(1)}, bf16[256,256]{1,0:T(8,128)(2,1)S(1)}, u32[]{:S(2)}, u32[]{:S(2)}) collective-permute-start(bf16[256,256]{1,0:T(8,128)(2,1)S(1)} %gather_half.1.mine_ref), channel_id=1, source_target_pairs={{0,4},{4,0},{8,12},{12,8},{1,5},{5,1},{9,13},{13,9},{2,6},{6,2},{1... | collective-permute-start | bytes 393224 | tf_op jit(solution)/shard_map/ppermute | solution.py:21
where the time goes:
time: 58.9 us; the launch traced here: 58.6 us
  Pallas kernels  28 us (48%)
  starting transfers between devices  17 us (29%)
  waiting for transfers between devices  12.7 us (22%)
  between operations  0.84 us (1%)
    ppermute x10, waiting for transfers between devices, permute_pairs(): lax.ppermute(block, axis, [(i, partner(i)) for i in range(lax.axis_size(a...  12.7 us
    ppermute x10, starting transfers between devices, permute_pairs(): lax.ppermute(block, axis, [(i, partner(i)) for i in range(lax.axis_size(a...  12 us
    pallas_call x1, Pallas kernels, per_device(): call(third_kernel, [whole(plane), whole(plane), tables, block, block, wid...  8.18 us
    ppermute x3, starting transfers between devices, from_behind(): return lax.ppermute(block, axis, route)  4.98 us
    pallas_call x1, Pallas kernels, per_device(): call(first_kernel, [own_block, rim_block, whole(plane), whole(plane), tab...  4.87 us
    pallas_call x1, Pallas kernels, per_device(): call(second_kernel, [own_block, rim_block, wide_block, tables], [block, w...  3.65 us
    pallas_call x1, Pallas kernels, per_device(): call(place_kernel, [whole(grad_shape), whole((planes, height, width))], [...  2.45 us
    pallas_call x1, Pallas kernels, per_device(): pl.pallas_call(second_prep_kernel, in_specs=[smem, hbm, vmem], out_specs=...  2.43 us
  transfers between devices with their start and end apart: 13, of which 7 were waited for; matrix products, arithmetic and copies ran while one was open for 0% of the time, Pallas kernels for 28%

commit v1 on v0

--- a/solution.py
+++ b/solution.py
@@ -11,7 +11,8 @@
 
 step_object = 0.05
 step_probe = 0.5
-SMALL_FLOPS = 2000000000
+SMALL_FLOPS = 4000000000
+LATE_FROM = 99
 SMALL_VMEM = 8 * 1024 * 1024
 LARGE_VMEM = 24 * 1024 * 1024
 POSITIONS_AT_ONCE = 4
@@ -21,10 +22,9 @@
     return lax.ppermute(block, axis, [(i, partner(i)) for i in range(lax.axis_size(axis))])
 
 
-def from_behind(block, axis, distance):
-    devices = range(lax.axis_size(axis))
-    route = [(i - distance, i) for i in devices if i - distance in devices]
-    return lax.ppermute(block, axis, route)
+def around(block, axis, distance):
+    size = lax.axis_size(axis)
+    return lax.ppermute(block, axis, [(i, (i + distance) % size) for i in range(size)])
 
 
 def dft_table(length):
@@ -49,8 +49,8 @@
         out_ref[p] = product(middle_ref[p], table_ref[...])
 
 
-def chunks(n):
-    size = min(32, n)
+def chunks(n, size=32):
+    size = min(size, n)
     return [slice(a, a + size) for a in range(0, n, size)]
 
 
@@ -90,15 +90,27 @@
     return corner_ref[position, 0, :1, :1], corner_ref[position, 1, :1, :1]
 
 
-def cut(own_ref, rim_ref, patch_ref, corner_ref, base, count):
+def cut(own_ref, rim_ref, patch_ref, spot_ref, tile_ref, place_ref, sem, base, count):
     n = patch_ref.shape[2]
-    height = own_ref.shape[1] + rim_ref.shape[1]
-    width = own_ref.shape[2]
-    planes = jnp.concatenate([jnp.concatenate([own_ref[c], rim_ref[c]], 0) for c in range(2)], 1)
-    for p in range(count):
-        corner_y, corner_x = spot(corner_ref, base + p)
-        rows = product(one_hot_rows((n, height), corner_y), planes).astype(jnp.bfloat16)
-        rows = jnp.concatenate([rows[:, :width], rows[:, width:]], 0)
+    height, width = own_ref.shape[1:]
+    copy = pltpu.make_async_copy(spot_ref, place_ref, sem)
+    copy.start()
+    ends = lax.axis_index("row") == lax.axis_size("row") - 1
+    for c in range(2):
+        tile_ref[c, : height // 8] = own_ref[c].astype(jnp.float32).reshape(height // 8, 8, width)
+        rim = jnp.where(ends, 0.0, rim_ref[c].astype(jnp.float32))
+        tile_ref[c, height // 8 :] = rim.reshape(-1, 8, width)
+    copy.wait()
+    within = lax.broadcasted_iota(jnp.int32, (n // 8, 8, width), 1)
+    for p in range(count):
+        corner_y, corner_x = place_ref[base + p, 0], place_ref[base + p, 1]
+        group = corner_y // 8
+        shift = corner_y - group * 8
+        rows = []
+        for c in range(2):
+            turned = pltpu.roll(tile_ref[c, pl.ds(group, n // 8 + 1)], 8 - shift, 1)
+            rows.append(jnp.where(within < 8 - shift, turned[:-1], turned[1:]).reshape(n, width))
+        rows = jnp.concatenate(rows, 0).astype(jnp.bfloat16)
         both = product(rows, one_hot_columns((width, n), corner_x)).astype(jnp.bfloat16)
         patch_ref[p, 0] = both[:n]
         patch_ref[p, 1] = both[n:]
@@ -108,19 +120,28 @@
     return ref[p, 0, rows].astype(jnp.float32), ref[p, 1, rows].astype(jnp.float32)
 
 
-def first_prep_kernel(slab_ref, own_ref, wide_ref, sems):
-    planes = own_ref.shape[0]
-    copies = [pltpu.make_async_copy(slab_ref.at[c], wide_ref.at[c], sems.at[c]) for c in range(planes)]
+def own_kernel(slab_hbm, own_ref, wide_ref, sems):
+    parts = [(c, rows) for c in range(own_ref.shape[0]) for rows in chunks(own_ref.shape[1], 64)]
+    copies = [
+        pltpu.make_async_copy(slab_hbm.at[c, rows], wide_ref.at[c, rows], sems.at[i])
+        for i, (c, rows) in enumerate(parts)
+    ]
     for copy in copies:
         copy.start()
-    for c, copy in enumerate(copies):
+    for (c, rows), copy in zip(parts, copies):
         copy.wait()
-        own_ref[c] = wide_ref[c].astype(jnp.bfloat16)
-
-
-def second_prep_kernel(source_ref, slab_hbm, intensity_ref, own_ref, *rest):
-    message_refs, wide_ref, sem = rest[:-2], rest[-2], rest[-1]
-    copy = pltpu.make_async_copy(slab_hbm.at[pl.ds(own_ref.shape[0], own_ref.shape[0])], wide_ref, sem)
+        own_ref[c, rows] = wide_ref[c, rows].astype(jnp.bfloat16)
+
+
+def prepare_kernel(
+    corner_ref, source_ref, phase_ref, table_hbm, slab_hbm, intensity_ref,
+    own_ref, table_ref, kernel_ref, vector_ref, spot_ref, *rest,
+):
+    message_refs, wide_ref, sems = rest[:-2], rest[-2], rest[-1]
+    planes = own_ref.shape[0]
+    slab_copy = pltpu.make_async_copy(slab_hbm.at[pl.ds(planes, planes)], wide_ref, sems.at[0])
+    slab_copy.start()
+    copy = pltpu.make_async_copy(table_hbm, table_ref, sems.at[1])
     copy.start()
     for s, message_ref in enumerate(message_refs):
         target = lax.axis_index("row") ^ s
@@ -129,29 +150,27 @@
             slot = jnp.where(source_ref[k] == target, k, slot)
         chosen = intensity_ref[jnp.maximum(slot, 0)]
         message_ref[...] = jnp.where(slot >= 0, chosen, -1.0).astype(jnp.bfloat16)
-    copy.wait()
-    own_ref[...] = wide_ref[...].astype(jnp.bfloat16)
-
-
-def third_prep_kernel(corner_ref, phase_ref, table_hbm, table_ref, kernel_ref, spot_ref, sem):
-    copy = pltpu.make_async_copy(table_hbm, table_ref, sem)
-    copy.start()
-    for p in range(spot_ref.shape[0]):
+    lane = lax.broadcasted_iota(jnp.int32, (1, spot_ref.shape[1]), 1)
+    for p in range(vector_ref.shape[0]):
         owner = lax.axis_index("row") ^ p
         for k in range(2):
-            spot_ref[p, k] = jnp.full(spot_ref.shape[2:], corner_ref[owner, k], jnp.int32)
+            vector_ref[p, k] = jnp.full(vector_ref.shape[2:], corner_ref[owner, k], jnp.int32)
+        spot_ref[p : p + 1] = jnp.where(lane == 0, corner_ref[owner, 0], corner_ref[owner, 1])
     for rows in chunks(phase_ref.shape[0]):
         kernel_ref[0, rows] = jnp.cos(phase_ref[rows])
         kernel_ref[1, rows] = jnp.sin(phase_ref[rows])
+    slab_copy.wait()
+    own_ref[...] = wide_ref[...].astype(jnp.bfloat16)
     copy.wait()
 
 
 def first_kernel(
-    corner_ref, own_ref, rim_ref, probe_ref, kernel_ref, table_ref, patch_ref, moved_ref,
-    field_ref, middle_ref, out_ref,
+    spot_ref, own_ref, rim_ref, probe_ref, kernel_ref, table_ref, patch_ref, moved_ref,
+    tile_ref, place_ref, sem, field_ref, middle_ref, out_ref,
 ):
     count, _, n, _ = patch_ref.shape
-    cut(own_ref, rim_ref, patch_ref, corner_ref, pl.program_id(0) * count, count)
+    base = pl.program_id(0) * count
+    cut(own_ref, rim_ref, patch_ref, spot_ref, tile_ref, place_ref, sem, base, count)
     for p in range(count):
         for rows in chunks(n):
             q_re, q_im = probe_ref[0, rows], probe_ref[1, rows]
@@ -167,10 +186,12 @@
 
 
 def second_kernel(
-    corner_ref, own_ref, rim_ref, moved_ref, table_ref, patch_ref, far_ref, field_ref, middle_ref
+    spot_ref, own_ref, rim_ref, moved_ref, table_ref, patch_ref, far_ref,
+    tile_ref, place_ref, sem, field_ref, middle_ref,
 ):
     count, _, n, _ = patch_ref.shape
-    cut(own_ref, rim_ref, patch_ref, corner_ref, pl.program_id(0) * count, count)
+    base = pl.program_id(0) * count
+    cut(own_ref, rim_ref, patch_ref, spot_ref, tile_ref, place_ref, sem, base, count)
     for p in range(count):
         for rows in chunks(n):
             m_re, m_im = get_backward(moved_ref, p, rows)
@@ -179,25 +200,26 @@
     transform(table_ref, field_ref, middle_ref, far_ref, range(count))
 
 
-def third_kernel(corner_ref, probe_ref, kernel_ref, table_ref, zero_ref, one_ref, moved_ref, far_ref, *rest):
-    measured_refs = rest[:-9]
-    grad_ref, rim_ref, keep_ref, send_ref, probe_grad_ref, measured_ref = rest[-9:-3]
+def third_kernel(probe_ref, kernel_ref, table_ref, zero_ref, one_ref, moved_ref, far_ref, *rest, steps):
+    measured_refs = rest[:-8]
+    grad_ref, keep_ref, send_ref, probe_grad_ref, measured_ref = rest[-8:-3]
     field_ref, middle_ref, out_ref = rest[-3:]
     count, _, n, _ = zero_ref.shape
-    planes = grad_ref.shape[0]
-    base = pl.program_id(0) * count
-    last = pl.program_id(0) == pl.num_programs(0) - 1
-
-    @pl.when(pl.program_id(0) == 0)
-    def _():
+    base = pl.program_id(0) * count if steps > 1 else 0
+
+    def start():
         for s, ref in enumerate(measured_refs):
             measured_ref[s] = ref[...]
         probe_grad_ref[...] = jnp.zeros_like(probe_grad_ref)
 
+    if steps > 1:
+        pl.when(pl.program_id(0) == 0)(start)
+
     for p in range(count):
         for rows in chunks(n):
             f_re, f_im = get_forward(far_ref, p, rows)
-            measured = measured_ref[base + p, rows].astype(jnp.float32)
+            measured = measured_ref[base + p, rows] if steps > 1 else measured_refs[p][rows]
+            measured = measured.astype(jnp.float32)
             misfit = jnp.where(measured < 0.0, 0.0, f_re * f_re + f_im * f_im - measured)
             put_backward(field_ref, p, rows, misfit * f_re, misfit * f_im)
     transform(table_ref, field_ref, middle_ref, out_ref, range(count))
@@ -217,7 +239,7 @@
             put_backward(field_ref, p, rows, k_re * r + k_im * i, k_re * i - k_im * r)
     transform(table_ref, field_ref, middle_ref, out_ref, range(count))
     for rows in chunks(n):
-        total_re, total_im = probe_grad_ref[0, rows], probe_grad_ref[1, rows]
+        total_re, total_im = (probe_grad_ref[0, rows], probe_grad_ref[1, rows]) if steps > 1 else (0.0, 0.0)
         q_re, q_im = probe_ref[0, rows], probe_ref[1, rows]
         for p in range(count):
             b_re, b_im = get_backward(out_ref, p, rows)
@@ -229,47 +251,61 @@
         probe_grad_ref[0, rows] = total_re
         probe_grad_ref[1, rows] = total_im
 
-    @pl.when(last)
-    def _():
+    def end():
         core = lax.axis_index("row") % 2
         keep_ref[...] = probe_grad_ref[core]
         send_ref[...] = probe_grad_ref[1 - core].astype(jnp.bfloat16)
-        rows, width = rim_ref.shape[1:]
-        moves, tall = placements(corner_ref, grad_ref.shape[1], n, width, rows, rows)
-        for plane in range(planes):
-            rim_ref[plane] = placed(grad_ref, plane, moves, tall).astype(jnp.bfloat16)
-
-
-def placements(corner_ref, positions, n, width, rows, first_row):
-    moves, tall = [], []
+
+    if steps > 1:
+        pl.when(pl.program_id(0) == steps - 1)(end)
+    else:
+        end()
+
+
+def placed(corner_ref, grad_ref, tall_ref, rows, width, first_row):
+    planes, positions, n, _ = grad_ref.shape
+    moves = []
     for p in range(positions):
         corner_y, corner_x = spot(corner_ref, p)
         moves.append(one_hot_rows((n, width), corner_x))
-        tall.append(one_hot_columns((rows, n), corner_y - first_row))
-    return moves, jnp.concatenate(tall, 1)
-
-
-def placed(grad_ref, plane, moves, tall):
-    wide = [product(grad_ref[plane, p], move).astype(jnp.bfloat16) for p, move in enumerate(moves)]
-    return product(tall, jnp.concatenate(wide, 0))
-
-
-def place_kernel(corner_ref, grad_ref, slab_ref, part_ref):
+        every = jnp.concatenate([grad_ref[plane, p] for plane in range(planes)], 1)
+        tall = product(one_hot_columns((rows, n), corner_y - first_row), every).astype(jnp.bfloat16)
+        for plane in range(planes):
+            tall_ref[plane, :, p * n : (p + 1) * n] = tall[:, plane * n : (plane + 1) * n]
+    moves = jnp.concatenate(moves, 0)
+    for plane in range(planes):
+        yield plane, product(tall_ref[plane], moves)
+
+
+def place_rim_kernel(corner_ref, grad_ref, rim_ref, tall_ref, *, height):
+    rows, width = rim_ref.shape[1:]
+    for plane, total in placed(corner_ref, grad_ref, tall_ref, rows, width, height):
+        rim_ref[plane] = total.astype(jnp.bfloat16)
+
+
+def place_kernel(corner_ref, grad_ref, slab_ref, part_ref, tall_ref):
     rows, width = part_ref.shape[1:]
-    moves, tall = placements(corner_ref, grad_ref.shape[1], grad_ref.shape[2], width, rows, 0)
-    for plane in range(grad_ref.shape[0]):
-        part_ref[plane] = slab_ref[plane] - step_object * placed(grad_ref, plane, moves, tall)
+    for plane, total in placed(corner_ref, grad_ref, tall_ref, rows, width, 0):
+        part_ref[plane] = slab_ref[plane] - step_object * total
 
 
 def in_hbm(array):
     return pltpu.with_memory_space_constraint(array, pltpu.HBM)
 
 
-def finish_kernel(part_ref, rim_ref, out_ref):
-    rows = rim_ref.shape[1]
-    out_ref[:, :rows] = part_ref[:, :rows] - step_object * rim_ref[...].astype(jnp.float32)
-    if rows < part_ref.shape[1]:
-        out_ref[:, rows:] = part_ref[:, rows:]
+def finish_kernel(part_ref, rim_ref, out_hbm, sums_ref, sems):
+    parts = [(c, rows) for c in range(part_ref.shape[0]) for rows in chunks(part_ref.shape[1], 128)]
+    copies = []
+    step = jnp.where(lax.axis_index("row") == 0, 0.0, step_object)
+    for i, (c, rows) in enumerate(parts):
+        value = part_ref[c, rows]
+        if rows.start < rim_ref.shape[1]:
+            value -= step * rim_ref[c, rows].astype(jnp.float32)
+        sums_ref[c, rows] = value
+        copies.append(pltpu.make_async_copy(sums_ref.at[c, rows], out_hbm.at[c, rows], sems.at[i]))
+        copies[-1].start()
+    for copy in copies:
+        copy.wait()
 
 
 def whole(shape):
@@ -335,13 +371,14 @@
     )(*arrays)
 
 
-def probe_sum(keep, send, part):
+def probe_sum(keep, send, rim_grad, part):
     n = keep.shape[0]
     row_count, col_count = lax.axis_size("row"), lax.axis_size("col")
     chips = row_count // 2
     shape = (n // chips, n)
     wide, narrow = jax.ShapeDtypeStruct(shape, jnp.float32), jax.ShapeDtypeStruct(shape, jnp.bfloat16)
     other = permute_pairs(send, "row", lambda i: i ^ 1)
+    rim_grad = around(rim_grad, "row", 1)
     mine, *sends = small_call(
         half_sum_kernel, [keep, other], [wide] + [narrow] * (chips - 1), "half_sum", [pltpu.VMEM((n, n), jnp.float32)]
     )
@@ -353,7 +390,7 @@
     others = [permute_pairs(total, "row", lambda i: i ^ (2 * s)) for s in range(1, chips)]
     half = jax.ShapeDtypeStruct((n, n), jnp.bfloat16)
     (mine,) = small_call(gather_kernel, [total, *others], [half], "gather_half")
-    return mine, permute_pairs(mine, "row", lambda i: i ^ 1), part
+    return mine, permute_pairs(mine, "row", lambda i: i ^ 1), rim_grad, part
 
 
 def per_device(object_slab, probe_field, prop_phase, intensities, corners, slot_source):
@@ -379,48 +416,54 @@
         return pltpu.with_memory_space_constraint(array, pltpu.VMEM) if small else array
 
     tile = (pair_count, height, width)
+    spot_shape = (-(-row_count // 8) * 8, 128)
     own_zero = pl.pallas_call(
-        first_prep_kernel,
+        own_kernel,
         in_specs=[hbm],
         out_specs=vmem,
         out_shape=kept(tile, jnp.bfloat16),
-        scratch_shapes=[pltpu.VMEM(tile, jnp.float32), pltpu.SemaphoreType.DMA((pair_count,))],
+        scratch_shapes=[
+            pltpu.VMEM(tile, jnp.float32),
+            pltpu.SemaphoreType.DMA((pair_count * len(chunks(height, 64)),)),
+        ],
         compiler_params=pltpu.CompilerParams(vmem_limit_bytes=SMALL_VMEM),
-        name="prepare_zero",
+        name="own_zero",
     )(in_hbm(slab))
-    rim_zero = from_behind(own_zero[:, :n], "row", -1)
-    own_one, *messages = pl.pallas_call(
-        second_prep_kernel,
-        in_specs=[smem, hbm, vmem],
-        out_specs=[vmem] * (1 + row_count),
-        out_shape=[kept(tile, jnp.bfloat16)] + [kept((n, n), jnp.bfloat16)] * row_count,
-        scratch_shapes=[pltpu.VMEM(tile, jnp.float32), pltpu.SemaphoreType.DMA],
-        compiler_params=pltpu.CompilerParams(vmem_limit_bytes=SMALL_VMEM),
-        name="prepare_one",
-    )(sources, in_hbm(slab), intensities)
-    table, kernel, spots = pl.pallas_call(
-        third_prep_kernel,
-        in_specs=[smem, vmem, hbm],
-        out_specs=[vmem] * 3,
+    rim_zero = around(own_zero[:, :n], "row", -1)
+    own_one, table, kernel, vectors, spots, *messages = pl.pallas_call(
+        prepare_kernel,
+        in_specs=[smem, smem, vmem, hbm, hbm, vmem],
+        out_specs=[vmem] * (5 + row_count),
         out_shape=[
+            kept(tile, jnp.bfloat16),
             kept((2 * n, 2 * n), jnp.bfloat16),
             kept((2, n, n), jnp.float32),
             kept((row_count, 2, 8, 128), jnp.int32),
-        ],
-        scratch_shapes=[pltpu.SemaphoreType.DMA],
+            kept(spot_shape, jnp.int32),
+        ]
+        + [kept((n, n), jnp.bfloat16)] * row_count,
+        scratch_shapes=[pltpu.VMEM(tile, jnp.float32), pltpu.SemaphoreType.DMA((2,))],
         compiler_params=pltpu.CompilerParams(vmem_limit_bytes=SMALL_VMEM),
-        name="prepare_two",
-    )(corners.reshape(row_count, 2), prop_phase, in_hbm(dft_table(n)))
-    rim_one = from_behind(own_one[:, :n], "row", -1)
-    measured = [messages[0]]
+        name="prepare",
+    )(corners.reshape(row_count, 2), sources, prop_phase, in_hbm(dft_table(n)), in_hbm(slab), intensities)
+    rim_one = around(own_one[:, :n], "row", -1)
+    measured = {0: messages[0]}
+    late = [s for s in range(1, row_count) if s >= LATE_FROM]
     for s in range(1, row_count):
-        measured.append(permute_pairs(messages[s], "row", lambda i: i ^ s))
+        if s not in late:
+            measured[s] = permute_pairs(messages[s], "row", lambda i: i ^ s)
 
     count = min(POSITIONS_AT_ONCE, row_count)
     plane = (2, n, n)
     positions = (row_count, 2, n, n)
     block = per_position((count, 2, n, n))
     own_block, rim_block, tables = whole(tile), whole((pair_count, n, width)), whole((2 * n, 2 * n))
+    spot_block, vector_block = whole(spot_shape), whole((row_count, 2, 8, 128))
+    cutting = [
+        pltpu.VMEM((pair_count, (height + n) // 8, 8, width), jnp.float32),
+        pltpu.SMEM(spot_shape, jnp.int32),
+        pltpu.SemaphoreType.DMA,
+    ]
     wide = (row_count, n, 2 * n)
     wide_block = per_position((count, n, 2 * n))
     work = [
@@ -434,7 +477,7 @@
         return pl.pallas_call(
             body,
             grid=(steps,),
-            in_specs=[whole((row_count, 2, 8, 128))] + in_specs,
+            in_specs=in_specs,
             out_specs=out_specs,
             scratch_shapes=scratch,
             out_shape=out_shape,
@@ -447,64 +490,77 @@
 
     patch_zero, moved = call(
         first_kernel,
-        [own_block, rim_block, whole(plane), whole(plane), tables],
+        [spot_block, own_block, rim_block, whole(plane), whole(plane), tables],
         [block, wide_block],
         [kept(positions, jnp.bfloat16), kept(wide, jnp.float32)],
         28,
         "moved",
-        scratch=work,
+        scratch=cutting + work,
     )(near(spots), near(own_zero), near(rim_zero), probe_field, near(kernel), near(table))
+    moved, waiting = lax.optimization_barrier((moved, [messages[s] for s in late]))
+    for s, message in zip(late, waiting):
+        measured[s] = permute_pairs(message, "row", lambda i: i ^ s)
     patch_one, far = call(
         second_kernel,
-        [own_block, rim_block, wide_block, tables],
+        [spot_block, own_block, rim_block, wide_block, tables],
         [block, wide_block],
         [kept(positions, jnp.bfloat16), kept(wide, jnp.float32)],
         20,
         "far",
-        scratch=work[:2],
+        scratch=cutting + work[:2],
     )(near(spots), near(own_one), near(rim_one), near(moved), near(table))
     grad_shape = (planes, row_count, n, n)
-    grads, rim_grad, keep, send = call(
-        third_kernel,
+    grads, keep, send = call(
+        functools.partial(third_kernel, steps=row_count // count),
         [whole(plane), whole(plane), tables, block, block, wide_block, wide_block] + [whole((n, n))] * row_count,
-        [whole(grad_shape), whole((planes, n, width)), whole((n, n)), whole((n, n))],
+        [whole(grad_shape), whole((n, n)), whole((n, n))],
         [
             kept(grad_shape, jnp.bfloat16),
-            kept((planes, n, width), jnp.bfloat16),
             kept((n, n), jnp.float32),
             kept((n, n), jnp.bfloat16),
         ],
-        40,
+        24,
         "gradients",
         scratch=[pltpu.VMEM(plane, jnp.float32), pltpu.VMEM((row_count, n, n), jnp.bfloat16)] + work,
     )(
-        near(spots), probe_field, near(kernel), near(table), near(patch_zero), near(patch_one), near(moved), near(far),
-        *[near(array) for array in measured],
+        probe_field, near(kernel), near(table), near(patch_zero), near(patch_one), near(moved), near(far),
+        *[near(measured[s]) for s in range(row_count)],
     )
+    (rim_grad,) = call(
+        functools.partial(place_rim_kernel, height=height),
+        [vector_block, whole(grad_shape)],
+        [whole((planes, n, width))],
+        [kept((planes, n, width), jnp.bfloat16)],
+        12,
+        "place_rim",
+        scratch=[pltpu.VMEM((planes, n, row_count * n), jnp.bfloat16)],
+        steps=1,
+    )(near(vectors), near(grads))
     (part,) = call(
         place_kernel,
-        [whole(grad_shape), whole((planes, height, width))],
+        [vector_block, whole(grad_shape), whole((planes, height, width))],
         [whole((planes, height, width))],
         [kept((planes, height, width), jnp.float32)],
-        16,
+        12,
         "place",
+        scratch=[pltpu.VMEM((planes, height, row_count * n), jnp.bfloat16)],
         steps=1,
-    )(near(spots), near(grads), slab)
-
-    rim_grad = from_behind(rim_grad, "row", 1)
-    mine, other, part = probe_sum(keep, send, part)
+    )(near(vectors), near(grads), slab)
+
+    mine, other, rim_grad, part = probe_sum(keep, send, rim_grad, part)
     updated_slab = pl.pallas_call(
         finish_kernel,
-        grid=(planes,),
-        in_specs=[
-            pl.BlockSpec((1, height, width), lambda i: (i, 0, 0)),
-            pl.BlockSpec((1, n, width), lambda i: (i, 0, 0)),
+        in_specs=[vmem, vmem],
+        out_specs=hbm,
+        out_shape=pltpu.HBM((planes, height, width), jnp.float32),
+        scratch_shapes=[
+            pltpu.VMEM((planes, height, width), jnp.float32),
+            pltpu.SemaphoreType.DMA((planes * len(chunks(height, 128)),)),
         ],
-        out_specs=pl.BlockSpec((1, height, width), lambda i: (i, 0, 0)),
-        out_shape=jax.ShapeDtypeStruct((planes, height, width), jnp.float32),
         compiler_params=pltpu.CompilerParams(vmem_limit_bytes=SMALL_VMEM),
         name="finish",
     )(near(part), near(rim_grad)).reshape(object_slab.shape)
+    other, updated_slab = lax.optimization_barrier((other, updated_slab))
     (updated_probe,) = small_call(
         functools.partial(probe_kernel, scale=step_probe / (row_count * col_count * slot_count)),
         [probe_field, mine, other],

time: 58.9 us -> 50.9 us (0.86)
  Pallas kernels: 28 us -> 21.6 us
  starting transfers between devices: 17 us -> 13.8 us
  waiting for transfers between devices: 12.7 us -> 14.4 us
    pallas_call x8, Pallas kernels: 27 us -> 20.6 us  [the longest x1 4.61 us: per_device(): call(functools.partial(third_kernel, steps=row_count // count), [whole(pl...]
    ppermute x3, waiting for transfers between devices: 0.01 us -> 5.8 us  [around(): lax.ppermute(block, axis, [(i, (i + distance) % size) for i in range(size)])]
    ppermute x10, waiting for transfers between devices: 12.7 us -> 8.58 us  [permute_pairs(): lax.ppermute(block, axis, [(i, partner(i)) for i in range(lax.axis_size(a...]
    ppermute x10, starting transfers between devices: 12 us -> 10.4 us  [permute_pairs(): lax.ppermute(block, axis, [(i, partner(i)) for i in range(lax.axis_size(a...]
    ppermute x3, starting transfers between devices: 4.98 us -> 3.45 us  [around(): lax.ppermute(block, axis, [(i, (i + distance) % size) for i in range(size)])]
  transfers between devices with their start and end apart: 13 -> 13, of which waited for: 7 -> 7; matrix products, arithmetic and copies ran while one was open for 0% -> 0% of each run, Pallas kernels for 28% -> 29%
where the time goes in v1:
time: 50.9 us; the launch traced here: 50.7 us
  Pallas kernels  21.6 us (42%)
  waiting for transfers between devices  14.4 us (28%)
  starting transfers between devices  13.8 us (27%)
  between operations  0.81 us (2%)
    ppermute x10, starting transfers between devices, permute_pairs(): lax.ppermute(block, axis, [(i, partner(i)) for i in range(lax.axis_size(a...  10.4 us
    ppermute x10, waiting for transfers between devices, permute_pairs(): lax.ppermute(block, axis, [(i, partner(i)) for i in range(lax.axis_size(a...  8.58 us
    ppermute x3, waiting for transfers between devices, around(): lax.ppermute(block, axis, [(i, (i + distance) % size) for i in range(size)])  5.8 us
    pallas_call x1, Pallas kernels, per_device(): call(functools.partial(third_kernel, steps=row_count // count), [whole(pl...  4.61 us
    pallas_call x1, Pallas kernels, per_device(): call(first_kernel, [spot_block, own_block, rim_block, whole(plane), whole...  4.07 us
    ppermute x3, starting transfers between devices, around(): lax.ppermute(block, axis, [(i, (i + distance) % size) for i in range(size)])  3.45 us
    pallas_call x1, Pallas kernels, per_device(): call(second_kernel, [spot_block, own_block, rim_block, wide_block, tables...  2.85 us
    pallas_call x1, Pallas kernels, per_device(): pl.pallas_call(prepare_kernel, in_specs=[smem, smem, vmem, hbm, hbm, vmem...  2.37 us
  transfers between devices with their start and end apart: 13, of which 7 were waited for; matrix products, arithmetic and copies ran while one was open for 0% of the time, Pallas kernels for 29%

profile of v1, /device:TPU:0, one launch (start us, length us, event | category | flops | bytes accessed | tf_op | source)
XLA Modules:
  0.0 50.7 jit_solution(12347991058011342128)
XLA Ops:
  0.6 0.0 copy-start.5
  0.6 0.0 copy-start.3
  0.7 0.0 copy-start.1
  0.7 0.0 copy-start.2
  0.7 1.4 %own_zero.1.own_ref = bf16[2,256,512]{2,1,0:T(8,128)(2,1)S(1)} custom-call(f32[4,256,512]{2,1,0:T(8,128)} %bitcast.4), custom_call_target="tpu_custom_call" | custom-call | tf_op jit(solution)/shard_map/own_zero/pallas_call | solution.py:420
  2.1 0.0 copy-start.4
  2.1 2.4 %collective-permute-start = (bf16[2,256,512]{2,1,0:T(8,128)(2,1)S(1)}, bf16[2,256,512]{2,1,0:T(8,128)(2,1)S(1)}, u32[]{:S(2)}, u32[]{:S(2)}) collective-permute-start(bf16[2,256,512]{2,1,0:T(8,128)(2,1)S(1)} %own_zero.1.own_ref), channel_id=1, source_target_pairs={{0,12},{4,0},{8,4},{12,8},{1,13},{5,1},{9,5},{13,9},{2,14},{6,2},{... | collective-permute-start | bytes 1572872 | tf_op jit(solution)/shard_map/ppermute | solution.py:27
  4.5 0.0 copy-done.5
  4.5 0.1 copy.9.corner_ref
  4.6 0.0 copy-done.3
  4.6 0.0 copy-done.1
  4.6 0.0 copy-done.2
  4.6 2.4 %prepare.1 = (bf16[2,256,512]{2,1,0:T(8,128)(2,1)S(1)}, bf16[512,512]{1,0:T(8,128)(2,1)S(1)}, f32[2,256,256]{2,1,0:T(8,128)S(1)}, s32[4,2,8,128]{3,2,1,0:T(8,128...) custom-call(s32[4,2]{1,0:T(4,128)S(1)} %copy.9.corner_ref, ...), custom_call_target="tpu_custom_call" | custom-call | tf_op jit(solution)/shard_map/prepare/pallas_call | solution.py:433
  7.0 0.9 %collective-permute-start.1 = (bf16[2,256,512]{2,1,0:T(8,128)(2,1)S(1)}, bf16[2,256,512]{2,1,0:T(8,128)(2,1)S(1)}, u32[]{:S(2)}, u32[]{:S(2)}) collective-permute-start(bf16[2,256,512]{2,1,0:T(8,128)(2,1)S(1)} %get-tuple-element.32.own_ref), channel_id=1, source_target_pairs={{0,12},{4,0},{8,4},{12,8},{1,13},{5,1},{9,5},{13,9},{2,14},{6,2},{... | collective-permute-start | bytes 1572872 | tf_op jit(solution)/shard_map/ppermute | solution.py:27
  7.9 0.0 collective-permute-start.2
  7.9 0.5 collective-permute-start.3
  8.4 1.4 %collective-permute-start.4 = (bf16[256,256]{1,0:T(8,128)(2,1)S(1)}, bf16[256,256]{1,0:T(8,128)(2,1)S(1)}, u32[]{:S(2)}, u32[]{:S(2)}) collective-permute-start(bf16[256,256]{1,0:T(8,128)(2,1)S(1)} %get-tuple-element.39), channel_id=1, source_target_pairs={{0,12},{4,8},{8,4},{12,0},{1,13},{5,9},{9,5},{13,1},{2,14},{6,10},... | collective-permute-start | bytes 393224 | tf_op jit(solution)/shard_map/ppermute | solution.py:22
  9.8 3.8 %collective-permute-done.rim_ref = bf16[2,256,512]{2,1,0:T(8,128)(2,1)S(1)} collective-permute-done((bf16[2,256,512]{2,1,0:T(8,128)(2,1)S(1)}, bf16[2,256,512]{2,1,0:T(8,128)(2,1)S(1)}, u32[]{:S(2)}, u32[]{:S(2)}) %collective-permute-start) | collective-permute-done | bytes 524320 | tf_op jit(solution)/shard_map/ppermute | solution.py:27
  13.6 0.0 copy-done.4
  13.6 4.1 %moved.1 = (bf16[4,2,256,256]{3,2,1,0:T(8,128)(2,1)S(1)}, f32[4,256,512]{2,1,0:T(8,128)S(1)}) custom-call(s32[8,128]{1,0:T(8,128)S(1)} %get-tuple-element.30.spot_ref, bf16[2,256,512]{2,1,0:T(8,128)(2,1)S(1)} %own_zero.1.own_ref, bf16[2,256,512]{2,1,0:T(8,128)(2,1)S(1)} %collective-permute-done.rim_ref, f32[2,256,256]{2,1,0:T(8,128)S(1)} %copy-done.4, ...), custom_call_target="tpu_custom_call" | custom-call | flops 3758096384 | bytes 2097152 | tf_op jit(solution)/shard_map/moved/pallas_call | solution.py:491
  17.7 2.0 %collective-permute-done.1.rim_ref = bf16[2,256,512]{2,1,0:T(8,128)(2,1)S(1)} collective-permute-done((bf16[2,256,512]{2,1,0:T(8,128)(2,1)S(1)}, bf16[2,256,512]{2,1,0:T(8,128)(2,1)S(1)}, u32[]{:S(2)}, u32[]{:S(2)}) %collective-permute-start.1) | collective-permute-done | bytes 524320 | tf_op jit(solution)/shard_map/ppermute | solution.py:27
  19.7 2.9 %far.1 = (bf16[4,2,256,256]{3,2,1,0:T(8,128)(2,1)S(1)}, f32[4,256,512]{2,1,0:T(8,128)S(1)}) custom-call(s32[8,128]{1,0:T(8,128)S(1)} %get-tuple-element.30.spot_ref, bf16[2,256,512]{2,1,0:T(8,128)(2,1)S(1)} %get-tuple-element.32.own_ref, bf16[2,256,512]{2,1,0:T(8,128)(2,1)S(1)} %collective-permute-done.1.rim_ref, ...), custom_call_target="tpu_custom_call" | custom-call | flops 2684354560 | bytes 2097152 | tf_op jit(solution)/shard_map/far/pallas_call | solution.py:503
  22.5 0.0 collective-permute-done.2.rest_1_
  22.5 0.0 collective-permute-done.3.rest_2_
  22.6 0.0 collective-permute-done.4.rest_3_
  22.6 4.6 %gradients.1 = (bf16[4,4,256,256]{3,2,1,0:T(8,128)(2,1)S(1)}, f32[256,256]{1,0:T(8,128)S(1)}, bf16[256,256]{1,0:T(8,128)(2,1)S(1)}) custom-call(f32[2,256,256]{2,1,0:T(8,128)S(1)} %copy-done.4, f32[2,256,256]{2,1,0:T(8,128)S(1)} %get-tuple-element.28.kernel_ref, bf16[512,512]{1,0:T(8,128)(2,1)S(1)} %get-tuple-element.29.table_ref, ...), custom_call_target="tpu_custom_call" | custom-call | flops 3221225472 | bytes 2097152 | tf_op jit(solution)/shard_map/gradients/pallas_call | solution.py:513
  27.2 0.9 %collective-permute-start.5 = (bf16[256,256]{1,0:T(8,128)(2,1)S(1)}, bf16[256,256]{1,0:T(8,128)(2,1)S(1)}, u32[]{:S(2)}, u32[]{:S(2)}) collective-permute-start(bf16[256,256]{1,0:T(8,128)(2,1)S(1)} %get-tuple-element.41), channel_id=1, source_target_pairs={{0,4},{4,0},{8,12},{12,8},{1,5},{5,1},{9,13},{13,9},{2,6},{6,2},{1... | collective-permute-start | bytes 393224 | tf_op jit(solution)/shard_map/ppermute | solution.py:22
  28.1 1.0 %collective-permute-done.5.other_ref = bf16[256,256]{1,0:T(8,128)(2,1)S(1)} collective-permute-done((bf16[256,256]{1,0:T(8,128)(2,1)S(1)}, bf16[256,256]{1,0:T(8,128)(2,1)S(1)}, u32[]{:S(2)}, u32[]{:S(2)}) %collective-permute-start.5) | collective-permute-done | bytes 131104 | tf_op jit(solution)/shard_map/ppermute | solution.py:22
  29.1 1.5 %collective-permute-start.6 = (bf16[128,256]{1,0:T(8,128)(2,1)S(1)}, bf16[128,256]{1,0:T(8,128)(2,1)S(1)}, u32[]{:S(2)}, u32[]{:S(2)}) collective-permute-start(bf16[128,256]{1,0:T(8,128)(2,1)S(1)} %get-tuple-element.43), channel_id=1, source_target_pairs={{0,8},{4,12},{8,0},{12,4},{1,9},{5,13},{9,1},{13,5},{2,10},{6,14},... | collective-permute-start | bytes 196616 | tf_op jit(solution)/shard_map/ppermute | solution.py:22
  30.7 1.9 %place_rim.1 = bf16[4,256,512]{2,1,0:T(8,128)(2,1)S(1)} custom-call(s32[4,2,8,128]{3,2,1,0:T(8,128)S(1)} %get-tuple-element.46.corner_ref, bf16[4,4,256,256]{3,2,1,0:T(8,128)(2,1)S(1)} %get-tuple-element.47.grad_ref), custom_call_target="tpu_custom_call" | custom-call | flops 1610612736 | bytes 2097152 | tf_op jit(solution)/shard_map/place_rim/pallas_call | solution.py:529
  32.6 0.1 collective-permute-start.12
  32.7 0.8 %collective-permute-done.6.rest_0_ = bf16[128,256]{1,0:T(8,128)(2,1)S(1)} collective-permute-done((bf16[128,256]{1,0:T(8,128)(2,1)S(1)}, bf16[128,256]{1,0:T(8,128)(2,1)S(1)}, u32[]{:S(2)}, u32[]{:S(2)}) %collective-permute-start.6) | collective-permute-done | bytes 65568 | tf_op jit(solution)/shard_map/ppermute | solution.py:22
  33.5 0.0 copy-start
  33.6 1.6 %collective-permute-start.9 = (bf16[128,256]{1,0:T(8,128)(2,1)S(1)}, bf16[128,256]{1,0:T(8,128)(2,1)S(1)}, u32[]{:S(2)}, u32[]{:S(2)}) collective-permute-start(bf16[128,256]{1,0:T(8,128)(2,1)S(1)} %get-tuple-element.45), channel_id=1, source_target_pairs={{0,1},{1,0},{2,3},{3,2},{4,5},{5,4},{6,7},{7,6},{8,9},{9,8},{10,11... | collective-permute-start | bytes 196616 | tf_op jit(solution)/shard_map/ppermute | solution.py:22
  35.2 2.6 %collective-permute-start.8 = (bf16[128,256]{1,0:T(8,128)(2,1)S(1)}, bf16[128,256]{1,0:T(8,128)(2,1)S(1)}, u32[]{:S(2)}, u32[]{:S(2)}) collective-permute-start(bf16[128,256]{1,0:T(8,128)(2,1)S(1)} %get-tuple-element.45), channel_id=1, source_target_pairs={{0,2},{1,3},{2,0},{3,1},{4,6},{5,7},{6,4},{7,5},{8,10},{9,11},{10,... | collective-permute-start | bytes 196616 | tf_op jit(solution)/shard_map/ppermute | solution.py:22
  37.8 0.2 collective-permute-start.7
  38.0 0.0 copy-done
  38.0 1.9 %place.1.part_ref = f32[4,256,512]{2,1,0:T(8,128)S(1)} custom-call(s32[4,2,8,128]{3,2,1,0:T(8,128)S(1)} %get-tuple-element.46.corner_ref, bf16[4,4,256,256]{3,2,1,0:T(8,128)(2,1)S(1)} %get-tuple-element.47.grad_ref, f32[4,256,512]{2,1,0:T(8,128)S(1)} %bitcast.6), custom_call_target="tpu_custom_call" | custom-call | flops 1610612736 | bytes 2097152 | tf_op jit(solution)/shard_map/place/pallas_call | solution.py:539
  40.0 0.0 collective-permute-done.9.rest_2_
  40.0 2.5 %collective-permute-done.8.rest_1_ = bf16[128,256]{1,0:T(8,128)(2,1)S(1)} collective-permute-done((bf16[128,256]{1,0:T(8,128)(2,1)S(1)}, bf16[128,256]{1,0:T(8,128)(2,1)S(1)}, u32[]{:S(2)}, u32[]{:S(2)}) %collective-permute-start.8) | collective-permute-done | bytes 65568 | tf_op jit(solution)/shard_map/ppermute | solution.py:22
  42.4 1.4 %collective-permute-done.7.rest_0_ = bf16[128,256]{1,0:T(8,128)(2,1)S(1)} collective-permute-done((bf16[128,256]{1,0:T(8,128)(2,1)S(1)}, bf16[128,256]{1,0:T(8,128)(2,1)S(1)}, u32[]{:S(2)}, u32[]{:S(2)}) %collective-permute-start.7) | collective-permute-done | bytes 65568 | tf_op jit(solution)/shard_map/ppermute | solution.py:22
  43.9 1.5 %collective-permute-start.10 = (bf16[128,256]{1,0:T(8,128)(2,1)S(1)}, bf16[128,256]{1,0:T(8,128)(2,1)S(1)}, u32[]{:S(2)}, u32[]{:S(2)}) collective-permute-start(bf16[128,256]{1,0:T(8,128)(2,1)S(1)} %full_sum.1.mine_ref), channel_id=1, source_target_pairs={{0,8},{4,12},{8,0},{12,4},{1,9},{5,13},{9,1},{13,5},{2,10},{6,14},... | collective-permute-start | bytes 196616 | tf_op jit(solution)/shard_map/ppermute | solution.py:22
  45.4 2.8 %collective-permute-done.10.rest_0_ = bf16[128,256]{1,0:T(8,128)(2,1)S(1)} collective-permute-done((bf16[128,256]{1,0:T(8,128)(2,1)S(1)}, bf16[128,256]{1,0:T(8,128)(2,1)S(1)}, u32[]{:S(2)}, u32[]{:S(2)}) %collective-permute-start.10) | collective-permute-done | bytes 65568 | tf_op jit(solution)/shard_map/ppermute | solution.py:22
  48.3 0.1 collective-permute-start.11
  48.4 0.0 collective-permute-done.12.rim_ref
  48.4 1.4 %finish.1 = f32[4,256,512]{2,1,0:T(8,128)} custom-call(f32[4,256,512]{2,1,0:T(8,128)S(1)} %place.1.part_ref, bf16[4,256,512]{2,1,0:T(8,128)(2,1)S(1)} %collective-permute-done.12.rim_ref), custom_call_target="tpu_custom_call" | custom-call | tf_op jit(solution)/shard_map/finish/pallas_call | solution.py:551
  49.8 0.0 collective-permute-done.11.other_ref
  49.8 0.9 %update_probe.1 = f32[2,256,256]{2,1,0:T(8,128)} custom-call(f32[2,256,256]{2,1,0:T(8,128)S(1)} %copy-done.4, bf16[256,256]{1,0:T(8,128)(2,1)S(1)} %gather_half.1.mine_ref, bf16[256,256]{1,0:T(8,128)(2,1)S(1)} %collective-permute-done.11.other_ref), custom_call_target="tpu_custom_call" | custom-call | flops 4000000000 | bytes 262144 | tf_op jit(solution)/shard_map/update_probe/pallas_call | solution.py:362
  (4 shorter events, 0.1 us)
Async XLA Ops:
  0.6 3.9 %copy-start.5 = (s32[4,1,2]{0,2,1:T(2,128)S(1)}, s32[4,1,2]{0,2,1:T(2,128)}, u32[]{:S(2)}) copy-start(s32[4,1,2]{0,2,1:T(2,128)} %param.11) | copy-start | bytes 100
  0.6 4.0 %copy-start.3 = (s32[2,1]{0,1:T(1,128)S(1)}, s32[2,1]{0,1:T(1,128)}, u32[]{:S(2)}) copy-start(s32[2,1]{0,1:T(1,128)} %param.12) | copy-start | bytes 28
  0.7 4.0 %copy-start.1 = (f32[2,256,256]{2,1,0:T(8,128)S(1)}, f32[2,256,256]{2,1,0:T(8,128)}, u32[]{:S(2)}) copy-start(f32[2,256,256]{2,1,0:T(8,128)} %intensity_ref.1) | copy-start | bytes 1572868
  0.7 4.0 %copy-start.2 = (f32[256,256]{1,0:T(8,128)S(1)}, f32[256,256]{1,0:T(8,128)}, u32[]{:S(2)}) copy-start(f32[256,256]{1,0:T(8,128)} %phase_ref.1) | copy-start | bytes 786436
  2.1 11.5 %copy-start.4 = (f32[2,256,256]{2,1,0:T(8,128)S(1)}, f32[2,256,256]{2,1,0:T(8,128)}, u32[]{:S(2)}) copy-start(f32[2,256,256]{2,1,0:T(8,128)} %probe_ref.5) | copy-start | bytes 1572868
  2.1 11.5 %collective-permute-start = (bf16[2,256,512]{2,1,0:T(8,128)(2,1)S(1)}, bf16[2,256,512]{2,1,0:T(8,128)(2,1)S(1)}, u32[]{:S(2)}, u32[]{:S(2)}) collective-permute-start(bf16[2,256,512]{2,1,0:T(8,128)(2,1)S(1)} %own_zero.1.own_ref), channel_id=1, source_target_pairs={{0,12},{4,0},{8,4},{12,8},{1,13},{5,1},{9,5},{13,9},{2,14},{6,2},{... | collective-permute-start | bytes 1572872 | tf_op jit(solution)/shard_map/ppermute | solution.py:27
  7.0 12.6 %collective-permute-start.1 = (bf16[2,256,512]{2,1,0:T(8,128)(2,1)S(1)}, bf16[2,256,512]{2,1,0:T(8,128)(2,1)S(1)}, u32[]{:S(2)}, u32[]{:S(2)}) collective-permute-start(bf16[2,256,512]{2,1,0:T(8,128)(2,1)S(1)} %get-tuple-element.32.own_ref), channel_id=1, source_target_pairs={{0,12},{4,0},{8,4},{12,8},{1,13},{5,1},{9,5},{13,9},{2,14},{6,2},{... | collective-permute-start | bytes 1572872 | tf_op jit(solution)/shard_map/ppermute | solution.py:27
  7.9 14.6 %collective-permute-start.2 = (bf16[256,256]{1,0:T(8,128)(2,1)S(1)}, bf16[256,256]{1,0:T(8,128)(2,1)S(1)}, u32[]{:S(2)}, u32[]{:S(2)}) collective-permute-start(bf16[256,256]{1,0:T(8,128)(2,1)S(1)} %get-tuple-element.37), channel_id=1, source_target_pairs={{0,4},{4,0},{8,12},{12,8},{1,5},{5,1},{9,13},{13,9},{2,6},{6,2},{1... | collective-permute-start | bytes 393224 | tf_op jit(solution)/shard_map/ppermute | solution.py:22
  7.9 14.6 %collective-permute-start.3 = (bf16[256,256]{1,0:T(8,128)(2,1)S(1)}, bf16[256,256]{1,0:T(8,128)(2,1)S(1)}, u32[]{:S(2)}, u32[]{:S(2)}) collective-permute-start(bf16[256,256]{1,0:T(8,128)(2,1)S(1)} %get-tuple-element.38), channel_id=1, source_target_pairs={{0,8},{4,12},{8,0},{12,4},{1,9},{5,13},{9,1},{13,5},{2,10},{6,14},... | collective-permute-start | bytes 393224 | tf_op jit(solution)/shard_map/ppermute | solution.py:22
  8.4 14.1 %collective-permute-start.4 = (bf16[256,256]{1,0:T(8,128)(2,1)S(1)}, bf16[256,256]{1,0:T(8,128)(2,1)S(1)}, u32[]{:S(2)}, u32[]{:S(2)}) collective-permute-start(bf16[256,256]{1,0:T(8,128)(2,1)S(1)} %get-tuple-element.39), channel_id=1, source_target_pairs={{0,12},{4,8},{8,4},{12,0},{1,13},{5,9},{9,5},{13,1},{2,14},{6,10},... | collective-permute-start | bytes 393224 | tf_op jit(solution)/shard_map/ppermute | solution.py:22
  27.2 1.9 %collective-permute-start.5 = (bf16[256,256]{1,0:T(8,128)(2,1)S(1)}, bf16[256,256]{1,0:T(8,128)(2,1)S(1)}, u32[]{:S(2)}, u32[]{:S(2)}) collective-permute-start(bf16[256,256]{1,0:T(8,128)(2,1)S(1)} %get-tuple-element.41), channel_id=1, source_target_pairs={{0,4},{4,0},{8,12},{12,8},{1,5},{5,1},{9,13},{13,9},{2,6},{6,2},{1... | collective-permute-start | bytes 393224 | tf_op jit(solution)/shard_map/ppermute | solution.py:22
  29.1 4.4 %collective-permute-start.6 = (bf16[128,256]{1,0:T(8,128)(2,1)S(1)}, bf16[128,256]{1,0:T(8,128)(2,1)S(1)}, u32[]{:S(2)}, u32[]{:S(2)}) collective-permute-start(bf16[128,256]{1,0:T(8,128)(2,1)S(1)} %get-tuple-element.43), channel_id=1, source_target_pairs={{0,8},{4,12},{8,0},{12,4},{1,9},{5,13},{9,1},{13,5},{2,10},{6,14},... | collective-permute-start | bytes 196616 | tf_op jit(solution)/shard_map/ppermute | solution.py:22
  32.6 15.8 %collective-permute-start.12 = (bf16[4,256,512]{2,1,0:T(8,128)(2,1)S(1)}, bf16[4,256,512]{2,1,0:T(8,128)(2,1)S(1)}, u32[]{:S(2)}, u32[]{:S(2)}) collective-permute-start(bf16[4,256,512]{2,1,0:T(8,128)(2,1)S(1)} %place_rim.1), channel_id=1, source_target_pairs={{0,4},{4,8},{8,12},{12,0},{1,5},{5,9},{9,13},{13,1},{2,6},{6,10},{... | collective-permute-start | bytes 3145736 | tf_op jit(solution)/shard_map/ppermute | solution.py:27
  33.5 4.5 %copy-start = (f32[2,2,256,512]{3,2,1,0:T(8,128)S(1)}, f32[2,2,256,512]{3,2,1,0:T(8,128)}, u32[]{:S(2)}) copy-start(f32[2,2,256,512]{3,2,1,0:T(8,128)} %param.7) | copy-start | bytes 6291460
  33.6 6.4 %collective-permute-start.9 = (bf16[128,256]{1,0:T(8,128)(2,1)S(1)}, bf16[128,256]{1,0:T(8,128)(2,1)S(1)}, u32[]{:S(2)}, u32[]{:S(2)}) collective-permute-start(bf16[128,256]{1,0:T(8,128)(2,1)S(1)} %get-tuple-element.45), channel_id=1, source_target_pairs={{0,1},{1,0},{2,3},{3,2},{4,5},{5,4},{6,7},{7,6},{8,9},{9,8},{10,11... | collective-permute-start | bytes 196616 | tf_op jit(solution)/shard_map/ppermute | solution.py:22
  35.2 7.2 %collective-permute-start.8 = (bf16[128,256]{1,0:T(8,128)(2,1)S(1)}, bf16[128,256]{1,0:T(8,128)(2,1)S(1)}, u32[]{:S(2)}, u32[]{:S(2)}) collective-permute-start(bf16[128,256]{1,0:T(8,128)(2,1)S(1)} %get-tuple-element.45), channel_id=1, source_target_pairs={{0,2},{1,3},{2,0},{3,1},{4,6},{5,7},{6,4},{7,5},{8,10},{9,11},{10,... | collective-permute-start | bytes 196616 | tf_op jit(solution)/shard_map/ppermute | solution.py:22
  37.8 6.1 %collective-permute-start.7 = (bf16[128,256]{1,0:T(8,128)(2,1)S(1)}, bf16[128,256]{1,0:T(8,128)(2,1)S(1)}, u32[]{:S(2)}, u32[]{:S(2)}) collective-permute-start(bf16[128,256]{1,0:T(8,128)(2,1)S(1)} %get-tuple-element.45), channel_id=1, source_target_pairs={{0,3},{1,2},{2,1},{3,0},{4,7},{5,6},{6,5},{7,4},{8,11},{9,10},{10,... | collective-permute-start | bytes 196616 | tf_op jit(solution)/shard_map/ppermute | solution.py:22
  43.9 4.4 %collective-permute-start.10 = (bf16[128,256]{1,0:T(8,128)(2,1)S(1)}, bf16[128,256]{1,0:T(8,128)(2,1)S(1)}, u32[]{:S(2)}, u32[]{:S(2)}) collective-permute-start(bf16[128,256]{1,0:T(8,128)(2,1)S(1)} %full_sum.1.mine_ref), channel_id=1, source_target_pairs={{0,8},{4,12},{8,0},{12,4},{1,9},{5,13},{9,1},{13,5},{2,10},{6,14},... | collective-permute-start | bytes 196616 | tf_op jit(solution)/shard_map/ppermute | solution.py:22
  48.3 1.5 %collective-permute-start.11 = (bf16[256,256]{1,0:T(8,128)(2,1)S(1)}, bf16[256,256]{1,0:T(8,128)(2,1)S(1)}, u32[]{:S(2)}, u32[]{:S(2)}) collective-permute-start(bf16[256,256]{1,0:T(8,128)(2,1)S(1)} %gather_half.1.mine_ref), channel_id=1, source_target_pairs={{0,4},{4,0},{8,12},{12,8},{1,5},{5,1},{9,13},{13,9},{2,6},{6,2},{1... | collective-permute-start | bytes 393224 | tf_op jit(solution)/shard_map/ppermute | solution.py:22

commit v2 on v1

--- a/solution.py
+++ b/solution.py
@@ -11,7 +11,7 @@
 
 step_object = 0.05
 step_probe = 0.5
-SMALL_FLOPS = 4000000000
+SMALL_FLOPS = 1000000000
 LATE_FROM = 99
 SMALL_VMEM = 8 * 1024 * 1024
 LARGE_VMEM = 24 * 1024 * 1024
@@ -46,6 +46,7 @@
         middle = product(table_ref[...], field_ref[p])
         middle_ref[p, :, n:] = middle[:n].astype(jnp.bfloat16)
         middle_ref[p, :, :n] = middle[n:].astype(jnp.bfloat16)
+    for p in positions:
         out_ref[p] = product(middle_ref[p], table_ref[...])
 
 
@@ -262,13 +263,14 @@
         end()
 
 
-def placed(corner_ref, grad_ref, tall_ref, rows, width, first_row):
-    planes, positions, n, _ = grad_ref.shape
+def placed(corner_ref, grad_ref, tall_ref, rows, width, first_row, first_plane):
+    planes = tall_ref.shape[0]
+    _, positions, n, _ = grad_ref.shape
     moves = []
     for p in range(positions):
         corner_y, corner_x = spot(corner_ref, p)
         moves.append(one_hot_rows((n, width), corner_x))
-        every = jnp.concatenate([grad_ref[plane, p] for plane in range(planes)], 1)
+        every = jnp.concatenate([grad_ref[first_plane + plane, p] for plane in range(planes)], 1)
         tall = product(one_hot_columns((rows, n), corner_y - first_row), every).astype(jnp.bfloat16)
         for plane in range(planes):
             tall_ref[plane, :, p * n : (p + 1) * n] = tall[:, plane * n : (plane + 1) * n]
@@ -277,15 +279,15 @@
         yield plane, product(tall_ref[plane], moves)
 
 
-def place_rim_kernel(corner_ref, grad_ref, rim_ref, tall_ref, *, height):
+def place_rim_kernel(corner_ref, grad_ref, rim_ref, tall_ref, *, height, first_plane):
     rows, width = rim_ref.shape[1:]
-    for plane, total in placed(corner_ref, grad_ref, tall_ref, rows, width, height):
+    for plane, total in placed(corner_ref, grad_ref, tall_ref, rows, width, height, first_plane):
         rim_ref[plane] = total.astype(jnp.bfloat16)
 
 
 def place_kernel(corner_ref, grad_ref, slab_ref, part_ref, tall_ref):
     rows, width = part_ref.shape[1:]
-    for plane, total in placed(corner_ref, grad_ref, tall_ref, rows, width, 0):
+    for plane, total in placed(corner_ref, grad_ref, tall_ref, rows, width, 0, 0):
         part_ref[plane] = slab_ref[plane] - step_object * total
 
 
@@ -293,14 +295,16 @@
     return pltpu.with_memory_space_constraint(array, pltpu.HBM)
 
 
-def finish_kernel(part_ref, rim_ref, out_hbm, sums_ref, sems):
+def finish_kernel(part_ref, *rest):
+    rim_refs, (out_hbm, sums_ref, sems) = rest[:-3], rest[-3:]
+    each, rim_rows, _ = rim_refs[0].shape
     parts = [(c, rows) for c in range(part_ref.shape[0]) for rows in chunks(part_ref.shape[1], 128)]
     copies = []
     step = jnp.where(lax.axis_index("row") == 0, 0.0, step_object)
     for i, (c, rows) in enumerate(parts):
         value = part_ref[c, rows]
-        if rows.start < rim_ref.shape[1]:
-            value -= step * rim_ref[c, rows].astype(jnp.float32)
+        if rows.start < rim_rows:
+            value -= step * rim_refs[c // each][c % each, rows].astype(jnp.float32)
         sums_ref[c, rows] = value
         copies.append(pltpu.make_async_copy(sums_ref.at[c, rows], out_hbm.at[c, rows], sems.at[i]))
         copies[-1].start()
@@ -371,26 +375,28 @@
     )(*arrays)
 
 
-def probe_sum(keep, send, rim_grad, part):
+def probe_sum(keep, send, rim_grads, part):
     n = keep.shape[0]
     row_count, col_count = lax.axis_size("row"), lax.axis_size("col")
     chips = row_count // 2
     shape = (n // chips, n)
     wide, narrow = jax.ShapeDtypeStruct(shape, jnp.float32), jax.ShapeDtypeStruct(shape, jnp.bfloat16)
     other = permute_pairs(send, "row", lambda i: i ^ 1)
-    rim_grad = around(rim_grad, "row", 1)
+    other, rim_grads[0] = lax.optimization_barrier((other, rim_grads[0]))
+    rim_grads = [around(rim_grad, "row", 1) for rim_grad in rim_grads]
     mine, *sends = small_call(
         half_sum_kernel, [keep, other], [wide] + [narrow] * (chips - 1), "half_sum", [pltpu.VMEM((n, n), jnp.float32)]
     )
     others = [permute_pairs(sends[s - 1], "row", lambda i: i ^ (2 * s)) for s in range(1, chips)]
     total, send = small_call(row_sum_kernel, [mine, *others], [wide, narrow], "row_sum")
-    others = [permute_pairs(send, "col", lambda i: i ^ s) for s in range(col_count - 1, 0, -1)]
+    steps = [1] + list(range(col_count - 1, 1, -1)) if col_count > 1 else []
+    others = [permute_pairs(send, "col", lambda i: i ^ s) for s in steps]
     others, part = lax.optimization_barrier((others, part))
     (total,) = small_call(full_sum_kernel, [total, *others], [narrow], "full_sum")
     others = [permute_pairs(total, "row", lambda i: i ^ (2 * s)) for s in range(1, chips)]
     half = jax.ShapeDtypeStruct((n, n), jnp.bfloat16)
     (mine,) = small_call(gather_kernel, [total, *others], [half], "gather_half")
-    return mine, permute_pairs(mine, "row", lambda i: i ^ 1), rim_grad, part
+    return mine, permute_pairs(mine, "row", lambda i: i ^ 1), rim_grads, part
 
 
 def per_device(object_slab, probe_field, prop_phase, intensities, corners, slot_source):
@@ -526,16 +532,18 @@
         probe_field, near(kernel), near(table), near(patch_zero), near(patch_one), near(moved), near(far),
         *[near(measured[s]) for s in range(row_count)],
     )
-    (rim_grad,) = call(
-        functools.partial(place_rim_kernel, height=height),
-        [vector_block, whole(grad_shape)],
-        [whole((planes, n, width))],
-        [kept((planes, n, width), jnp.bfloat16)],
-        12,
-        "place_rim",
-        scratch=[pltpu.VMEM((planes, n, row_count * n), jnp.bfloat16)],
-        steps=1,
-    )(near(vectors), near(grads))
+    rim_grads = []
+    for piece in range(slice_count):
+        rim_grads += call(
+            functools.partial(place_rim_kernel, height=height, first_plane=piece * pair_count),
+            [vector_block, whole(grad_shape)],
+            [whole((pair_count, n, width))],
+            [kept((pair_count, n, width), jnp.bfloat16)],
+            6,
+            "place_rim",
+            scratch=[pltpu.VMEM((pair_count, n, row_count * n), jnp.bfloat16)],
+            steps=1,
+        )(near(vectors), near(grads))
     (part,) = call(
         place_kernel,
         [vector_block, whole(grad_shape), whole((planes, height, width))],
@@ -547,10 +555,10 @@
         steps=1,
     )(near(vectors), near(grads), slab)
 
-    mine, other, rim_grad, part = probe_sum(keep, send, rim_grad, part)
+    mine, other, rim_grads, part = probe_sum(keep, send, rim_grads, part)
     updated_slab = pl.pallas_call(
         finish_kernel,
-        in_specs=[vmem, vmem],
+        in_specs=[vmem] * (1 + slice_count),
         out_specs=hbm,
         out_shape=pltpu.HBM((planes, height, width), jnp.float32),
         scratch_shapes=[
@@ -559,7 +567,7 @@
         ],
         compiler_params=pltpu.CompilerParams(vmem_limit_bytes=SMALL_VMEM),
         name="finish",
-    )(near(part), near(rim_grad)).reshape(object_slab.shape)
+    )(near(part), *[near(rim) for rim in rim_grads]).reshape(object_slab.shape)
     other, updated_slab = lax.optimization_barrier((other, updated_slab))
     (updated_probe,) = small_call(
         functools.partial(probe_kernel, scale=step_probe / (row_count * col_count * slot_count)),

time: 50.9 us -> 49.8 us (0.978)
  waiting for transfers between devices: 14.4 us -> 13.1 us
    ppermute x10, waiting for transfers between devices: 8.58 us -> 7.25 us  [permute_pairs(): lax.ppermute(block, axis, [(i, partner(i)) for i in range(lax.axis_size(a...]
    ppermute x3 -> x4, starting transfers between devices: 3.45 us -> 4.07 us  [around(): lax.ppermute(block, axis, [(i, (i + distance) % size) for i in range(size)])]
    pallas_call x2 -> x3, Pallas kernels: 3.33 us -> 3.65 us  [the longest x2 2.24 us: per_device(): call(functools.partial(place_rim_kernel, height=height, first_plane=piece...]
    ppermute x3 -> x4, waiting for transfers between devices: 5.8 us -> 5.9 us  [around(): lax.ppermute(block, axis, [(i, (i + distance) % size) for i in range(size)])]
  transfers between devices with their start and end apart: 13 -> 14, of which waited for: 7 -> 7; matrix products, arithmetic and copies ran while one was open for 0% -> 0% of each run, Pallas kernels for 29% -> 30%
where the time goes in v2:
time: 49.8 us; the launch traced here: 49.6 us
  Pallas kernels  21.3 us (43%)
  starting transfers between devices  14.2 us (29%)
  waiting for transfers between devices  13.1 us (26%)
  between operations  0.84 us (2%)
    ppermute x10, starting transfers between devices, permute_pairs(): lax.ppermute(block, axis, [(i, partner(i)) for i in range(lax.axis_size(a...  10.1 us
    ppermute x10, waiting for transfers between devices, permute_pairs(): lax.ppermute(block, axis, [(i, partner(i)) for i in range(lax.axis_size(a...  7.25 us
    ppermute x4, waiting for transfers between devices, around(): lax.ppermute(block, axis, [(i, (i + distance) % size) for i in range(size)])  5.9 us
    pallas_call x1, Pallas kernels, per_device(): call(functools.partial(third_kernel, steps=row_count // count), [whole(pl...  4.23 us
    ppermute x4, starting transfers between devices, around(): lax.ppermute(block, axis, [(i, (i + distance) % size) for i in range(size)])  4.07 us
    pallas_call x1, Pallas kernels, per_device(): call(first_kernel, [spot_block, own_block, rim_block, whole(plane), whole...  3.97 us
    pallas_call x1, Pallas kernels, per_device(): call(second_kernel, [spot_block, own_block, rim_block, wide_block, tables...  2.72 us
    pallas_call x1, Pallas kernels, per_device(): pl.pallas_call(prepare_kernel, in_specs=[smem, smem, vmem, hbm, hbm, vmem...  2.37 us
  transfers between devices with their start and end apart: 14, of which 7 were waited for; matrix products, arithmetic and copies ran while one was open for 0% of the time, Pallas kernels for 30%

profile of v2, /device:TPU:0, one launch (start us, length us, event | category | flops | bytes accessed | tf_op | source)
XLA Modules:
  0.0 49.6 jit_solution(16149362955036846098)
XLA Ops:
  0.6 0.0 copy-start.5
  0.6 0.0 copy-start.3
  0.7 0.0 copy-start.1
  0.7 0.0 copy-start.2
  0.7 1.4 %own_zero.1.own_ref = bf16[2,256,512]{2,1,0:T(8,128)(2,1)S(1)} custom-call(f32[4,256,512]{2,1,0:T(8,128)} %bitcast.4), custom_call_target="tpu_custom_call" | custom-call | tf_op jit(solution)/shard_map/own_zero/pallas_call | solution.py:426
  2.1 0.0 copy-start.4
  2.1 2.4 %collective-permute-start = (bf16[2,256,512]{2,1,0:T(8,128)(2,1)S(1)}, bf16[2,256,512]{2,1,0:T(8,128)(2,1)S(1)}, u32[]{:S(2)}, u32[]{:S(2)}) collective-permute-start(bf16[2,256,512]{2,1,0:T(8,128)(2,1)S(1)} %own_zero.1.own_ref), channel_id=1, source_target_pairs={{0,12},{4,0},{8,4},{12,8},{1,13},{5,1},{9,5},{13,9},{2,14},{6,2},{... | collective-permute-start | bytes 1572872 | tf_op jit(solution)/shard_map/ppermute | solution.py:27
  4.5 0.0 copy-done.5
  4.5 0.1 copy.9.corner_ref
  4.6 0.0 copy-done.3
  4.6 0.0 copy-done.1
  4.6 0.0 copy-done.2
  4.6 2.4 %prepare.1 = (bf16[2,256,512]{2,1,0:T(8,128)(2,1)S(1)}, bf16[512,512]{1,0:T(8,128)(2,1)S(1)}, f32[2,256,256]{2,1,0:T(8,128)S(1)}, s32[4,2,8,128]{3,2,1,0:T(8,128...) custom-call(s32[4,2]{1,0:T(4,128)S(1)} %copy.9.corner_ref, ...), custom_call_target="tpu_custom_call" | custom-call | tf_op jit(solution)/shard_map/prepare/pallas_call | solution.py:439
  7.0 0.9 %collective-permute-start.1 = (bf16[2,256,512]{2,1,0:T(8,128)(2,1)S(1)}, bf16[2,256,512]{2,1,0:T(8,128)(2,1)S(1)}, u32[]{:S(2)}, u32[]{:S(2)}) collective-permute-start(bf16[2,256,512]{2,1,0:T(8,128)(2,1)S(1)} %get-tuple-element.34.own_ref), channel_id=1, source_target_pairs={{0,12},{4,0},{8,4},{12,8},{1,13},{5,1},{9,5},{13,9},{2,14},{6,2},{... | collective-permute-start | bytes 1572872 | tf_op jit(solution)/shard_map/ppermute | solution.py:27
  7.9 0.0 collective-permute-start.2
  7.9 0.5 collective-permute-start.3
  8.4 1.4 %collective-permute-start.4 = (bf16[256,256]{1,0:T(8,128)(2,1)S(1)}, bf16[256,256]{1,0:T(8,128)(2,1)S(1)}, u32[]{:S(2)}, u32[]{:S(2)}) collective-permute-start(bf16[256,256]{1,0:T(8,128)(2,1)S(1)} %get-tuple-element.41), channel_id=1, source_target_pairs={{0,12},{4,8},{8,4},{12,0},{1,13},{5,9},{9,5},{13,1},{2,14},{6,10},... | collective-permute-start | bytes 393224 | tf_op jit(solution)/shard_map/ppermute | solution.py:22
  9.8 3.8 %collective-permute-done.rim_ref = bf16[2,256,512]{2,1,0:T(8,128)(2,1)S(1)} collective-permute-done((bf16[2,256,512]{2,1,0:T(8,128)(2,1)S(1)}, bf16[2,256,512]{2,1,0:T(8,128)(2,1)S(1)}, u32[]{:S(2)}, u32[]{:S(2)}) %collective-permute-start) | collective-permute-done | bytes 524320 | tf_op jit(solution)/shard_map/ppermute | solution.py:27
  13.6 0.0 copy-done.4
  13.6 4.0 %moved.1 = (bf16[4,2,256,256]{3,2,1,0:T(8,128)(2,1)S(1)}, f32[4,256,512]{2,1,0:T(8,128)S(1)}) custom-call(s32[8,128]{1,0:T(8,128)S(1)} %get-tuple-element.32.spot_ref, bf16[2,256,512]{2,1,0:T(8,128)(2,1)S(1)} %own_zero.1.own_ref, bf16[2,256,512]{2,1,0:T(8,128)(2,1)S(1)} %collective-permute-done.rim_ref, f32[2,256,256]{2,1,0:T(8,128)S(1)} %copy-done.4, ...), custom_call_target="tpu_custom_call" | custom-call | flops 3758096384 | bytes 2097152 | tf_op jit(solution)/shard_map/moved/pallas_call | solution.py:497
  17.6 2.1 %collective-permute-done.1.rim_ref = bf16[2,256,512]{2,1,0:T(8,128)(2,1)S(1)} collective-permute-done((bf16[2,256,512]{2,1,0:T(8,128)(2,1)S(1)}, bf16[2,256,512]{2,1,0:T(8,128)(2,1)S(1)}, u32[]{:S(2)}, u32[]{:S(2)}) %collective-permute-start.1) | collective-permute-done | bytes 524320 | tf_op jit(solution)/shard_map/ppermute | solution.py:27
  19.7 2.7 %far.1 = (bf16[4,2,256,256]{3,2,1,0:T(8,128)(2,1)S(1)}, f32[4,256,512]{2,1,0:T(8,128)S(1)}) custom-call(s32[8,128]{1,0:T(8,128)S(1)} %get-tuple-element.32.spot_ref, bf16[2,256,512]{2,1,0:T(8,128)(2,1)S(1)} %get-tuple-element.34.own_ref, bf16[2,256,512]{2,1,0:T(8,128)(2,1)S(1)} %collective-permute-done.1.rim_ref, ...), custom_call_target="tpu_custom_call" | custom-call | flops 2684354560 | bytes 2097152 | tf_op jit(solution)/shard_map/far/pallas_call | solution.py:509
  22.4 0.0 collective-permute-done.2.rest_1_
  22.4 0.0 collective-permute-done.3.rest_2_
  22.4 0.1 collective-permute-done.4.rest_3_
  22.5 4.2 %gradients.1 = (bf16[4,4,256,256]{3,2,1,0:T(8,128)(2,1)S(1)}, f32[256,256]{1,0:T(8,128)S(1)}, bf16[256,256]{1,0:T(8,128)(2,1)S(1)}) custom-call(f32[2,256,256]{2,1,0:T(8,128)S(1)} %copy-done.4, f32[2,256,256]{2,1,0:T(8,128)S(1)} %get-tuple-element.30.kernel_ref, bf16[512,512]{1,0:T(8,128)(2,1)S(1)} %get-tuple-element.31.table_ref, ...), custom_call_target="tpu_custom_call" | custom-call | flops 3221225472 | bytes 2097152 | tf_op jit(solution)/shard_map/gradients/pallas_call | solution.py:519
  26.7 0.9 %collective-permute-start.5 = (bf16[256,256]{1,0:T(8,128)(2,1)S(1)}, bf16[256,256]{1,0:T(8,128)(2,1)S(1)}, u32[]{:S(2)}, u32[]{:S(2)}) collective-permute-start(bf16[256,256]{1,0:T(8,128)(2,1)S(1)} %get-tuple-element.43), channel_id=1, source_target_pairs={{0,4},{4,0},{8,12},{12,8},{1,5},{5,1},{9,13},{13,9},{2,6},{6,2},{1... | collective-permute-start | bytes 393224 | tf_op jit(solution)/shard_map/ppermute | solution.py:22
  27.6 1.1 %place_rim.2 = bf16[2,256,512]{2,1,0:T(8,128)(2,1)S(1)} custom-call(s32[4,2,8,128]{3,2,1,0:T(8,128)S(1)} %get-tuple-element.44.corner_ref, bf16[4,4,256,256]{3,2,1,0:T(8,128)(2,1)S(1)} %get-tuple-element.45.grad_ref), custom_call_target="tpu_custom_call" | custom-call | flops 805306368 | bytes 2097152 | tf_op jit(solution)/shard_map/place_rim/pallas_call | solution.py:537
  28.8 0.0 collective-permute-done.5.other_ref
  28.8 1.5 %collective-permute-start.6 = (bf16[128,256]{1,0:T(8,128)(2,1)S(1)}, bf16[128,256]{1,0:T(8,128)(2,1)S(1)}, u32[]{:S(2)}, u32[]{:S(2)}) collective-permute-start(bf16[128,256]{1,0:T(8,128)(2,1)S(1)} %get-tuple-element.48), channel_id=1, source_target_pairs={{0,8},{4,12},{8,0},{12,4},{1,9},{5,13},{9,1},{13,5},{2,10},{6,14},... | collective-permute-start | bytes 196616 | tf_op jit(solution)/shard_map/ppermute | solution.py:22
  30.3 1.1 %place_rim.3 = bf16[2,256,512]{2,1,0:T(8,128)(2,1)S(1)} custom-call(s32[4,2,8,128]{3,2,1,0:T(8,128)S(1)} %get-tuple-element.44.corner_ref, bf16[4,4,256,256]{3,2,1,0:T(8,128)(2,1)S(1)} %get-tuple-element.45.grad_ref), custom_call_target="tpu_custom_call" | custom-call | flops 805306368 | bytes 2097152 | tf_op jit(solution)/shard_map/place_rim/pallas_call | solution.py:537
  31.5 0.0 copy-start
  31.5 0.1 collective-permute-start.13
  31.5 0.7 %collective-permute-start.12 = (bf16[2,256,512]{2,1,0:T(8,128)(2,1)S(1)}, bf16[2,256,512]{2,1,0:T(8,128)(2,1)S(1)}, u32[]{:S(2)}, u32[]{:S(2)}) collective-permute-start(bf16[2,256,512]{2,1,0:T(8,128)(2,1)S(1)} %place_rim.2), channel_id=1, source_target_pairs={{0,4},{4,8},{8,12},{12,0},{1,5},{5,9},{9,13},{13,1},{2,6},{6,10},{... | collective-permute-start | bytes 1572872 | tf_op jit(solution)/shard_map/ppermute | solution.py:27
  32.2 0.9 %collective-permute-done.6.rest_0_ = bf16[128,256]{1,0:T(8,128)(2,1)S(1)} collective-permute-done((bf16[128,256]{1,0:T(8,128)(2,1)S(1)}, bf16[128,256]{1,0:T(8,128)(2,1)S(1)}, u32[]{:S(2)}, u32[]{:S(2)}) %collective-permute-start.6) | collective-permute-done | bytes 65568 | tf_op jit(solution)/shard_map/ppermute | solution.py:22
  33.2 2.7 %collective-permute-start.9 = (bf16[128,256]{1,0:T(8,128)(2,1)S(1)}, bf16[128,256]{1,0:T(8,128)(2,1)S(1)}, u32[]{:S(2)}, u32[]{:S(2)}) collective-permute-start(bf16[128,256]{1,0:T(8,128)(2,1)S(1)} %get-tuple-element.50), channel_id=1, source_target_pairs={{0,2},{1,3},{2,0},{3,1},{4,6},{5,7},{6,4},{7,5},{8,10},{9,11},{10,... | collective-permute-start | bytes 196616 | tf_op jit(solution)/shard_map/ppermute | solution.py:22
  35.8 1.4 %collective-permute-start.8 = (bf16[128,256]{1,0:T(8,128)(2,1)S(1)}, bf16[128,256]{1,0:T(8,128)(2,1)S(1)}, u32[]{:S(2)}, u32[]{:S(2)}) collective-permute-start(bf16[128,256]{1,0:T(8,128)(2,1)S(1)} %get-tuple-element.50), channel_id=1, source_target_pairs={{0,3},{1,2},{2,1},{3,0},{4,7},{5,6},{6,5},{7,4},{8,11},{9,10},{10,... | collective-permute-start | bytes 196616 | tf_op jit(solution)/shard_map/ppermute | solution.py:22
  37.2 0.2 collective-permute-start.7
  37.4 0.0 copy-done
  37.4 1.9 %place.1.part_ref = f32[4,256,512]{2,1,0:T(8,128)S(1)} custom-call(s32[4,2,8,128]{3,2,1,0:T(8,128)S(1)} %get-tuple-element.44.corner_ref, bf16[4,4,256,256]{3,2,1,0:T(8,128)(2,1)S(1)} %get-tuple-element.45.grad_ref, f32[4,256,512]{2,1,0:T(8,128)S(1)} %bitcast.6), custom_call_target="tpu_custom_call" | custom-call | flops 1610612736 | bytes 2097152 | tf_op jit(solution)/shard_map/place/pallas_call | solution.py:547
  39.4 0.0 collective-permute-done.9.rest_2_
  39.4 2.6 %collective-permute-done.8.rest_1_ = bf16[128,256]{1,0:T(8,128)(2,1)S(1)} collective-permute-done((bf16[128,256]{1,0:T(8,128)(2,1)S(1)}, bf16[128,256]{1,0:T(8,128)(2,1)S(1)}, u32[]{:S(2)}, u32[]{:S(2)}) %collective-permute-start.8) | collective-permute-done | bytes 65568 | tf_op jit(solution)/shard_map/ppermute | solution.py:22
  42.0 0.1 collective-permute-done.7.rest_0_
  42.2 1.5 %collective-permute-start.10 = (bf16[128,256]{1,0:T(8,128)(2,1)S(1)}, bf16[128,256]{1,0:T(8,128)(2,1)S(1)}, u32[]{:S(2)}, u32[]{:S(2)}) collective-permute-start(bf16[128,256]{1,0:T(8,128)(2,1)S(1)} %full_sum.1.mine_ref), channel_id=1, source_target_pairs={{0,8},{4,12},{8,0},{12,4},{1,9},{5,13},{9,1},{13,5},{2,10},{6,14},... | collective-permute-start | bytes 196616 | tf_op jit(solution)/shard_map/ppermute | solution.py:22
  43.7 3.4 %collective-permute-done.10.rest_0_ = bf16[128,256]{1,0:T(8,128)(2,1)S(1)} collective-permute-done((bf16[128,256]{1,0:T(8,128)(2,1)S(1)}, bf16[128,256]{1,0:T(8,128)(2,1)S(1)}, u32[]{:S(2)}, u32[]{:S(2)}) %collective-permute-start.10) | collective-permute-done | bytes 65568 | tf_op jit(solution)/shard_map/ppermute | solution.py:22
  47.2 0.1 collective-permute-start.11
  47.3 0.0 collective-permute-done.13.rest_1_
  47.3 0.0 collective-permute-done.12.rest_0_
  47.3 1.4 %finish.1 = f32[4,256,512]{2,1,0:T(8,128)} custom-call(f32[4,256,512]{2,1,0:T(8,128)S(1)} %place.1.part_ref, bf16[2,256,512]{2,1,0:T(8,128)(2,1)S(1)} %collective-permute-done.12.rest_0_, bf16[2,256,512]{2,1,0:T(8,128)(2,1)S(1)} %collective-permute-done.13.rest_1_), custom_call_target="tpu_custom_call" | custom-call | tf_op jit(solution)/shard_map/finish/pallas_call | solution.py:559
  48.7 0.0 collective-permute-done.11.other_ref
  48.7 0.9 %update_probe.1 = f32[2,256,256]{2,1,0:T(8,128)} custom-call(f32[2,256,256]{2,1,0:T(8,128)S(1)} %copy-done.4, bf16[256,256]{1,0:T(8,128)(2,1)S(1)} %gather_half.1.mine_ref, bf16[256,256]{1,0:T(8,128)(2,1)S(1)} %collective-permute-done.11.other_ref), custom_call_target="tpu_custom_call" | custom-call | flops 1000000000 | bytes 262144 | tf_op jit(solution)/shard_map/update_probe/pallas_call | solution.py:366
  (4 shorter events, 0.1 us)
Async XLA Ops:
  0.6 3.9 %copy-start.5 = (s32[4,1,2]{0,2,1:T(2,128)S(1)}, s32[4,1,2]{0,2,1:T(2,128)}, u32[]{:S(2)}) copy-start(s32[4,1,2]{0,2,1:T(2,128)} %param.11) | copy-start | bytes 100
  0.6 4.0 %copy-start.3 = (s32[2,1]{0,1:T(1,128)S(1)}, s32[2,1]{0,1:T(1,128)}, u32[]{:S(2)}) copy-start(s32[2,1]{0,1:T(1,128)} %param.12) | copy-start | bytes 28
  0.7 4.0 %copy-start.1 = (f32[2,256,256]{2,1,0:T(8,128)S(1)}, f32[2,256,256]{2,1,0:T(8,128)}, u32[]{:S(2)}) copy-start(f32[2,256,256]{2,1,0:T(8,128)} %intensity_ref.1) | copy-start | bytes 1572868
  0.7 4.0 %copy-start.2 = (f32[256,256]{1,0:T(8,128)S(1)}, f32[256,256]{1,0:T(8,128)}, u32[]{:S(2)}) copy-start(f32[256,256]{1,0:T(8,128)} %phase_ref.1) | copy-start | bytes 786436
  2.1 11.5 %copy-start.4 = (f32[2,256,256]{2,1,0:T(8,128)S(1)}, f32[2,256,256]{2,1,0:T(8,128)}, u32[]{:S(2)}) copy-start(f32[2,256,256]{2,1,0:T(8,128)} %probe_ref.5) | copy-start | bytes 1572868
  2.1 11.5 %collective-permute-start = (bf16[2,256,512]{2,1,0:T(8,128)(2,1)S(1)}, bf16[2,256,512]{2,1,0:T(8,128)(2,1)S(1)}, u32[]{:S(2)}, u32[]{:S(2)}) collective-permute-start(bf16[2,256,512]{2,1,0:T(8,128)(2,1)S(1)} %own_zero.1.own_ref), channel_id=1, source_target_pairs={{0,12},{4,0},{8,4},{12,8},{1,13},{5,1},{9,5},{13,9},{2,14},{6,2},{... | collective-permute-start | bytes 1572872 | tf_op jit(solution)/shard_map/ppermute | solution.py:27
  7.0 12.6 %collective-permute-start.1 = (bf16[2,256,512]{2,1,0:T(8,128)(2,1)S(1)}, bf16[2,256,512]{2,1,0:T(8,128)(2,1)S(1)}, u32[]{:S(2)}, u32[]{:S(2)}) collective-permute-start(bf16[2,256,512]{2,1,0:T(8,128)(2,1)S(1)} %get-tuple-element.34.own_ref), channel_id=1, source_target_pairs={{0,12},{4,0},{8,4},{12,8},{1,13},{5,1},{9,5},{13,9},{2,14},{6,2},{... | collective-permute-start | bytes 1572872 | tf_op jit(solution)/shard_map/ppermute | solution.py:27
  7.9 14.5 %collective-permute-start.2 = (bf16[256,256]{1,0:T(8,128)(2,1)S(1)}, bf16[256,256]{1,0:T(8,128)(2,1)S(1)}, u32[]{:S(2)}, u32[]{:S(2)}) collective-permute-start(bf16[256,256]{1,0:T(8,128)(2,1)S(1)} %get-tuple-element.39), channel_id=1, source_target_pairs={{0,4},{4,0},{8,12},{12,8},{1,5},{5,1},{9,13},{13,9},{2,6},{6,2},{1... | collective-permute-start | bytes 393224 | tf_op jit(solution)/shard_map/ppermute | solution.py:22
  7.9 14.5 %collective-permute-start.3 = (bf16[256,256]{1,0:T(8,128)(2,1)S(1)}, bf16[256,256]{1,0:T(8,128)(2,1)S(1)}, u32[]{:S(2)}, u32[]{:S(2)}) collective-permute-start(bf16[256,256]{1,0:T(8,128)(2,1)S(1)} %get-tuple-element.40), channel_id=1, source_target_pairs={{0,8},{4,12},{8,0},{12,4},{1,9},{5,13},{9,1},{13,5},{2,10},{6,14},... | collective-permute-start | bytes 393224 | tf_op jit(solution)/shard_map/ppermute | solution.py:22
  8.4 14.1 %collective-permute-start.4 = (bf16[256,256]{1,0:T(8,128)(2,1)S(1)}, bf16[256,256]{1,0:T(8,128)(2,1)S(1)}, u32[]{:S(2)}, u32[]{:S(2)}) collective-permute-start(bf16[256,256]{1,0:T(8,128)(2,1)S(1)} %get-tuple-element.41), channel_id=1, source_target_pairs={{0,12},{4,8},{8,4},{12,0},{1,13},{5,9},{9,5},{13,1},{2,14},{6,10},... | collective-permute-start | bytes 393224 | tf_op jit(solution)/shard_map/ppermute | solution.py:22
  26.7 2.0 %collective-permute-start.5 = (bf16[256,256]{1,0:T(8,128)(2,1)S(1)}, bf16[256,256]{1,0:T(8,128)(2,1)S(1)}, u32[]{:S(2)}, u32[]{:S(2)}) collective-permute-start(bf16[256,256]{1,0:T(8,128)(2,1)S(1)} %get-tuple-element.43), channel_id=1, source_target_pairs={{0,4},{4,0},{8,12},{12,8},{1,5},{5,1},{9,13},{13,9},{2,6},{6,2},{1... | collective-permute-start | bytes 393224 | tf_op jit(solution)/shard_map/ppermute | solution.py:22
  28.8 4.3 %collective-permute-start.6 = (bf16[128,256]{1,0:T(8,128)(2,1)S(1)}, bf16[128,256]{1,0:T(8,128)(2,1)S(1)}, u32[]{:S(2)}, u32[]{:S(2)}) collective-permute-start(bf16[128,256]{1,0:T(8,128)(2,1)S(1)} %get-tuple-element.48), channel_id=1, source_target_pairs={{0,8},{4,12},{8,0},{12,4},{1,9},{5,13},{9,1},{13,5},{2,10},{6,14},... | collective-permute-start | bytes 196616 | tf_op jit(solution)/shard_map/ppermute | solution.py:22
  31.5 5.9 %copy-start = (f32[2,2,256,512]{3,2,1,0:T(8,128)S(1)}, f32[2,2,256,512]{3,2,1,0:T(8,128)}, u32[]{:S(2)}) copy-start(f32[2,2,256,512]{3,2,1,0:T(8,128)} %param.7) | copy-start | bytes 6291460
  31.5 15.8 %collective-permute-start.13 = (bf16[2,256,512]{2,1,0:T(8,128)(2,1)S(1)}, bf16[2,256,512]{2,1,0:T(8,128)(2,1)S(1)}, u32[]{:S(2)}, u32[]{:S(2)}) collective-permute-start(bf16[2,256,512]{2,1,0:T(8,128)(2,1)S(1)} %place_rim.3), channel_id=1, source_target_pairs={{0,4},{4,8},{8,12},{12,0},{1,5},{5,9},{9,13},{13,1},{2,6},{6,10},{... | collective-permute-start | bytes 1572872 | tf_op jit(solution)/shard_map/ppermute | solution.py:27
  31.5 15.7 %collective-permute-start.12 = (bf16[2,256,512]{2,1,0:T(8,128)(2,1)S(1)}, bf16[2,256,512]{2,1,0:T(8,128)(2,1)S(1)}, u32[]{:S(2)}, u32[]{:S(2)}) collective-permute-start(bf16[2,256,512]{2,1,0:T(8,128)(2,1)S(1)} %place_rim.2), channel_id=1, source_target_pairs={{0,4},{4,8},{8,12},{12,0},{1,5},{5,9},{9,13},{13,1},{2,6},{6,10},{... | collective-permute-start | bytes 1572872 | tf_op jit(solution)/shard_map/ppermute | solution.py:27
  33.2 6.2 %collective-permute-start.9 = (bf16[128,256]{1,0:T(8,128)(2,1)S(1)}, bf16[128,256]{1,0:T(8,128)(2,1)S(1)}, u32[]{:S(2)}, u32[]{:S(2)}) collective-permute-start(bf16[128,256]{1,0:T(8,128)(2,1)S(1)} %get-tuple-element.50), channel_id=1, source_target_pairs={{0,2},{1,3},{2,0},{3,1},{4,6},{5,7},{6,4},{7,5},{8,10},{9,11},{10,... | collective-permute-start | bytes 196616 | tf_op jit(solution)/shard_map/ppermute | solution.py:22
  35.8 6.2 %collective-permute-start.8 = (bf16[128,256]{1,0:T(8,128)(2,1)S(1)}, bf16[128,256]{1,0:T(8,128)(2,1)S(1)}, u32[]{:S(2)}, u32[]{:S(2)}) collective-permute-start(bf16[128,256]{1,0:T(8,128)(2,1)S(1)} %get-tuple-element.50), channel_id=1, source_target_pairs={{0,3},{1,2},{2,1},{3,0},{4,7},{5,6},{6,5},{7,4},{8,11},{9,10},{10,... | collective-permute-start | bytes 196616 | tf_op jit(solution)/shard_map/ppermute | solution.py:22
  37.2 5.0 %collective-permute-start.7 = (bf16[128,256]{1,0:T(8,128)(2,1)S(1)}, bf16[128,256]{1,0:T(8,128)(2,1)S(1)}, u32[]{:S(2)}, u32[]{:S(2)}) collective-permute-start(bf16[128,256]{1,0:T(8,128)(2,1)S(1)} %get-tuple-element.50), channel_id=1, source_target_pairs={{0,1},{1,0},{2,3},{3,2},{4,5},{5,4},{6,7},{7,6},{8,9},{9,8},{10,11... | collective-permute-start | bytes 196616 | tf_op jit(solution)/shard_map/ppermute | solution.py:22
  42.2 5.0 %collective-permute-start.10 = (bf16[128,256]{1,0:T(8,128)(2,1)S(1)}, bf16[128,256]{1,0:T(8,128)(2,1)S(1)}, u32[]{:S(2)}, u32[]{:S(2)}) collective-permute-start(bf16[128,256]{1,0:T(8,128)(2,1)S(1)} %full_sum.1.mine_ref), channel_id=1, source_target_pairs={{0,8},{4,12},{8,0},{12,4},{1,9},{5,13},{9,1},{13,5},{2,10},{6,14},... | collective-permute-start | bytes 196616 | tf_op jit(solution)/shard_map/ppermute | solution.py:22
  47.2 1.5 %collective-permute-start.11 = (bf16[256,256]{1,0:T(8,128)(2,1)S(1)}, bf16[256,256]{1,0:T(8,128)(2,1)S(1)}, u32[]{:S(2)}, u32[]{:S(2)}) collective-permute-start(bf16[256,256]{1,0:T(8,128)(2,1)S(1)} %gather_half.1.mine_ref), channel_id=1, source_target_pairs={{0,4},{4,0},{8,12},{12,8},{1,5},{5,1},{9,13},{13,9},{2,6},{6,2},{1... | collective-permute-start | bytes 393224 | tf_op jit(solution)/shard_map/ppermute | solution.py:22

commit v3 on v2

--- a/solution.py
+++ b/solution.py
@@ -11,7 +11,7 @@
 
 step_object = 0.05
 step_probe = 0.5
-SMALL_FLOPS = 1000000000
+SMALL_FLOPS = 1500000000
 LATE_FROM = 99
 SMALL_VMEM = 8 * 1024 * 1024
 LARGE_VMEM = 24 * 1024 * 1024
@@ -295,18 +295,17 @@
     return pltpu.with_memory_space_constraint(array, pltpu.HBM)
 
 
-def finish_kernel(part_ref, *rest):
-    rim_refs, (out_hbm, sums_ref, sems) = rest[:-3], rest[-3:]
-    each, rim_rows, _ = rim_refs[0].shape
-    parts = [(c, rows) for c in range(part_ref.shape[0]) for rows in chunks(part_ref.shape[1], 128)]
+def finish_kernel(part_ref, rim_ref, *rest, first_plane):
+    out_hbm, sums_ref, sems = rest[-3:]
+    parts = [(c, rows) for c in range(rim_ref.shape[0]) for rows in chunks(part_ref.shape[1], 128)]
     copies = []
     step = jnp.where(lax.axis_index("row") == 0, 0.0, step_object)
     for i, (c, rows) in enumerate(parts):
-        value = part_ref[c, rows]
-        if rows.start < rim_rows:
-            value -= step * rim_refs[c // each][c % each, rows].astype(jnp.float32)
+        value = part_ref[first_plane + c, rows]
+        if rows.start < rim_ref.shape[1]:
+            value -= step * rim_ref[c, rows].astype(jnp.float32)
         sums_ref[c, rows] = value
-        copies.append(pltpu.make_async_copy(sums_ref.at[c, rows], out_hbm.at[c, rows], sems.at[i]))
+        copies.append(pltpu.make_async_copy(sums_ref.at[c, rows], out_hbm.at[first_plane + c, rows], sems.at[i]))
         copies[-1].start()
     for copy in copies:
         copy.wait()
@@ -375,7 +374,7 @@
     )(*arrays)
 
 
-def probe_sum(keep, send, rim_grads, part):
+def probe_sum(keep, send, rim_grads, part, finish):
     n = keep.shape[0]
     row_count, col_count = lax.axis_size("row"), lax.axis_size("col")
     chips = row_count // 2
@@ -394,9 +393,14 @@
     others, part = lax.optimization_barrier((others, part))
     (total,) = small_call(full_sum_kernel, [total, *others], [narrow], "full_sum")
     others = [permute_pairs(total, "row", lambda i: i ^ (2 * s)) for s in range(1, chips)]
+    others, updated = lax.optimization_barrier((others, finish(0, part, rim_grads[0], None)))
     half = jax.ShapeDtypeStruct((n, n), jnp.bfloat16)
     (mine,) = small_call(gather_kernel, [total, *others], [half], "gather_half")
-    return mine, permute_pairs(mine, "row", lambda i: i ^ 1), rim_grads, part
+    other = permute_pairs(mine, "row", lambda i: i ^ 1)
+    for piece in range(1, len(rim_grads)):
+        updated = finish(piece, part, rim_grads[piece], updated)
+    other, updated = lax.optimization_barrier((other, updated))
+    return mine, other, updated
 
 
 def per_device(object_slab, probe_field, prop_phase, intensities, corners, slot_source):
@@ -555,20 +559,24 @@
         steps=1,
     )(near(vectors), near(grads), slab)
 
-    mine, other, rim_grads, part = probe_sum(keep, send, rim_grads, part)
-    updated_slab = pl.pallas_call(
-        finish_kernel,
-        in_specs=[vmem] * (1 + slice_count),
-        out_specs=hbm,
-        out_shape=pltpu.HBM((planes, height, width), jnp.float32),
-        scratch_shapes=[
-            pltpu.VMEM((planes, height, width), jnp.float32),
-            pltpu.SemaphoreType.DMA((planes * len(chunks(height, 128)),)),
-        ],
-        compiler_params=pltpu.CompilerParams(vmem_limit_bytes=SMALL_VMEM),
-        name="finish",
-    )(near(part), *[near(rim) for rim in rim_grads]).reshape(object_slab.shape)
-    other, updated_slab = lax.optimization_barrier((other, updated_slab))
+    def finish(piece, part, rim, updated):
+        given = [near(part), near(rim)] + ([] if updated is None else [updated])
+        return pl.pallas_call(
+            functools.partial(finish_kernel, first_plane=piece * pair_count),
+            in_specs=[vmem, vmem] + [hbm] * (len(given) - 2),
+            out_specs=hbm,
+            out_shape=pltpu.HBM((planes, height, width), jnp.float32),
+            scratch_shapes=[
+                pltpu.VMEM(tile, jnp.float32),
+                pltpu.SemaphoreType.DMA((pair_count * len(chunks(height, 128)),)),
+            ],
+            input_output_aliases={} if updated is None else {2: 0},
+            compiler_params=pltpu.CompilerParams(vmem_limit_bytes=SMALL_VMEM),
+            name="finish",
+        )(*given)
+
+    mine, other, updated_slab = probe_sum(keep, send, rim_grads, part, finish)
+    updated_slab = updated_slab.reshape(object_slab.shape)
     (updated_probe,) = small_call(
         functools.partial(probe_kernel, scale=step_probe / (row_count * col_count * slot_count)),
         [probe_field, mine, other],

time: 49.8 us -> 49.1 us (0.986)
  waiting for transfers between devices: 13.1 us -> 11 us
  starting transfers between devices: 14.2 us -> 15.1 us
  Pallas kernels: 21.3 us -> 21.9 us
    ppermute x10, waiting for transfers between devices: 7.25 us -> 5.08 us  [permute_pairs(): lax.ppermute(block, axis, [(i, partner(i)) for i in range(lax.axis_size(a...]
    ppermute x10, starting transfers between devices: 10.1 us -> 10.8 us  [permute_pairs(): lax.ppermute(block, axis, [(i, partner(i)) for i in range(lax.axis_size(a...]
    pallas_call x1 -> x2, Pallas kernels: 1.41 us -> 2.06 us  [finish(): pl.pallas_call(functools.partial(finish_kernel, first_plane=piece * pair_...]
  transfers between devices with their start and end apart: 14 -> 14, of which waited for: 7 -> 8; matrix products, arithmetic and copies ran while one was open for 0% -> 0% of each run, Pallas kernels for 30% -> 31%
where the time goes in v3:
time: 49.1 us; the launch traced here: 49 us
  Pallas kernels  21.9 us (45%)
  starting transfers between devices  15.1 us (31%)
  waiting for transfers between devices  11 us (22%)
  between operations  0.82 us (2%)
    ppermute x10, starting transfers between devices, permute_pairs(): lax.ppermute(block, axis, [(i, partner(i)) for i in range(lax.axis_size(a...  10.8 us
    ppermute x4, waiting for transfers between devices, around(): lax.ppermute(block, axis, [(i, (i + distance) % size) for i in range(size)])  5.9 us
    ppermute x10, waiting for transfers between devices, permute_pairs(): lax.ppermute(block, axis, [(i, partner(i)) for i in range(lax.axis_size(a...  5.08 us
    ppermute x4, starting transfers between devices, around(): lax.ppermute(block, axis, [(i, (i + distance) % size) for i in range(size)])  4.29 us
    pallas_call x1, Pallas kernels, per_device(): call(functools.partial(third_kernel, steps=row_count // count), [whole(pl...  4.23 us
    pallas_call x1, Pallas kernels, per_device(): call(first_kernel, [spot_block, own_block, rim_block, whole(plane), whole...  3.97 us
    pallas_call x1, Pallas kernels, per_device(): call(second_kernel, [spot_block, own_block, rim_block, wide_block, tables...  2.72 us
    pallas_call x1, Pallas kernels, per_device(): pl.pallas_call(prepare_kernel, in_specs=[smem, smem, vmem, hbm, hbm, vmem...  2.37 us
  transfers between devices with their start and end apart: 14, of which 8 were waited for; matrix products, arithmetic and copies ran while one was open for 0% of the time, Pallas kernels for 31%

profile of v3, /device:TPU:0, one launch (start us, length us, event | category | flops | bytes accessed | tf_op | source)
XLA Modules:
  0.0 49.0 jit_solution(5690121372598183697)
XLA Ops:
  0.6 0.0 copy-start.5
  0.6 0.0 copy-start.3
  0.7 0.0 copy-start.1
  0.7 0.0 copy-start.2
  0.7 1.4 %own_zero.1.own_ref = bf16[2,256,512]{2,1,0:T(8,128)(2,1)S(1)} custom-call(f32[4,256,512]{2,1,0:T(8,128)} %bitcast.4), custom_call_target="tpu_custom_call" | custom-call | tf_op jit(solution)/shard_map/own_zero/pallas_call | solution.py:430
  2.1 0.0 copy-start.4
  2.1 2.4 %collective-permute-start = (bf16[2,256,512]{2,1,0:T(8,128)(2,1)S(1)}, bf16[2,256,512]{2,1,0:T(8,128)(2,1)S(1)}, u32[]{:S(2)}, u32[]{:S(2)}) collective-permute-start(bf16[2,256,512]{2,1,0:T(8,128)(2,1)S(1)} %own_zero.1.own_ref), channel_id=1, source_target_pairs={{0,12},{4,0},{8,4},{12,8},{1,13},{5,1},{9,5},{13,9},{2,14},{6,2},{... | collective-permute-start | bytes 1572872 | tf_op jit(solution)/shard_map/ppermute | solution.py:27
  4.5 0.0 copy-done.5
  4.5 0.1 copy.10.corner_ref
  4.6 0.0 copy-done.3
  4.6 0.0 copy-done.1
  4.6 0.0 copy-done.2
  4.6 2.4 %prepare.1 = (bf16[2,256,512]{2,1,0:T(8,128)(2,1)S(1)}, bf16[512,512]{1,0:T(8,128)(2,1)S(1)}, f32[2,256,256]{2,1,0:T(8,128)S(1)}, s32[4,2,8,128]{3,2,1,0:T(8,128...) custom-call(s32[4,2]{1,0:T(4,128)S(1)} %copy.10.corner_ref, ...), custom_call_target="tpu_custom_call" | custom-call | tf_op jit(solution)/shard_map/prepare/pallas_call | solution.py:443
  7.0 0.9 %collective-permute-start.1 = (bf16[2,256,512]{2,1,0:T(8,128)(2,1)S(1)}, bf16[2,256,512]{2,1,0:T(8,128)(2,1)S(1)}, u32[]{:S(2)}, u32[]{:S(2)}) collective-permute-start(bf16[2,256,512]{2,1,0:T(8,128)(2,1)S(1)} %get-tuple-element.36.own_ref), channel_id=1, source_target_pairs={{0,12},{4,0},{8,4},{12,8},{1,13},{5,1},{9,5},{13,9},{2,14},{6,2},{... | collective-permute-start | bytes 1572872 | tf_op jit(solution)/shard_map/ppermute | solution.py:27
  7.9 0.0 collective-permute-start.2
  7.9 0.5 collective-permute-start.3
  8.4 1.4 %collective-permute-start.4 = (bf16[256,256]{1,0:T(8,128)(2,1)S(1)}, bf16[256,256]{1,0:T(8,128)(2,1)S(1)}, u32[]{:S(2)}, u32[]{:S(2)}) collective-permute-start(bf16[256,256]{1,0:T(8,128)(2,1)S(1)} %get-tuple-element.43), channel_id=1, source_target_pairs={{0,12},{4,8},{8,4},{12,0},{1,13},{5,9},{9,5},{13,1},{2,14},{6,10},... | collective-permute-start | bytes 393224 | tf_op jit(solution)/shard_map/ppermute | solution.py:22
  9.8 3.8 %collective-permute-done.rim_ref = bf16[2,256,512]{2,1,0:T(8,128)(2,1)S(1)} collective-permute-done((bf16[2,256,512]{2,1,0:T(8,128)(2,1)S(1)}, bf16[2,256,512]{2,1,0:T(8,128)(2,1)S(1)}, u32[]{:S(2)}, u32[]{:S(2)}) %collective-permute-start) | collective-permute-done | bytes 524320 | tf_op jit(solution)/shard_map/ppermute | solution.py:27
  13.6 0.0 copy-done.4
  13.6 4.0 %moved.1 = (bf16[4,2,256,256]{3,2,1,0:T(8,128)(2,1)S(1)}, f32[4,256,512]{2,1,0:T(8,128)S(1)}) custom-call(s32[8,128]{1,0:T(8,128)S(1)} %get-tuple-element.34.spot_ref, bf16[2,256,512]{2,1,0:T(8,128)(2,1)S(1)} %own_zero.1.own_ref, bf16[2,256,512]{2,1,0:T(8,128)(2,1)S(1)} %collective-permute-done.rim_ref, f32[2,256,256]{2,1,0:T(8,128)S(1)} %copy-done.4, ...), custom_call_target="tpu_custom_call" | custom-call | flops 3758096384 | bytes 2097152 | tf_op jit(solution)/shard_map/moved/pallas_call | solution.py:501
  17.6 2.1 %collective-permute-done.1.rim_ref = bf16[2,256,512]{2,1,0:T(8,128)(2,1)S(1)} collective-permute-done((bf16[2,256,512]{2,1,0:T(8,128)(2,1)S(1)}, bf16[2,256,512]{2,1,0:T(8,128)(2,1)S(1)}, u32[]{:S(2)}, u32[]{:S(2)}) %collective-permute-start.1) | collective-permute-done | bytes 524320 | tf_op jit(solution)/shard_map/ppermute | solution.py:27
  19.7 2.7 %far.1 = (bf16[4,2,256,256]{3,2,1,0:T(8,128)(2,1)S(1)}, f32[4,256,512]{2,1,0:T(8,128)S(1)}) custom-call(s32[8,128]{1,0:T(8,128)S(1)} %get-tuple-element.34.spot_ref, bf16[2,256,512]{2,1,0:T(8,128)(2,1)S(1)} %get-tuple-element.36.own_ref, bf16[2,256,512]{2,1,0:T(8,128)(2,1)S(1)} %collective-permute-done.1.rim_ref, ...), custom_call_target="tpu_custom_call" | custom-call | flops 2684354560 | bytes 2097152 | tf_op jit(solution)/shard_map/far/pallas_call | solution.py:513
  22.4 0.0 collective-permute-done.2.rest_1_
  22.4 0.0 collective-permute-done.3.rest_2_
  22.4 0.1 collective-permute-done.4.rest_3_
  22.5 4.2 %gradients.1 = (bf16[4,4,256,256]{3,2,1,0:T(8,128)(2,1)S(1)}, f32[256,256]{1,0:T(8,128)S(1)}, bf16[256,256]{1,0:T(8,128)(2,1)S(1)}) custom-call(f32[2,256,256]{2,1,0:T(8,128)S(1)} %copy-done.4, f32[2,256,256]{2,1,0:T(8,128)S(1)} %get-tuple-element.32.kernel_ref, bf16[512,512]{1,0:T(8,128)(2,1)S(1)} %get-tuple-element.33.table_ref, ...), custom_call_target="tpu_custom_call" | custom-call | flops 3221225472 | bytes 2097152 | tf_op jit(solution)/shard_map/gradients/pallas_call | solution.py:523
  26.7 0.9 %collective-permute-start.5 = (bf16[256,256]{1,0:T(8,128)(2,1)S(1)}, bf16[256,256]{1,0:T(8,128)(2,1)S(1)}, u32[]{:S(2)}, u32[]{:S(2)}) collective-permute-start(bf16[256,256]{1,0:T(8,128)(2,1)S(1)} %get-tuple-element.45), channel_id=1, source_target_pairs={{0,4},{4,0},{8,12},{12,8},{1,5},{5,1},{9,13},{13,9},{2,6},{6,2},{1... | collective-permute-start | bytes 393224 | tf_op jit(solution)/shard_map/ppermute | solution.py:22
  27.6 1.1 %place_rim.2 = bf16[2,256,512]{2,1,0:T(8,128)(2,1)S(1)} custom-call(s32[4,2,8,128]{3,2,1,0:T(8,128)S(1)} %get-tuple-element.46.corner_ref, bf16[4,4,256,256]{3,2,1,0:T(8,128)(2,1)S(1)} %get-tuple-element.47.grad_ref), custom_call_target="tpu_custom_call" | custom-call | flops 805306368 | bytes 2097152 | tf_op jit(solution)/shard_map/place_rim/pallas_call | solution.py:541
  28.8 0.0 collective-permute-done.5.other_ref
  28.8 1.5 %collective-permute-start.6 = (bf16[128,256]{1,0:T(8,128)(2,1)S(1)}, bf16[128,256]{1,0:T(8,128)(2,1)S(1)}, u32[]{:S(2)}, u32[]{:S(2)}) collective-permute-start(bf16[128,256]{1,0:T(8,128)(2,1)S(1)} %get-tuple-element.50), channel_id=1, source_target_pairs={{0,8},{4,12},{8,0},{12,4},{1,9},{5,13},{9,1},{13,5},{2,10},{6,14},... | collective-permute-start | bytes 196616 | tf_op jit(solution)/shard_map/ppermute | solution.py:22
  30.3 0.0 collective-permute-start.11
  30.3 1.1 %place_rim.3 = bf16[2,256,512]{2,1,0:T(8,128)(2,1)S(1)} custom-call(s32[4,2,8,128]{3,2,1,0:T(8,128)S(1)} %get-tuple-element.46.corner_ref, bf16[4,4,256,256]{3,2,1,0:T(8,128)(2,1)S(1)} %get-tuple-element.47.grad_ref), custom_call_target="tpu_custom_call" | custom-call | flops 805306368 | bytes 2097152 | tf_op jit(solution)/shard_map/place_rim/pallas_call | solution.py:541
  31.5 1.0 %collective-permute-start.13 = (bf16[2,256,512]{2,1,0:T(8,128)(2,1)S(1)}, bf16[2,256,512]{2,1,0:T(8,128)(2,1)S(1)}, u32[]{:S(2)}, u32[]{:S(2)}) collective-permute-start(bf16[2,256,512]{2,1,0:T(8,128)(2,1)S(1)} %place_rim.3), channel_id=1, source_target_pairs={{0,4},{4,8},{8,12},{12,0},{1,5},{5,9},{9,13},{13,1},{2,6},{6,10},{... | collective-permute-start | bytes 1572872 | tf_op jit(solution)/shard_map/ppermute | solution.py:27
  32.4 0.7 %collective-permute-done.6.rest_0_ = bf16[128,256]{1,0:T(8,128)(2,1)S(1)} collective-permute-done((bf16[128,256]{1,0:T(8,128)(2,1)S(1)}, bf16[128,256]{1,0:T(8,128)(2,1)S(1)}, u32[]{:S(2)}, u32[]{:S(2)}) %collective-permute-start.6) | collective-permute-done | bytes 65568 | tf_op jit(solution)/shard_map/ppermute | solution.py:22
  33.2 0.0 copy-start
  33.2 2.7 %collective-permute-start.9 = (bf16[128,256]{1,0:T(8,128)(2,1)S(1)}, bf16[128,256]{1,0:T(8,128)(2,1)S(1)}, u32[]{:S(2)}, u32[]{:S(2)}) collective-permute-start(bf16[128,256]{1,0:T(8,128)(2,1)S(1)} %get-tuple-element.52), channel_id=1, source_target_pairs={{0,2},{1,3},{2,0},{3,1},{4,6},{5,7},{6,4},{7,5},{8,10},{9,11},{10,... | collective-permute-start | bytes 196616 | tf_op jit(solution)/shard_map/ppermute | solution.py:22
  35.8 1.4 %collective-permute-start.8 = (bf16[128,256]{1,0:T(8,128)(2,1)S(1)}, bf16[128,256]{1,0:T(8,128)(2,1)S(1)}, u32[]{:S(2)}, u32[]{:S(2)}) collective-permute-start(bf16[128,256]{1,0:T(8,128)(2,1)S(1)} %get-tuple-element.52), channel_id=1, source_target_pairs={{0,3},{1,2},{2,1},{3,0},{4,7},{5,6},{6,5},{7,4},{8,11},{9,10},{10,... | collective-permute-start | bytes 196616 | tf_op jit(solution)/shard_map/ppermute | solution.py:22
  37.2 0.2 collective-permute-start.7
  37.4 0.0 copy-done
  37.4 1.9 %place.1.part_ref = f32[4,256,512]{2,1,0:T(8,128)S(1)} custom-call(s32[4,2,8,128]{3,2,1,0:T(8,128)S(1)} %get-tuple-element.46.corner_ref, bf16[4,4,256,256]{3,2,1,0:T(8,128)(2,1)S(1)} %get-tuple-element.47.grad_ref, f32[4,256,512]{2,1,0:T(8,128)S(1)} %bitcast.6), custom_call_target="tpu_custom_call" | custom-call | flops 1610612736 | bytes 2097152 | tf_op jit(solution)/shard_map/place/pallas_call | solution.py:551
  39.4 0.0 collective-permute-done.9.rest_2_
  39.4 2.7 %collective-permute-done.8.rest_1_ = bf16[128,256]{1,0:T(8,128)(2,1)S(1)} collective-permute-done((bf16[128,256]{1,0:T(8,128)(2,1)S(1)}, bf16[128,256]{1,0:T(8,128)(2,1)S(1)}, u32[]{:S(2)}, u32[]{:S(2)}) %collective-permute-start.8) | collective-permute-done | bytes 65568 | tf_op jit(solution)/shard_map/ppermute | solution.py:22
  42.0 0.1 collective-permute-done.7.rest_0_
  42.2 2.2 %collective-permute-start.10 = (bf16[128,256]{1,0:T(8,128)(2,1)S(1)}, bf16[128,256]{1,0:T(8,128)(2,1)S(1)}, u32[]{:S(2)}, u32[]{:S(2)}) collective-permute-start(bf16[128,256]{1,0:T(8,128)(2,1)S(1)} %full_sum.1.mine_ref), channel_id=1, source_target_pairs={{0,8},{4,12},{8,0},{12,4},{1,9},{5,13},{9,1},{13,5},{2,10},{6,14},... | collective-permute-start | bytes 196616 | tf_op jit(solution)/shard_map/ppermute | solution.py:22
  44.4 0.0 collective-permute-done.11.rim_ref
  44.4 1.0 %finish.2.rest_0_ = f32[4,256,512]{2,1,0:T(8,128)} custom-call(f32[4,256,512]{2,1,0:T(8,128)S(1)} %place.1.part_ref, bf16[2,256,512]{2,1,0:T(8,128)(2,1)S(1)} %collective-permute-done.11.rim_ref), custom_call_target="tpu_custom_call" | custom-call | tf_op jit(solution)/shard_map/finish/pallas_call | solution.py:564
  45.4 1.2 %collective-permute-done.10.rest_0_ = bf16[128,256]{1,0:T(8,128)(2,1)S(1)} collective-permute-done((bf16[128,256]{1,0:T(8,128)(2,1)S(1)}, bf16[128,256]{1,0:T(8,128)(2,1)S(1)}, u32[]{:S(2)}, u32[]{:S(2)}) %collective-permute-start.10) | collective-permute-done | bytes 65568 | tf_op jit(solution)/shard_map/ppermute | solution.py:22
  46.7 0.1 collective-permute-start.12
  46.8 0.0 collective-permute-done.13.rim_ref
  46.8 1.0 %finish.3 = f32[4,256,512]{2,1,0:T(8,128)} custom-call(f32[4,256,512]{2,1,0:T(8,128)S(1)} %place.1.part_ref, bf16[2,256,512]{2,1,0:T(8,128)(2,1)S(1)} %collective-permute-done.13.rim_ref, f32[4,256,512]{2,1,0:T(8,128)} %finish.2.rest_0_), custom_call_target="tpu_custom_call", output_to_operand_aliasing={{}: (2, {})} | custom-call | tf_op jit(solution)/shard_map/finish/pallas_call | solution.py:564
  47.8 0.3 collective-permute-done.12.other_ref
  48.1 0.9 %update_probe.1 = f32[2,256,256]{2,1,0:T(8,128)} custom-call(f32[2,256,256]{2,1,0:T(8,128)S(1)} %copy-done.4, bf16[256,256]{1,0:T(8,128)(2,1)S(1)} %gather_half.1.mine_ref, bf16[256,256]{1,0:T(8,128)(2,1)S(1)} %collective-permute-done.12.other_ref), custom_call_target="tpu_custom_call" | custom-call | flops 1500000000 | bytes 262144 | tf_op jit(solution)/shard_map/update_probe/pallas_call | solution.py:365
  (4 shorter events, 0.1 us)
Async XLA Ops:
  0.6 3.9 %copy-start.5 = (s32[4,1,2]{0,2,1:T(2,128)S(1)}, s32[4,1,2]{0,2,1:T(2,128)}, u32[]{:S(2)}) copy-start(s32[4,1,2]{0,2,1:T(2,128)} %param.11) | copy-start | bytes 100
  0.6 4.0 %copy-start.3 = (s32[2,1]{0,1:T(1,128)S(1)}, s32[2,1]{0,1:T(1,128)}, u32[]{:S(2)}) copy-start(s32[2,1]{0,1:T(1,128)} %param.12) | copy-start | bytes 28
  0.7 4.0 %copy-start.1 = (f32[2,256,256]{2,1,0:T(8,128)S(1)}, f32[2,256,256]{2,1,0:T(8,128)}, u32[]{:S(2)}) copy-start(f32[2,256,256]{2,1,0:T(8,128)} %intensity_ref.1) | copy-start | bytes 1572868
  0.7 4.0 %copy-start.2 = (f32[256,256]{1,0:T(8,128)S(1)}, f32[256,256]{1,0:T(8,128)}, u32[]{:S(2)}) copy-start(f32[256,256]{1,0:T(8,128)} %phase_ref.1) | copy-start | bytes 786436
  2.1 11.5 %copy-start.4 = (f32[2,256,256]{2,1,0:T(8,128)S(1)}, f32[2,256,256]{2,1,0:T(8,128)}, u32[]{:S(2)}) copy-start(f32[2,256,256]{2,1,0:T(8,128)} %probe_ref.5) | copy-start | bytes 1572868
  2.1 11.5 %collective-permute-start = (bf16[2,256,512]{2,1,0:T(8,128)(2,1)S(1)}, bf16[2,256,512]{2,1,0:T(8,128)(2,1)S(1)}, u32[]{:S(2)}, u32[]{:S(2)}) collective-permute-start(bf16[2,256,512]{2,1,0:T(8,128)(2,1)S(1)} %own_zero.1.own_ref), channel_id=1, source_target_pairs={{0,12},{4,0},{8,4},{12,8},{1,13},{5,1},{9,5},{13,9},{2,14},{6,2},{... | collective-permute-start | bytes 1572872 | tf_op jit(solution)/shard_map/ppermute | solution.py:27
  7.0 12.6 %collective-permute-start.1 = (bf16[2,256,512]{2,1,0:T(8,128)(2,1)S(1)}, bf16[2,256,512]{2,1,0:T(8,128)(2,1)S(1)}, u32[]{:S(2)}, u32[]{:S(2)}) collective-permute-start(bf16[2,256,512]{2,1,0:T(8,128)(2,1)S(1)} %get-tuple-element.36.own_ref), channel_id=1, source_target_pairs={{0,12},{4,0},{8,4},{12,8},{1,13},{5,1},{9,5},{13,9},{2,14},{6,2},{... | collective-permute-start | bytes 1572872 | tf_op jit(solution)/shard_map/ppermute | solution.py:27
  7.9 14.5 %collective-permute-start.2 = (bf16[256,256]{1,0:T(8,128)(2,1)S(1)}, bf16[256,256]{1,0:T(8,128)(2,1)S(1)}, u32[]{:S(2)}, u32[]{:S(2)}) collective-permute-start(bf16[256,256]{1,0:T(8,128)(2,1)S(1)} %get-tuple-element.41), channel_id=1, source_target_pairs={{0,4},{4,0},{8,12},{12,8},{1,5},{5,1},{9,13},{13,9},{2,6},{6,2},{1... | collective-permute-start | bytes 393224 | tf_op jit(solution)/shard_map/ppermute | solution.py:22
  7.9 14.5 %collective-permute-start.3 = (bf16[256,256]{1,0:T(8,128)(2,1)S(1)}, bf16[256,256]{1,0:T(8,128)(2,1)S(1)}, u32[]{:S(2)}, u32[]{:S(2)}) collective-permute-start(bf16[256,256]{1,0:T(8,128)(2,1)S(1)} %get-tuple-element.42), channel_id=1, source_target_pairs={{0,8},{4,12},{8,0},{12,4},{1,9},{5,13},{9,1},{13,5},{2,10},{6,14},... | collective-permute-start | bytes 393224 | tf_op jit(solution)/shard_map/ppermute | solution.py:22
  8.4 14.1 %collective-permute-start.4 = (bf16[256,256]{1,0:T(8,128)(2,1)S(1)}, bf16[256,256]{1,0:T(8,128)(2,1)S(1)}, u32[]{:S(2)}, u32[]{:S(2)}) collective-permute-start(bf16[256,256]{1,0:T(8,128)(2,1)S(1)} %get-tuple-element.43), channel_id=1, source_target_pairs={{0,12},{4,8},{8,4},{12,0},{1,13},{5,9},{9,5},{13,1},{2,14},{6,10},... | collective-permute-start | bytes 393224 | tf_op jit(solution)/shard_map/ppermute | solution.py:22
  26.7 2.0 %collective-permute-start.5 = (bf16[256,256]{1,0:T(8,128)(2,1)S(1)}, bf16[256,256]{1,0:T(8,128)(2,1)S(1)}, u32[]{:S(2)}, u32[]{:S(2)}) collective-permute-start(bf16[256,256]{1,0:T(8,128)(2,1)S(1)} %get-tuple-element.45), channel_id=1, source_target_pairs={{0,4},{4,0},{8,12},{12,8},{1,5},{5,1},{9,13},{13,9},{2,6},{6,2},{1... | collective-permute-start | bytes 393224 | tf_op jit(solution)/shard_map/ppermute | solution.py:22
  28.8 4.3 %collective-permute-start.6 = (bf16[128,256]{1,0:T(8,128)(2,1)S(1)}, bf16[128,256]{1,0:T(8,128)(2,1)S(1)}, u32[]{:S(2)}, u32[]{:S(2)}) collective-permute-start(bf16[128,256]{1,0:T(8,128)(2,1)S(1)} %get-tuple-element.50), channel_id=1, source_target_pairs={{0,8},{4,12},{8,0},{12,4},{1,9},{5,13},{9,1},{13,5},{2,10},{6,14},... | collective-permute-start | bytes 196616 | tf_op jit(solution)/shard_map/ppermute | solution.py:22
  30.3 14.1 %collective-permute-start.11 = (bf16[2,256,512]{2,1,0:T(8,128)(2,1)S(1)}, bf16[2,256,512]{2,1,0:T(8,128)(2,1)S(1)}, u32[]{:S(2)}, u32[]{:S(2)}) collective-permute-start(bf16[2,256,512]{2,1,0:T(8,128)(2,1)S(1)} %place_rim.2), channel_id=1, source_target_pairs={{0,4},{4,8},{8,12},{12,0},{1,5},{5,9},{9,13},{13,1},{2,6},{6,10},{... | collective-permute-start | bytes 1572872 | tf_op jit(solution)/shard_map/ppermute | solution.py:27
  31.5 15.3 %collective-permute-start.13 = (bf16[2,256,512]{2,1,0:T(8,128)(2,1)S(1)}, bf16[2,256,512]{2,1,0:T(8,128)(2,1)S(1)}, u32[]{:S(2)}, u32[]{:S(2)}) collective-permute-start(bf16[2,256,512]{2,1,0:T(8,128)(2,1)S(1)} %place_rim.3), channel_id=1, source_target_pairs={{0,4},{4,8},{8,12},{12,0},{1,5},{5,9},{9,13},{13,1},{2,6},{6,10},{... | collective-permute-start | bytes 1572872 | tf_op jit(solution)/shard_map/ppermute | solution.py:27
  33.2 4.3 %copy-start = (f32[2,2,256,512]{3,2,1,0:T(8,128)S(1)}, f32[2,2,256,512]{3,2,1,0:T(8,128)}, u32[]{:S(2)}) copy-start(f32[2,2,256,512]{3,2,1,0:T(8,128)} %param.7) | copy-start | bytes 6291460
  33.2 6.2 %collective-permute-start.9 = (bf16[128,256]{1,0:T(8,128)(2,1)S(1)}, bf16[128,256]{1,0:T(8,128)(2,1)S(1)}, u32[]{:S(2)}, u32[]{:S(2)}) collective-permute-start(bf16[128,256]{1,0:T(8,128)(2,1)S(1)} %get-tuple-element.52), channel_id=1, source_target_pairs={{0,2},{1,3},{2,0},{3,1},{4,6},{5,7},{6,4},{7,5},{8,10},{9,11},{10,... | collective-permute-start | bytes 196616 | tf_op jit(solution)/shard_map/ppermute | solution.py:22
  35.8 6.2 %collective-permute-start.8 = (bf16[128,256]{1,0:T(8,128)(2,1)S(1)}, bf16[128,256]{1,0:T(8,128)(2,1)S(1)}, u32[]{:S(2)}, u32[]{:S(2)}) collective-permute-start(bf16[128,256]{1,0:T(8,128)(2,1)S(1)} %get-tuple-element.52), channel_id=1, source_target_pairs={{0,3},{1,2},{2,1},{3,0},{4,7},{5,6},{6,5},{7,4},{8,11},{9,10},{10,... | collective-permute-start | bytes 196616 | tf_op jit(solution)/shard_map/ppermute | solution.py:22
  37.2 5.0 %collective-permute-start.7 = (bf16[128,256]{1,0:T(8,128)(2,1)S(1)}, bf16[128,256]{1,0:T(8,128)(2,1)S(1)}, u32[]{:S(2)}, u32[]{:S(2)}) collective-permute-start(bf16[128,256]{1,0:T(8,128)(2,1)S(1)} %get-tuple-element.52), channel_id=1, source_target_pairs={{0,1},{1,0},{2,3},{3,2},{4,5},{5,4},{6,7},{7,6},{8,9},{9,8},{10,11... | collective-permute-start | bytes 196616 | tf_op jit(solution)/shard_map/ppermute | solution.py:22
  42.2 4.5 %collective-permute-start.10 = (bf16[128,256]{1,0:T(8,128)(2,1)S(1)}, bf16[128,256]{1,0:T(8,128)(2,1)S(1)}, u32[]{:S(2)}, u32[]{:S(2)}) collective-permute-start(bf16[128,256]{1,0:T(8,128)(2,1)S(1)} %full_sum.1.mine_ref), channel_id=1, source_target_pairs={{0,8},{4,12},{8,0},{12,4},{1,9},{5,13},{9,1},{13,5},{2,10},{6,14},... | collective-permute-start | bytes 196616 | tf_op jit(solution)/shard_map/ppermute | solution.py:22
  46.7 1.4 %collective-permute-start.12 = (bf16[256,256]{1,0:T(8,128)(2,1)S(1)}, bf16[256,256]{1,0:T(8,128)(2,1)S(1)}, u32[]{:S(2)}, u32[]{:S(2)}) collective-permute-start(bf16[256,256]{1,0:T(8,128)(2,1)S(1)} %gather_half.1.mine_ref), channel_id=1, source_target_pairs={{0,4},{4,0},{8,12},{12,8},{1,5},{5,1},{9,13},{13,9},{2,6},{6,2},{1... | collective-permute-start | bytes 393224 | tf_op jit(solution)/shard_map/ppermute | solution.py:22

commit v4 on v3

--- a/solution.py
+++ b/solution.py
@@ -102,17 +102,19 @@
         rim = jnp.where(ends, 0.0, rim_ref[c].astype(jnp.float32))
         tile_ref[c, height // 8 :] = rim.reshape(-1, 8, width)
     copy.wait()
-    within = lax.broadcasted_iota(jnp.int32, (n // 8, 8, width), 1)
+    window = min(n + 128, width)
+    within = lax.broadcasted_iota(jnp.int32, (n // 8, 8, window), 1)
     for p in range(count):
         corner_y, corner_x = place_ref[base + p, 0], place_ref[base + p, 1]
         group = corner_y // 8
         shift = corner_y - group * 8
+        left = pl.multiple_of(jnp.minimum(corner_x // 128 * 128, width - window), 128)
         rows = []
         for c in range(2):
-            turned = pltpu.roll(tile_ref[c, pl.ds(group, n // 8 + 1)], 8 - shift, 1)
-            rows.append(jnp.where(within < 8 - shift, turned[:-1], turned[1:]).reshape(n, width))
+            turned = pltpu.roll(tile_ref[c, pl.ds(group, n // 8 + 1), :, pl.ds(left, window)], 8 - shift, 1)
+            rows.append(jnp.where(within < 8 - shift, turned[:-1], turned[1:]).reshape(n, window))
         rows = jnp.concatenate(rows, 0).astype(jnp.bfloat16)
-        both = product(rows, one_hot_columns((width, n), corner_x)).astype(jnp.bfloat16)
+        both = product(rows, one_hot_columns((window, n), corner_x - left)).astype(jnp.bfloat16)
         patch_ref[p, 0] = both[:n]
         patch_ref[p, 1] = both[n:]
 
@@ -122,7 +124,7 @@
 
 
 def own_kernel(slab_hbm, own_ref, wide_ref, sems):
-    parts = [(c, rows) for c in range(own_ref.shape[0]) for rows in chunks(own_ref.shape[1], 64)]
+    parts = [(c, rows) for c in range(own_ref.shape[0]) for rows in chunks(own_ref.shape[1], 256)]
     copies = [
         pltpu.make_async_copy(slab_hbm.at[c, rows], wide_ref.at[c, rows], sems.at[i])
         for i, (c, rows) in enumerate(parts)
@@ -355,10 +357,17 @@
         half_ref[pl.ds(pl.multiple_of((chip ^ s) * piece, piece), piece)] = ref[...]
 
 
-def probe_kernel(probe_ref, mine_ref, other_ref, out_ref, *, scale):
+def probe_kernel(probe_ref, mine_ref, other_ref, out_hbm, sums_ref, sems, *, scale):
     core = lax.axis_index("row") % 2
-    out_ref[core] = probe_ref[core] - scale * mine_ref[...].astype(jnp.float32)
-    out_ref[1 - core] = probe_ref[1 - core] - scale * other_ref[...].astype(jnp.float32)
+    copies = []
+    for half, (plane, ref) in enumerate([(core, mine_ref), (1 - core, other_ref)]):
+        for i, rows in enumerate(chunks(ref.shape[0], 128)):
+            sums_ref[plane, rows] = probe_ref[plane, rows] - scale * ref[rows].astype(jnp.float32)
+            sem = sems.at[half, i]
+            copies.append(pltpu.make_async_copy(sums_ref.at[plane, rows], out_hbm.at[plane, rows], sem))
+            copies[-1].start()
+    for copy in copies:
+        copy.wait()
 
 
 def small_call(body, arrays, out_shape, name, scratch=()):
@@ -434,7 +443,7 @@
         out_shape=kept(tile, jnp.bfloat16),
         scratch_shapes=[
             pltpu.VMEM(tile, jnp.float32),
-            pltpu.SemaphoreType.DMA((pair_count * len(chunks(height, 64)),)),
+            pltpu.SemaphoreType.DMA((pair_count * len(chunks(height, 256)),)),
         ],
         compiler_params=pltpu.CompilerParams(vmem_limit_bytes=SMALL_VMEM),
         name="own_zero",
@@ -506,7 +515,7 @@
         28,
         "moved",
         scratch=cutting + work,
-    )(near(spots), near(own_zero), near(rim_zero), probe_field, near(kernel), near(table))
+    )(near(spots), near(own_zero), near(rim_zero), near(probe_field), near(kernel), near(table))
     moved, waiting = lax.optimization_barrier((moved, [messages[s] for s in late]))
     for s, message in zip(late, waiting):
         measured[s] = permute_pairs(message, "row", lambda i: i ^ s)
@@ -533,7 +542,7 @@
         "gradients",
         scratch=[pltpu.VMEM(plane, jnp.float32), pltpu.VMEM((row_count, n, n), jnp.bfloat16)] + work,
     )(
-        probe_field, near(kernel), near(table), near(patch_zero), near(patch_one), near(moved), near(far),
+        near(probe_field), near(kernel), near(table), near(patch_zero), near(patch_one), near(moved), near(far),
         *[near(measured[s]) for s in range(row_count)],
     )
     rim_grads = []
@@ -577,12 +586,18 @@
 
     mine, other, updated_slab = probe_sum(keep, send, rim_grads, part, finish)
     updated_slab = updated_slab.reshape(object_slab.shape)
-    (updated_probe,) = small_call(
+    updated_probe = pl.pallas_call(
         functools.partial(probe_kernel, scale=step_probe / (row_count * col_count * slot_count)),
-        [probe_field, mine, other],
-        [jax.ShapeDtypeStruct(probe_field.shape, jnp.float32)],
-        "update_probe",
-    )
+        in_specs=[vmem] * 3,
+        out_specs=hbm,
+        out_shape=pltpu.HBM(probe_field.shape, jnp.float32),
+        scratch_shapes=[
+            pltpu.VMEM(probe_field.shape, jnp.float32),
+            pltpu.SemaphoreType.DMA((2, len(chunks(n, 128)))),
+        ],
+        compiler_params=pltpu.CompilerParams(vmem_limit_bytes=SMALL_VMEM),
+        name="update_probe",
+    )(near(probe_field), mine, other)
     return (updated_slab, updated_probe)
 
 

time: 49.1 us -> 49.1 us (level)
  waiting for transfers between devices: 11 us -> 11.6 us
  Pallas kernels: 21.9 us -> 21.4 us
    pallas_call x5 -> x4, Pallas kernels: 0.97 us -> 0.11 us  [small_call(): pl.pallas_call(body, in_specs=[pl.BlockSpec(memory_space=pltpu.VMEM)] * l...]
    pallas_call x0 -> x1, Pallas kernels: none -> 0.84 us  [per_device(): pl.pallas_call(functools.partial(probe_kernel, scale=step_probe / (row_co...]
where the time goes in v4:
time: 49.1 us; the launch traced here: 48.9 us
  Pallas kernels  21.4 us (44%)
  starting transfers between devices  14.9 us (30%)
  waiting for transfers between devices  11.6 us (24%)
  between operations  0.98 us (2%)
    ppermute x10, starting transfers between devices, permute_pairs(): lax.ppermute(block, axis, [(i, partner(i)) for i in range(lax.axis_size(a...  10.8 us
    ppermute x4, waiting for transfers between devices, around(): lax.ppermute(block, axis, [(i, (i + distance) % size) for i in range(size)])  6.3 us
    ppermute x10, waiting for transfers between devices, permute_pairs(): lax.ppermute(block, axis, [(i, partner(i)) for i in range(lax.axis_size(a...  5.26 us
    pallas_call x1, Pallas kernels, per_device(): call(functools.partial(third_kernel, steps=row_count // count), [whole(pl...  4.17 us
    ppermute x4, starting transfers between devices, around(): lax.ppermute(block, axis, [(i, (i + distance) % size) for i in range(size)])  4.07 us
    pallas_call x1, Pallas kernels, per_device(): call(first_kernel, [spot_block, own_block, rim_block, whole(plane), whole...  3.75 us
    pallas_call x1, Pallas kernels, per_device(): call(second_kernel, [spot_block, own_block, rim_block, wide_block, tables...  2.57 us
    pallas_call x1, Pallas kernels, per_device(): pl.pallas_call(prepare_kernel, in_specs=[smem, smem, vmem, hbm, hbm, vmem...  2.37 us
  transfers between devices with their start and end apart: 14, of which 8 were waited for; matrix products, arithmetic and copies ran while one was open for 0% of the time, Pallas kernels for 31%

profile of v4, /device:TPU:0, one launch (start us, length us, event | category | flops | bytes accessed | tf_op | source)
XLA Modules:
  0.0 48.9 jit_solution(1764631607982862743)
XLA Ops:
  0.6 0.0 copy-start.5
  0.6 0.0 copy-start.4
  0.7 0.0 copy-start.1
  0.7 0.0 copy-start.3
  0.7 1.3 %own_zero.1.own_ref = bf16[2,256,512]{2,1,0:T(8,128)(2,1)S(1)} custom-call(f32[4,256,512]{2,1,0:T(8,128)} %bitcast.4), custom_call_target="tpu_custom_call" | custom-call | tf_op jit(solution)/shard_map/own_zero/pallas_call | solution.py:439
  2.0 0.0 copy-start.2
  2.0 2.4 %collective-permute-start = (bf16[2,256,512]{2,1,0:T(8,128)(2,1)S(1)}, bf16[2,256,512]{2,1,0:T(8,128)(2,1)S(1)}, u32[]{:S(2)}, u32[]{:S(2)}) collective-permute-start(bf16[2,256,512]{2,1,0:T(8,128)(2,1)S(1)} %own_zero.1.own_ref), channel_id=1, source_target_pairs={{0,12},{4,0},{8,4},{12,8},{1,13},{5,1},{9,5},{13,9},{2,14},{6,2},{... | collective-permute-start | bytes 1572872 | tf_op jit(solution)/shard_map/ppermute | solution.py:27
  4.4 0.0 copy-done.5
  4.4 0.1 copy.10.corner_ref
  4.5 0.0 copy-done.4
  4.5 0.0 copy-done.1
  4.5 0.0 copy-done.3
  4.5 2.4 %prepare.1 = (bf16[2,256,512]{2,1,0:T(8,128)(2,1)S(1)}, bf16[512,512]{1,0:T(8,128)(2,1)S(1)}, f32[2,256,256]{2,1,0:T(8,128)S(1)}, s32[4,2,8,128]{3,2,1,0:T(8,128...) custom-call(s32[4,2]{1,0:T(4,128)S(1)} %copy.10.corner_ref, ...), custom_call_target="tpu_custom_call" | custom-call | tf_op jit(solution)/shard_map/prepare/pallas_call | solution.py:452
  6.9 0.7 %collective-permute-start.1 = (bf16[2,256,512]{2,1,0:T(8,128)(2,1)S(1)}, bf16[2,256,512]{2,1,0:T(8,128)(2,1)S(1)}, u32[]{:S(2)}, u32[]{:S(2)}) collective-permute-start(bf16[2,256,512]{2,1,0:T(8,128)(2,1)S(1)} %get-tuple-element.36.own_ref), channel_id=1, source_target_pairs={{0,12},{4,0},{8,4},{12,8},{1,13},{5,1},{9,5},{13,9},{2,14},{6,2},{... | collective-permute-start | bytes 1572872 | tf_op jit(solution)/shard_map/ppermute | solution.py:27
  7.6 0.0 collective-permute-start.2
  7.6 0.5 collective-permute-start.3
  8.1 1.4 %collective-permute-start.4 = (bf16[256,256]{1,0:T(8,128)(2,1)S(1)}, bf16[256,256]{1,0:T(8,128)(2,1)S(1)}, u32[]{:S(2)}, u32[]{:S(2)}) collective-permute-start(bf16[256,256]{1,0:T(8,128)(2,1)S(1)} %get-tuple-element.43), channel_id=1, source_target_pairs={{0,12},{4,8},{8,4},{12,0},{1,13},{5,9},{9,5},{13,1},{2,14},{6,10},... | collective-permute-start | bytes 393224 | tf_op jit(solution)/shard_map/ppermute | solution.py:22
  9.5 4.1 %collective-permute-done.rim_ref = bf16[2,256,512]{2,1,0:T(8,128)(2,1)S(1)} collective-permute-done((bf16[2,256,512]{2,1,0:T(8,128)(2,1)S(1)}, bf16[2,256,512]{2,1,0:T(8,128)(2,1)S(1)}, u32[]{:S(2)}, u32[]{:S(2)}) %collective-permute-start) | collective-permute-done | bytes 524320 | tf_op jit(solution)/shard_map/ppermute | solution.py:27
  13.7 0.0 copy-done.2
  13.7 3.7 %moved.1 = (bf16[4,2,256,256]{3,2,1,0:T(8,128)(2,1)S(1)}, f32[4,256,512]{2,1,0:T(8,128)S(1)}) custom-call(s32[8,128]{1,0:T(8,128)S(1)} %get-tuple-element.34.spot_ref, bf16[2,256,512]{2,1,0:T(8,128)(2,1)S(1)} %own_zero.1.own_ref, bf16[2,256,512]{2,1,0:T(8,128)(2,1)S(1)} %collective-permute-done.rim_ref, f32[2,256,256]{2,1,0:T(8,128)S(1)} %copy-done.2, ...), custom_call_target="tpu_custom_call" | custom-call | flops 3758096384 | bytes 2097152 | tf_op jit(solution)/shard_map/moved/pallas_call | solution.py:510
  17.4 2.2 %collective-permute-done.1.rim_ref = bf16[2,256,512]{2,1,0:T(8,128)(2,1)S(1)} collective-permute-done((bf16[2,256,512]{2,1,0:T(8,128)(2,1)S(1)}, bf16[2,256,512]{2,1,0:T(8,128)(2,1)S(1)}, u32[]{:S(2)}, u32[]{:S(2)}) %collective-permute-start.1) | collective-permute-done | bytes 524320 | tf_op jit(solution)/shard_map/ppermute | solution.py:27
  19.6 2.6 %far.1 = (bf16[4,2,256,256]{3,2,1,0:T(8,128)(2,1)S(1)}, f32[4,256,512]{2,1,0:T(8,128)S(1)}) custom-call(s32[8,128]{1,0:T(8,128)S(1)} %get-tuple-element.34.spot_ref, bf16[2,256,512]{2,1,0:T(8,128)(2,1)S(1)} %get-tuple-element.36.own_ref, bf16[2,256,512]{2,1,0:T(8,128)(2,1)S(1)} %collective-permute-done.1.rim_ref, ...), custom_call_target="tpu_custom_call" | custom-call | flops 2684354560 | bytes 2097152 | tf_op jit(solution)/shard_map/far/pallas_call | solution.py:522
  22.1 0.0 collective-permute-done.2.rest_1_
  22.2 0.0 collective-permute-done.3.rest_2_
  22.2 0.2 collective-permute-done.4.rest_3_
  22.4 4.2 %gradients.1 = (bf16[4,4,256,256]{3,2,1,0:T(8,128)(2,1)S(1)}, f32[256,256]{1,0:T(8,128)S(1)}, bf16[256,256]{1,0:T(8,128)(2,1)S(1)}) custom-call(f32[2,256,256]{2,1,0:T(8,128)S(1)} %copy-done.2, f32[2,256,256]{2,1,0:T(8,128)S(1)} %get-tuple-element.32.kernel_ref, bf16[512,512]{1,0:T(8,128)(2,1)S(1)} %get-tuple-element.33.table_ref, ...), custom_call_target="tpu_custom_call" | custom-call | flops 3221225472 | bytes 2097152 | tf_op jit(solution)/shard_map/gradients/pallas_call | solution.py:532
  26.5 0.9 %collective-permute-start.5 = (bf16[256,256]{1,0:T(8,128)(2,1)S(1)}, bf16[256,256]{1,0:T(8,128)(2,1)S(1)}, u32[]{:S(2)}, u32[]{:S(2)}) collective-permute-start(bf16[256,256]{1,0:T(8,128)(2,1)S(1)} %get-tuple-element.45), channel_id=1, source_target_pairs={{0,4},{4,0},{8,12},{12,8},{1,5},{5,1},{9,13},{13,9},{2,6},{6,2},{1... | collective-permute-start | bytes 393224 | tf_op jit(solution)/shard_map/ppermute | solution.py:22
  27.5 1.1 %place_rim.2 = bf16[2,256,512]{2,1,0:T(8,128)(2,1)S(1)} custom-call(s32[4,2,8,128]{3,2,1,0:T(8,128)S(1)} %get-tuple-element.46.corner_ref, bf16[4,4,256,256]{3,2,1,0:T(8,128)(2,1)S(1)} %get-tuple-element.47.grad_ref), custom_call_target="tpu_custom_call" | custom-call | flops 805306368 | bytes 2097152 | tf_op jit(solution)/shard_map/place_rim/pallas_call | solution.py:550
  28.6 0.0 collective-permute-done.5.other_ref
  28.7 1.5 %collective-permute-start.6 = (bf16[128,256]{1,0:T(8,128)(2,1)S(1)}, bf16[128,256]{1,0:T(8,128)(2,1)S(1)}, u32[]{:S(2)}, u32[]{:S(2)}) collective-permute-start(bf16[128,256]{1,0:T(8,128)(2,1)S(1)} %get-tuple-element.50), channel_id=1, source_target_pairs={{0,8},{4,12},{8,0},{12,4},{1,9},{5,13},{9,1},{13,5},{2,10},{6,14},... | collective-permute-start | bytes 196616 | tf_op jit(solution)/shard_map/ppermute | solution.py:22
  30.2 0.0 collective-permute-start.11
  30.2 1.1 %place_rim.3 = bf16[2,256,512]{2,1,0:T(8,128)(2,1)S(1)} custom-call(s32[4,2,8,128]{3,2,1,0:T(8,128)S(1)} %get-tuple-element.46.corner_ref, bf16[4,4,256,256]{3,2,1,0:T(8,128)(2,1)S(1)} %get-tuple-element.47.grad_ref), custom_call_target="tpu_custom_call" | custom-call | flops 805306368 | bytes 2097152 | tf_op jit(solution)/shard_map/place_rim/pallas_call | solution.py:550
  31.3 0.9 %collective-permute-start.13 = (bf16[2,256,512]{2,1,0:T(8,128)(2,1)S(1)}, bf16[2,256,512]{2,1,0:T(8,128)(2,1)S(1)}, u32[]{:S(2)}, u32[]{:S(2)}) collective-permute-start(bf16[2,256,512]{2,1,0:T(8,128)(2,1)S(1)} %place_rim.3), channel_id=1, source_target_pairs={{0,4},{4,8},{8,12},{12,0},{1,5},{5,9},{9,13},{13,1},{2,6},{6,10},{... | collective-permute-start | bytes 1572872 | tf_op jit(solution)/shard_map/ppermute | solution.py:27
  32.2 0.8 %collective-permute-done.6.rest_0_ = bf16[128,256]{1,0:T(8,128)(2,1)S(1)} collective-permute-done((bf16[128,256]{1,0:T(8,128)(2,1)S(1)}, bf16[128,256]{1,0:T(8,128)(2,1)S(1)}, u32[]{:S(2)}, u32[]{:S(2)}) %collective-permute-start.6) | collective-permute-done | bytes 65568 | tf_op jit(solution)/shard_map/ppermute | solution.py:22
  33.0 0.0 copy-start
  33.0 2.7 %collective-permute-start.9 = (bf16[128,256]{1,0:T(8,128)(2,1)S(1)}, bf16[128,256]{1,0:T(8,128)(2,1)S(1)}, u32[]{:S(2)}, u32[]{:S(2)}) collective-permute-start(bf16[128,256]{1,0:T(8,128)(2,1)S(1)} %get-tuple-element.52), channel_id=1, source_target_pairs={{0,2},{1,3},{2,0},{3,1},{4,6},{5,7},{6,4},{7,5},{8,10},{9,11},{10,... | collective-permute-start | bytes 196616 | tf_op jit(solution)/shard_map/ppermute | solution.py:22
  35.7 1.3 %collective-permute-start.8 = (bf16[128,256]{1,0:T(8,128)(2,1)S(1)}, bf16[128,256]{1,0:T(8,128)(2,1)S(1)}, u32[]{:S(2)}, u32[]{:S(2)}) collective-permute-start(bf16[128,256]{1,0:T(8,128)(2,1)S(1)} %get-tuple-element.52), channel_id=1, source_target_pairs={{0,3},{1,2},{2,1},{3,0},{4,7},{5,6},{6,5},{7,4},{8,11},{9,10},{10,... | collective-permute-start | bytes 196616 | tf_op jit(solution)/shard_map/ppermute | solution.py:22
  37.0 0.2 collective-permute-start.7
  37.2 0.0 copy-done
  37.3 1.9 %place.1.part_ref = f32[4,256,512]{2,1,0:T(8,128)S(1)} custom-call(s32[4,2,8,128]{3,2,1,0:T(8,128)S(1)} %get-tuple-element.46.corner_ref, bf16[4,4,256,256]{3,2,1,0:T(8,128)(2,1)S(1)} %get-tuple-element.47.grad_ref, f32[4,256,512]{2,1,0:T(8,128)S(1)} %bitcast.6), custom_call_target="tpu_custom_call" | custom-call | flops 1610612736 | bytes 2097152 | tf_op jit(solution)/shard_map/place/pallas_call | solution.py:560
  39.2 0.0 collective-permute-done.9.rest_2_
  39.2 2.6 %collective-permute-done.8.rest_1_ = bf16[128,256]{1,0:T(8,128)(2,1)S(1)} collective-permute-done((bf16[128,256]{1,0:T(8,128)(2,1)S(1)}, bf16[128,256]{1,0:T(8,128)(2,1)S(1)}, u32[]{:S(2)}, u32[]{:S(2)}) %collective-permute-start.8) | collective-permute-done | bytes 65568 | tf_op jit(solution)/shard_map/ppermute | solution.py:22
  41.8 0.1 collective-permute-done.7.rest_0_
  42.0 2.2 %collective-permute-start.10 = (bf16[128,256]{1,0:T(8,128)(2,1)S(1)}, bf16[128,256]{1,0:T(8,128)(2,1)S(1)}, u32[]{:S(2)}, u32[]{:S(2)}) collective-permute-start(bf16[128,256]{1,0:T(8,128)(2,1)S(1)} %full_sum.1.mine_ref), channel_id=1, source_target_pairs={{0,8},{4,12},{8,0},{12,4},{1,9},{5,13},{9,1},{13,5},{2,10},{6,14},... | collective-permute-start | bytes 196616 | tf_op jit(solution)/shard_map/ppermute | solution.py:22
  44.2 0.0 collective-permute-done.11.rim_ref
  44.2 1.0 %finish.2.rest_0_ = f32[4,256,512]{2,1,0:T(8,128)} custom-call(f32[4,256,512]{2,1,0:T(8,128)S(1)} %place.1.part_ref, bf16[2,256,512]{2,1,0:T(8,128)(2,1)S(1)} %collective-permute-done.11.rim_ref), custom_call_target="tpu_custom_call" | custom-call | tf_op jit(solution)/shard_map/finish/pallas_call | solution.py:573
  45.3 1.2 %collective-permute-done.10.rest_0_ = bf16[128,256]{1,0:T(8,128)(2,1)S(1)} collective-permute-done((bf16[128,256]{1,0:T(8,128)(2,1)S(1)}, bf16[128,256]{1,0:T(8,128)(2,1)S(1)}, u32[]{:S(2)}, u32[]{:S(2)}) %collective-permute-start.10) | collective-permute-done | bytes 65568 | tf_op jit(solution)/shard_map/ppermute | solution.py:22
  46.5 0.1 collective-permute-start.12
  46.6 0.0 collective-permute-done.13.rim_ref
  46.6 1.0 %finish.3 = f32[4,256,512]{2,1,0:T(8,128)} custom-call(f32[4,256,512]{2,1,0:T(8,128)S(1)} %place.1.part_ref, bf16[2,256,512]{2,1,0:T(8,128)(2,1)S(1)} %collective-permute-done.13.rim_ref, f32[4,256,512]{2,1,0:T(8,128)} %finish.2.rest_0_), custom_call_target="tpu_custom_call", output_to_operand_aliasing={{}: (2, {})} | custom-call | tf_op jit(solution)/shard_map/finish/pallas_call | solution.py:573
  47.6 0.3 collective-permute-done.12.other_ref
  47.9 0.8 %update_probe.1 = f32[2,256,256]{2,1,0:T(8,128)} custom-call(f32[2,256,256]{2,1,0:T(8,128)S(1)} %copy-done.2, bf16[256,256]{1,0:T(8,128)(2,1)S(1)} %gather_half.1.mine_ref, bf16[256,256]{1,0:T(8,128)(2,1)S(1)} %collective-permute-done.12.other_ref), custom_call_target="tpu_custom_call" | custom-call | tf_op jit(solution)/shard_map/update_probe/pallas_call | solution.py:589
  (4 shorter events, 0.1 us)
Async XLA Ops:
  0.6 3.8 %copy-start.5 = (s32[4,1,2]{0,2,1:T(2,128)S(1)}, s32[4,1,2]{0,2,1:T(2,128)}, u32[]{:S(2)}) copy-start(s32[4,1,2]{0,2,1:T(2,128)} %param.11) | copy-start | bytes 100
  0.6 3.9 %copy-start.4 = (s32[2,1]{0,1:T(1,128)S(1)}, s32[2,1]{0,1:T(1,128)}, u32[]{:S(2)}) copy-start(s32[2,1]{0,1:T(1,128)} %param.12) | copy-start | bytes 28
  0.7 3.9 %copy-start.1 = (f32[2,256,256]{2,1,0:T(8,128)S(1)}, f32[2,256,256]{2,1,0:T(8,128)}, u32[]{:S(2)}) copy-start(f32[2,256,256]{2,1,0:T(8,128)} %intensity_ref.1) | copy-start | bytes 1572868
  0.7 3.9 %copy-start.3 = (f32[256,256]{1,0:T(8,128)S(1)}, f32[256,256]{1,0:T(8,128)}, u32[]{:S(2)}) copy-start(f32[256,256]{1,0:T(8,128)} %phase_ref.1) | copy-start | bytes 786436
  2.0 11.7 %copy-start.2 = (f32[2,256,256]{2,1,0:T(8,128)S(1)}, f32[2,256,256]{2,1,0:T(8,128)}, u32[]{:S(2)}) copy-start(f32[2,256,256]{2,1,0:T(8,128)} %probe_ref.5) | copy-start | bytes 1572868
  2.0 11.6 %collective-permute-start = (bf16[2,256,512]{2,1,0:T(8,128)(2,1)S(1)}, bf16[2,256,512]{2,1,0:T(8,128)(2,1)S(1)}, u32[]{:S(2)}, u32[]{:S(2)}) collective-permute-start(bf16[2,256,512]{2,1,0:T(8,128)(2,1)S(1)} %own_zero.1.own_ref), channel_id=1, source_target_pairs={{0,12},{4,0},{8,4},{12,8},{1,13},{5,1},{9,5},{13,9},{2,14},{6,2},{... | collective-permute-start | bytes 1572872 | tf_op jit(solution)/shard_map/ppermute | solution.py:27
  6.9 12.6 %collective-permute-start.1 = (bf16[2,256,512]{2,1,0:T(8,128)(2,1)S(1)}, bf16[2,256,512]{2,1,0:T(8,128)(2,1)S(1)}, u32[]{:S(2)}, u32[]{:S(2)}) collective-permute-start(bf16[2,256,512]{2,1,0:T(8,128)(2,1)S(1)} %get-tuple-element.36.own_ref), channel_id=1, source_target_pairs={{0,12},{4,0},{8,4},{12,8},{1,13},{5,1},{9,5},{13,9},{2,14},{6,2},{... | collective-permute-start | bytes 1572872 | tf_op jit(solution)/shard_map/ppermute | solution.py:27
  7.6 14.5 %collective-permute-start.2 = (bf16[256,256]{1,0:T(8,128)(2,1)S(1)}, bf16[256,256]{1,0:T(8,128)(2,1)S(1)}, u32[]{:S(2)}, u32[]{:S(2)}) collective-permute-start(bf16[256,256]{1,0:T(8,128)(2,1)S(1)} %get-tuple-element.41), channel_id=1, source_target_pairs={{0,4},{4,0},{8,12},{12,8},{1,5},{5,1},{9,13},{13,9},{2,6},{6,2},{1... | collective-permute-start | bytes 393224 | tf_op jit(solution)/shard_map/ppermute | solution.py:22
  7.6 14.5 %collective-permute-start.3 = (bf16[256,256]{1,0:T(8,128)(2,1)S(1)}, bf16[256,256]{1,0:T(8,128)(2,1)S(1)}, u32[]{:S(2)}, u32[]{:S(2)}) collective-permute-start(bf16[256,256]{1,0:T(8,128)(2,1)S(1)} %get-tuple-element.42), channel_id=1, source_target_pairs={{0,8},{4,12},{8,0},{12,4},{1,9},{5,13},{9,1},{13,5},{2,10},{6,14},... | collective-permute-start | bytes 393224 | tf_op jit(solution)/shard_map/ppermute | solution.py:22
  8.1 14.3 %collective-permute-start.4 = (bf16[256,256]{1,0:T(8,128)(2,1)S(1)}, bf16[256,256]{1,0:T(8,128)(2,1)S(1)}, u32[]{:S(2)}, u32[]{:S(2)}) collective-permute-start(bf16[256,256]{1,0:T(8,128)(2,1)S(1)} %get-tuple-element.43), channel_id=1, source_target_pairs={{0,12},{4,8},{8,4},{12,0},{1,13},{5,9},{9,5},{13,1},{2,14},{6,10},... | collective-permute-start | bytes 393224 | tf_op jit(solution)/shard_map/ppermute | solution.py:22
  26.5 2.0 %collective-permute-start.5 = (bf16[256,256]{1,0:T(8,128)(2,1)S(1)}, bf16[256,256]{1,0:T(8,128)(2,1)S(1)}, u32[]{:S(2)}, u32[]{:S(2)}) collective-permute-start(bf16[256,256]{1,0:T(8,128)(2,1)S(1)} %get-tuple-element.45), channel_id=1, source_target_pairs={{0,4},{4,0},{8,12},{12,8},{1,5},{5,1},{9,13},{13,9},{2,6},{6,2},{1... | collective-permute-start | bytes 393224 | tf_op jit(solution)/shard_map/ppermute | solution.py:22
  28.7 4.3 %collective-permute-start.6 = (bf16[128,256]{1,0:T(8,128)(2,1)S(1)}, bf16[128,256]{1,0:T(8,128)(2,1)S(1)}, u32[]{:S(2)}, u32[]{:S(2)}) collective-permute-start(bf16[128,256]{1,0:T(8,128)(2,1)S(1)} %get-tuple-element.50), channel_id=1, source_target_pairs={{0,8},{4,12},{8,0},{12,4},{1,9},{5,13},{9,1},{13,5},{2,10},{6,14},... | collective-permute-start | bytes 196616 | tf_op jit(solution)/shard_map/ppermute | solution.py:22
  30.2 14.1 %collective-permute-start.11 = (bf16[2,256,512]{2,1,0:T(8,128)(2,1)S(1)}, bf16[2,256,512]{2,1,0:T(8,128)(2,1)S(1)}, u32[]{:S(2)}, u32[]{:S(2)}) collective-permute-start(bf16[2,256,512]{2,1,0:T(8,128)(2,1)S(1)} %place_rim.2), channel_id=1, source_target_pairs={{0,4},{4,8},{8,12},{12,0},{1,5},{5,9},{9,13},{13,1},{2,6},{6,10},{... | collective-permute-start | bytes 1572872 | tf_op jit(solution)/shard_map/ppermute | solution.py:27
  31.3 15.3 %collective-permute-start.13 = (bf16[2,256,512]{2,1,0:T(8,128)(2,1)S(1)}, bf16[2,256,512]{2,1,0:T(8,128)(2,1)S(1)}, u32[]{:S(2)}, u32[]{:S(2)}) collective-permute-start(bf16[2,256,512]{2,1,0:T(8,128)(2,1)S(1)} %place_rim.3), channel_id=1, source_target_pairs={{0,4},{4,8},{8,12},{12,0},{1,5},{5,9},{9,13},{13,1},{2,6},{6,10},{... | collective-permute-start | bytes 1572872 | tf_op jit(solution)/shard_map/ppermute | solution.py:27
  33.0 4.3 %copy-start = (f32[2,2,256,512]{3,2,1,0:T(8,128)S(1)}, f32[2,2,256,512]{3,2,1,0:T(8,128)}, u32[]{:S(2)}) copy-start(f32[2,2,256,512]{3,2,1,0:T(8,128)} %param.7) | copy-start | bytes 6291460
  33.0 6.2 %collective-permute-start.9 = (bf16[128,256]{1,0:T(8,128)(2,1)S(1)}, bf16[128,256]{1,0:T(8,128)(2,1)S(1)}, u32[]{:S(2)}, u32[]{:S(2)}) collective-permute-start(bf16[128,256]{1,0:T(8,128)(2,1)S(1)} %get-tuple-element.52), channel_id=1, source_target_pairs={{0,2},{1,3},{2,0},{3,1},{4,6},{5,7},{6,4},{7,5},{8,10},{9,11},{10,... | collective-permute-start | bytes 196616 | tf_op jit(solution)/shard_map/ppermute | solution.py:22
  35.7 6.2 %collective-permute-start.8 = (bf16[128,256]{1,0:T(8,128)(2,1)S(1)}, bf16[128,256]{1,0:T(8,128)(2,1)S(1)}, u32[]{:S(2)}, u32[]{:S(2)}) collective-permute-start(bf16[128,256]{1,0:T(8,128)(2,1)S(1)} %get-tuple-element.52), channel_id=1, source_target_pairs={{0,3},{1,2},{2,1},{3,0},{4,7},{5,6},{6,5},{7,4},{8,11},{9,10},{10,... | collective-permute-start | bytes 196616 | tf_op jit(solution)/shard_map/ppermute | solution.py:22
  37.0 5.0 %collective-permute-start.7 = (bf16[128,256]{1,0:T(8,128)(2,1)S(1)}, bf16[128,256]{1,0:T(8,128)(2,1)S(1)}, u32[]{:S(2)}, u32[]{:S(2)}) collective-permute-start(bf16[128,256]{1,0:T(8,128)(2,1)S(1)} %get-tuple-element.52), channel_id=1, source_target_pairs={{0,1},{1,0},{2,3},{3,2},{4,5},{5,4},{6,7},{7,6},{8,9},{9,8},{10,11... | collective-permute-start | bytes 196616 | tf_op jit(solution)/shard_map/ppermute | solution.py:22
  42.0 4.5 %collective-permute-start.10 = (bf16[128,256]{1,0:T(8,128)(2,1)S(1)}, bf16[128,256]{1,0:T(8,128)(2,1)S(1)}, u32[]{:S(2)}, u32[]{:S(2)}) collective-permute-start(bf16[128,256]{1,0:T(8,128)(2,1)S(1)} %full_sum.1.mine_ref), channel_id=1, source_target_pairs={{0,8},{4,12},{8,0},{12,4},{1,9},{5,13},{9,1},{13,5},{2,10},{6,14},... | collective-permute-start | bytes 196616 | tf_op jit(solution)/shard_map/ppermute | solution.py:22
  46.5 1.4 %collective-permute-start.12 = (bf16[256,256]{1,0:T(8,128)(2,1)S(1)}, bf16[256,256]{1,0:T(8,128)(2,1)S(1)}, u32[]{:S(2)}, u32[]{:S(2)}) collective-permute-start(bf16[256,256]{1,0:T(8,128)(2,1)S(1)} %gather_half.1.mine_ref), channel_id=1, source_target_pairs={{0,4},{4,0},{8,12},{12,8},{1,5},{5,1},{9,13},{13,9},{2,6},{6,2},{1... | collective-permute-start | bytes 393224 | tf_op jit(solution)/shard_map/ppermute | solution.py:22

commit v5 on v3

--- a/solution.py
+++ b/solution.py
@@ -122,7 +122,7 @@
 
 
 def own_kernel(slab_hbm, own_ref, wide_ref, sems):
-    parts = [(c, rows) for c in range(own_ref.shape[0]) for rows in chunks(own_ref.shape[1], 64)]
+    parts = [(c, rows) for c in range(own_ref.shape[0]) for rows in chunks(own_ref.shape[1], 256)]
     copies = [
         pltpu.make_async_copy(slab_hbm.at[c, rows], wide_ref.at[c, rows], sems.at[i])
         for i, (c, rows) in enumerate(parts)
@@ -434,7 +434,7 @@
         out_shape=kept(tile, jnp.bfloat16),
         scratch_shapes=[
             pltpu.VMEM(tile, jnp.float32),
-            pltpu.SemaphoreType.DMA((pair_count * len(chunks(height, 64)),)),
+            pltpu.SemaphoreType.DMA((pair_count * len(chunks(height, 256)),)),
         ],
         compiler_params=pltpu.CompilerParams(vmem_limit_bytes=SMALL_VMEM),
         name="own_zero",

time: 49.1 us -> 49 us (level)
  no operation moved by 1% of the time
where the time goes in v5:
time: 49 us; the launch traced here: 48.8 us
  Pallas kernels  21.8 us (44%)
  starting transfers between devices  14.9 us (30%)
  waiting for transfers between devices  11.2 us (23%)
  between operations  0.82 us (2%)
    ppermute x10, starting transfers between devices, permute_pairs(): lax.ppermute(block, axis, [(i, partner(i)) for i in range(lax.axis_size(a...  10.8 us
    ppermute x4, waiting for transfers between devices, around(): lax.ppermute(block, axis, [(i, (i + distance) % size) for i in range(size)])  6.07 us
    ppermute x10, waiting for transfers between devices, permute_pairs(): lax.ppermute(block, axis, [(i, partner(i)) for i in range(lax.axis_size(a...  5.11 us
    pallas_call x1, Pallas kernels, per_device(): call(functools.partial(third_kernel, steps=row_count // count), [whole(pl...  4.24 us
    ppermute x4, starting transfers between devices, around(): lax.ppermute(block, axis, [(i, (i + distance) % size) for i in range(size)])  4.07 us
    pallas_call x1, Pallas kernels, per_device(): call(first_kernel, [spot_block, own_block, rim_block, whole(plane), whole...  3.98 us
    pallas_call x1, Pallas kernels, per_device(): call(second_kernel, [spot_block, own_block, rim_block, wide_block, tables...  2.71 us
    pallas_call x1, Pallas kernels, per_device(): pl.pallas_call(prepare_kernel, in_specs=[smem, smem, vmem, hbm, hbm, vmem...  2.37 us
  transfers between devices with their start and end apart: 14, of which 8 were waited for; matrix products, arithmetic and copies ran while one was open for 0% of the time, Pallas kernels for 31%

profile of v5, /device:TPU:0, one launch (start us, length us, event | category | flops | bytes accessed | tf_op | source)
XLA Modules:
  0.0 48.8 jit_solution(2637007022202655702)
XLA Ops:
  0.6 0.0 copy-start.5
  0.6 0.0 copy-start.3
  0.7 0.0 copy-start.1
  0.7 0.0 copy-start.2
  0.7 1.3 %own_zero.1.own_ref = bf16[2,256,512]{2,1,0:T(8,128)(2,1)S(1)} custom-call(f32[4,256,512]{2,1,0:T(8,128)} %bitcast.4), custom_call_target="tpu_custom_call" | custom-call | tf_op jit(solution)/shard_map/own_zero/pallas_call | solution.py:430
  2.0 0.0 copy-start.4
  2.0 2.4 %collective-permute-start = (bf16[2,256,512]{2,1,0:T(8,128)(2,1)S(1)}, bf16[2,256,512]{2,1,0:T(8,128)(2,1)S(1)}, u32[]{:S(2)}, u32[]{:S(2)}) collective-permute-start(bf16[2,256,512]{2,1,0:T(8,128)(2,1)S(1)} %own_zero.1.own_ref), channel_id=1, source_target_pairs={{0,12},{4,0},{8,4},{12,8},{1,13},{5,1},{9,5},{13,9},{2,14},{6,2},{... | collective-permute-start | bytes 1572872 | tf_op jit(solution)/shard_map/ppermute | solution.py:27
  4.4 0.0 copy-done.5
  4.4 0.1 copy.10.corner_ref
  4.5 0.0 copy-done.3
  4.5 0.0 copy-done.1
  4.5 0.0 copy-done.2
  4.5 2.4 %prepare.1 = (bf16[2,256,512]{2,1,0:T(8,128)(2,1)S(1)}, bf16[512,512]{1,0:T(8,128)(2,1)S(1)}, f32[2,256,256]{2,1,0:T(8,128)S(1)}, s32[4,2,8,128]{3,2,1,0:T(8,128...) custom-call(s32[4,2]{1,0:T(4,128)S(1)} %copy.10.corner_ref, ...), custom_call_target="tpu_custom_call" | custom-call | tf_op jit(solution)/shard_map/prepare/pallas_call | solution.py:443
  6.9 0.7 %collective-permute-start.1 = (bf16[2,256,512]{2,1,0:T(8,128)(2,1)S(1)}, bf16[2,256,512]{2,1,0:T(8,128)(2,1)S(1)}, u32[]{:S(2)}, u32[]{:S(2)}) collective-permute-start(bf16[2,256,512]{2,1,0:T(8,128)(2,1)S(1)} %get-tuple-element.36.own_ref), channel_id=1, source_target_pairs={{0,12},{4,0},{8,4},{12,8},{1,13},{5,1},{9,5},{13,9},{2,14},{6,2},{... | collective-permute-start | bytes 1572872 | tf_op jit(solution)/shard_map/ppermute | solution.py:27
  7.6 0.0 collective-permute-start.2
  7.6 0.5 collective-permute-start.3
  8.1 1.4 %collective-permute-start.4 = (bf16[256,256]{1,0:T(8,128)(2,1)S(1)}, bf16[256,256]{1,0:T(8,128)(2,1)S(1)}, u32[]{:S(2)}, u32[]{:S(2)}) collective-permute-start(bf16[256,256]{1,0:T(8,128)(2,1)S(1)} %get-tuple-element.43), channel_id=1, source_target_pairs={{0,12},{4,8},{8,4},{12,0},{1,13},{5,9},{9,5},{13,1},{2,14},{6,10},... | collective-permute-start | bytes 393224 | tf_op jit(solution)/shard_map/ppermute | solution.py:22
  9.5 4.1 %collective-permute-done.rim_ref = bf16[2,256,512]{2,1,0:T(8,128)(2,1)S(1)} collective-permute-done((bf16[2,256,512]{2,1,0:T(8,128)(2,1)S(1)}, bf16[2,256,512]{2,1,0:T(8,128)(2,1)S(1)}, u32[]{:S(2)}, u32[]{:S(2)}) %collective-permute-start) | collective-permute-done | bytes 524320 | tf_op jit(solution)/shard_map/ppermute | solution.py:27
  13.7 0.0 copy-done.4
  13.7 4.0 %moved.1 = (bf16[4,2,256,256]{3,2,1,0:T(8,128)(2,1)S(1)}, f32[4,256,512]{2,1,0:T(8,128)S(1)}) custom-call(s32[8,128]{1,0:T(8,128)S(1)} %get-tuple-element.34.spot_ref, bf16[2,256,512]{2,1,0:T(8,128)(2,1)S(1)} %own_zero.1.own_ref, bf16[2,256,512]{2,1,0:T(8,128)(2,1)S(1)} %collective-permute-done.rim_ref, f32[2,256,256]{2,1,0:T(8,128)S(1)} %copy-done.4, ...), custom_call_target="tpu_custom_call" | custom-call | flops 3758096384 | bytes 2097152 | tf_op jit(solution)/shard_map/moved/pallas_call | solution.py:501
  17.6 1.9 %collective-permute-done.1.rim_ref = bf16[2,256,512]{2,1,0:T(8,128)(2,1)S(1)} collective-permute-done((bf16[2,256,512]{2,1,0:T(8,128)(2,1)S(1)}, bf16[2,256,512]{2,1,0:T(8,128)(2,1)S(1)}, u32[]{:S(2)}, u32[]{:S(2)}) %collective-permute-start.1) | collective-permute-done | bytes 524320 | tf_op jit(solution)/shard_map/ppermute | solution.py:27
  19.6 2.7 %far.1 = (bf16[4,2,256,256]{3,2,1,0:T(8,128)(2,1)S(1)}, f32[4,256,512]{2,1,0:T(8,128)S(1)}) custom-call(s32[8,128]{1,0:T(8,128)S(1)} %get-tuple-element.34.spot_ref, bf16[2,256,512]{2,1,0:T(8,128)(2,1)S(1)} %get-tuple-element.36.own_ref, bf16[2,256,512]{2,1,0:T(8,128)(2,1)S(1)} %collective-permute-done.1.rim_ref, ...), custom_call_target="tpu_custom_call" | custom-call | flops 2684354560 | bytes 2097152 | tf_op jit(solution)/shard_map/far/pallas_call | solution.py:513
  22.3 0.0 collective-permute-done.2.rest_1_
  22.3 0.0 collective-permute-done.3.rest_2_
  22.3 0.1 collective-permute-done.4.rest_3_
  22.4 4.2 %gradients.1 = (bf16[4,4,256,256]{3,2,1,0:T(8,128)(2,1)S(1)}, f32[256,256]{1,0:T(8,128)S(1)}, bf16[256,256]{1,0:T(8,128)(2,1)S(1)}) custom-call(f32[2,256,256]{2,1,0:T(8,128)S(1)} %copy-done.4, f32[2,256,256]{2,1,0:T(8,128)S(1)} %get-tuple-element.32.kernel_ref, bf16[512,512]{1,0:T(8,128)(2,1)S(1)} %get-tuple-element.33.table_ref, ...), custom_call_target="tpu_custom_call" | custom-call | flops 3221225472 | bytes 2097152 | tf_op jit(solution)/shard_map/gradients/pallas_call | solution.py:523
  26.6 0.9 %collective-permute-start.5 = (bf16[256,256]{1,0:T(8,128)(2,1)S(1)}, bf16[256,256]{1,0:T(8,128)(2,1)S(1)}, u32[]{:S(2)}, u32[]{:S(2)}) collective-permute-start(bf16[256,256]{1,0:T(8,128)(2,1)S(1)} %get-tuple-element.45), channel_id=1, source_target_pairs={{0,4},{4,0},{8,12},{12,8},{1,5},{5,1},{9,13},{13,9},{2,6},{6,2},{1... | collective-permute-start | bytes 393224 | tf_op jit(solution)/shard_map/ppermute | solution.py:22
  27.5 1.1 %place_rim.2 = bf16[2,256,512]{2,1,0:T(8,128)(2,1)S(1)} custom-call(s32[4,2,8,128]{3,2,1,0:T(8,128)S(1)} %get-tuple-element.46.corner_ref, bf16[4,4,256,256]{3,2,1,0:T(8,128)(2,1)S(1)} %get-tuple-element.47.grad_ref), custom_call_target="tpu_custom_call" | custom-call | flops 805306368 | bytes 2097152 | tf_op jit(solution)/shard_map/place_rim/pallas_call | solution.py:541
  28.7 0.0 collective-permute-done.5.other_ref
  28.7 1.5 %collective-permute-start.6 = (bf16[128,256]{1,0:T(8,128)(2,1)S(1)}, bf16[128,256]{1,0:T(8,128)(2,1)S(1)}, u32[]{:S(2)}, u32[]{:S(2)}) collective-permute-start(bf16[128,256]{1,0:T(8,128)(2,1)S(1)} %get-tuple-element.50), channel_id=1, source_target_pairs={{0,8},{4,12},{8,0},{12,4},{1,9},{5,13},{9,1},{13,5},{2,10},{6,14},... | collective-permute-start | bytes 196616 | tf_op jit(solution)/shard_map/ppermute | solution.py:22
  30.2 0.0 collective-permute-start.11
  30.2 1.1 %place_rim.3 = bf16[2,256,512]{2,1,0:T(8,128)(2,1)S(1)} custom-call(s32[4,2,8,128]{3,2,1,0:T(8,128)S(1)} %get-tuple-element.46.corner_ref, bf16[4,4,256,256]{3,2,1,0:T(8,128)(2,1)S(1)} %get-tuple-element.47.grad_ref), custom_call_target="tpu_custom_call" | custom-call | flops 805306368 | bytes 2097152 | tf_op jit(solution)/shard_map/place_rim/pallas_call | solution.py:541
  31.4 0.9 %collective-permute-start.13 = (bf16[2,256,512]{2,1,0:T(8,128)(2,1)S(1)}, bf16[2,256,512]{2,1,0:T(8,128)(2,1)S(1)}, u32[]{:S(2)}, u32[]{:S(2)}) collective-permute-start(bf16[2,256,512]{2,1,0:T(8,128)(2,1)S(1)} %place_rim.3), channel_id=1, source_target_pairs={{0,4},{4,8},{8,12},{12,0},{1,5},{5,9},{9,13},{13,1},{2,6},{6,10},{... | collective-permute-start | bytes 1572872 | tf_op jit(solution)/shard_map/ppermute | solution.py:27
  32.3 0.8 %collective-permute-done.6.rest_0_ = bf16[128,256]{1,0:T(8,128)(2,1)S(1)} collective-permute-done((bf16[128,256]{1,0:T(8,128)(2,1)S(1)}, bf16[128,256]{1,0:T(8,128)(2,1)S(1)}, u32[]{:S(2)}, u32[]{:S(2)}) %collective-permute-start.6) | collective-permute-done | bytes 65568 | tf_op jit(solution)/shard_map/ppermute | solution.py:22
  33.1 0.0 copy-start
  33.1 2.7 %collective-permute-start.9 = (bf16[128,256]{1,0:T(8,128)(2,1)S(1)}, bf16[128,256]{1,0:T(8,128)(2,1)S(1)}, u32[]{:S(2)}, u32[]{:S(2)}) collective-permute-start(bf16[128,256]{1,0:T(8,128)(2,1)S(1)} %get-tuple-element.52), channel_id=1, source_target_pairs={{0,2},{1,3},{2,0},{3,1},{4,6},{5,7},{6,4},{7,5},{8,10},{9,11},{10,... | collective-permute-start | bytes 196616 | tf_op jit(solution)/shard_map/ppermute | solution.py:22
  35.7 1.3 %collective-permute-start.8 = (bf16[128,256]{1,0:T(8,128)(2,1)S(1)}, bf16[128,256]{1,0:T(8,128)(2,1)S(1)}, u32[]{:S(2)}, u32[]{:S(2)}) collective-permute-start(bf16[128,256]{1,0:T(8,128)(2,1)S(1)} %get-tuple-element.52), channel_id=1, source_target_pairs={{0,3},{1,2},{2,1},{3,0},{4,7},{5,6},{6,5},{7,4},{8,11},{9,10},{10,... | collective-permute-start | bytes 196616 | tf_op jit(solution)/shard_map/ppermute | solution.py:22
  37.1 0.2 collective-permute-start.7
  37.3 0.0 copy-done
  37.3 1.9 %place.1.part_ref = f32[4,256,512]{2,1,0:T(8,128)S(1)} custom-call(s32[4,2,8,128]{3,2,1,0:T(8,128)S(1)} %get-tuple-element.46.corner_ref, bf16[4,4,256,256]{3,2,1,0:T(8,128)(2,1)S(1)} %get-tuple-element.47.grad_ref, f32[4,256,512]{2,1,0:T(8,128)S(1)} %bitcast.6), custom_call_target="tpu_custom_call" | custom-call | flops 1610612736 | bytes 2097152 | tf_op jit(solution)/shard_map/place/pallas_call | solution.py:551
  39.2 0.0 collective-permute-done.9.rest_2_
  39.3 2.6 %collective-permute-done.8.rest_1_ = bf16[128,256]{1,0:T(8,128)(2,1)S(1)} collective-permute-done((bf16[128,256]{1,0:T(8,128)(2,1)S(1)}, bf16[128,256]{1,0:T(8,128)(2,1)S(1)}, u32[]{:S(2)}, u32[]{:S(2)}) %collective-permute-start.8) | collective-permute-done | bytes 65568 | tf_op jit(solution)/shard_map/ppermute | solution.py:22
  41.9 0.1 collective-permute-done.7.rest_0_
  42.1 2.2 %collective-permute-start.10 = (bf16[128,256]{1,0:T(8,128)(2,1)S(1)}, bf16[128,256]{1,0:T(8,128)(2,1)S(1)}, u32[]{:S(2)}, u32[]{:S(2)}) collective-permute-start(bf16[128,256]{1,0:T(8,128)(2,1)S(1)} %full_sum.1.mine_ref), channel_id=1, source_target_pairs={{0,8},{4,12},{8,0},{12,4},{1,9},{5,13},{9,1},{13,5},{2,10},{6,14},... | collective-permute-start | bytes 196616 | tf_op jit(solution)/shard_map/ppermute | solution.py:22
  44.3 0.0 collective-permute-done.11.rim_ref
  44.3 1.0 %finish.2.rest_0_ = f32[4,256,512]{2,1,0:T(8,128)} custom-call(f32[4,256,512]{2,1,0:T(8,128)S(1)} %place.1.part_ref, bf16[2,256,512]{2,1,0:T(8,128)(2,1)S(1)} %collective-permute-done.11.rim_ref), custom_call_target="tpu_custom_call" | custom-call | tf_op jit(solution)/shard_map/finish/pallas_call | solution.py:564
  45.3 1.2 %collective-permute-done.10.rest_0_ = bf16[128,256]{1,0:T(8,128)(2,1)S(1)} collective-permute-done((bf16[128,256]{1,0:T(8,128)(2,1)S(1)}, bf16[128,256]{1,0:T(8,128)(2,1)S(1)}, u32[]{:S(2)}, u32[]{:S(2)}) %collective-permute-start.10) | collective-permute-done | bytes 65568 | tf_op jit(solution)/shard_map/ppermute | solution.py:22
  46.6 0.1 collective-permute-start.12
  46.6 0.0 collective-permute-done.13.rim_ref
  46.6 1.0 %finish.3 = f32[4,256,512]{2,1,0:T(8,128)} custom-call(f32[4,256,512]{2,1,0:T(8,128)S(1)} %place.1.part_ref, bf16[2,256,512]{2,1,0:T(8,128)(2,1)S(1)} %collective-permute-done.13.rim_ref, f32[4,256,512]{2,1,0:T(8,128)} %finish.2.rest_0_), custom_call_target="tpu_custom_call", output_to_operand_aliasing={{}: (2, {})} | custom-call | tf_op jit(solution)/shard_map/finish/pallas_call | solution.py:564
  47.7 0.3 collective-permute-done.12.other_ref
  48.0 0.9 %update_probe.1 = f32[2,256,256]{2,1,0:T(8,128)} custom-call(f32[2,256,256]{2,1,0:T(8,128)S(1)} %copy-done.4, bf16[256,256]{1,0:T(8,128)(2,1)S(1)} %gather_half.1.mine_ref, bf16[256,256]{1,0:T(8,128)(2,1)S(1)} %collective-permute-done.12.other_ref), custom_call_target="tpu_custom_call" | custom-call | flops 1500000000 | bytes 262144 | tf_op jit(solution)/shard_map/update_probe/pallas_call | solution.py:365
  (4 shorter events, 0.1 us)
Async XLA Ops:
  0.6 3.8 %copy-start.5 = (s32[4,1,2]{0,2,1:T(2,128)S(1)}, s32[4,1,2]{0,2,1:T(2,128)}, u32[]{:S(2)}) copy-start(s32[4,1,2]{0,2,1:T(2,128)} %param.11) | copy-start | bytes 100
  0.6 3.9 %copy-start.3 = (s32[2,1]{0,1:T(1,128)S(1)}, s32[2,1]{0,1:T(1,128)}, u32[]{:S(2)}) copy-start(s32[2,1]{0,1:T(1,128)} %param.12) | copy-start | bytes 28
  0.7 3.9 %copy-start.1 = (f32[2,256,256]{2,1,0:T(8,128)S(1)}, f32[2,256,256]{2,1,0:T(8,128)}, u32[]{:S(2)}) copy-start(f32[2,256,256]{2,1,0:T(8,128)} %intensity_ref.1) | copy-start | bytes 1572868
  0.7 3.9 %copy-start.2 = (f32[256,256]{1,0:T(8,128)S(1)}, f32[256,256]{1,0:T(8,128)}, u32[]{:S(2)}) copy-start(f32[256,256]{1,0:T(8,128)} %phase_ref.1) | copy-start | bytes 786436
  2.0 11.7 %copy-start.4 = (f32[2,256,256]{2,1,0:T(8,128)S(1)}, f32[2,256,256]{2,1,0:T(8,128)}, u32[]{:S(2)}) copy-start(f32[2,256,256]{2,1,0:T(8,128)} %probe_ref.5) | copy-start | bytes 1572868
  2.0 11.6 %collective-permute-start = (bf16[2,256,512]{2,1,0:T(8,128)(2,1)S(1)}, bf16[2,256,512]{2,1,0:T(8,128)(2,1)S(1)}, u32[]{:S(2)}, u32[]{:S(2)}) collective-permute-start(bf16[2,256,512]{2,1,0:T(8,128)(2,1)S(1)} %own_zero.1.own_ref), channel_id=1, source_target_pairs={{0,12},{4,0},{8,4},{12,8},{1,13},{5,1},{9,5},{13,9},{2,14},{6,2},{... | collective-permute-start | bytes 1572872 | tf_op jit(solution)/shard_map/ppermute | solution.py:27
  6.9 12.6 %collective-permute-start.1 = (bf16[2,256,512]{2,1,0:T(8,128)(2,1)S(1)}, bf16[2,256,512]{2,1,0:T(8,128)(2,1)S(1)}, u32[]{:S(2)}, u32[]{:S(2)}) collective-permute-start(bf16[2,256,512]{2,1,0:T(8,128)(2,1)S(1)} %get-tuple-element.36.own_ref), channel_id=1, source_target_pairs={{0,12},{4,0},{8,4},{12,8},{1,13},{5,1},{9,5},{13,9},{2,14},{6,2},{... | collective-permute-start | bytes 1572872 | tf_op jit(solution)/shard_map/ppermute | solution.py:27
  7.6 14.6 %collective-permute-start.2 = (bf16[256,256]{1,0:T(8,128)(2,1)S(1)}, bf16[256,256]{1,0:T(8,128)(2,1)S(1)}, u32[]{:S(2)}, u32[]{:S(2)}) collective-permute-start(bf16[256,256]{1,0:T(8,128)(2,1)S(1)} %get-tuple-element.41), channel_id=1, source_target_pairs={{0,4},{4,0},{8,12},{12,8},{1,5},{5,1},{9,13},{13,9},{2,6},{6,2},{1... | collective-permute-start | bytes 393224 | tf_op jit(solution)/shard_map/ppermute | solution.py:22
  7.6 14.7 %collective-permute-start.3 = (bf16[256,256]{1,0:T(8,128)(2,1)S(1)}, bf16[256,256]{1,0:T(8,128)(2,1)S(1)}, u32[]{:S(2)}, u32[]{:S(2)}) collective-permute-start(bf16[256,256]{1,0:T(8,128)(2,1)S(1)} %get-tuple-element.42), channel_id=1, source_target_pairs={{0,8},{4,12},{8,0},{12,4},{1,9},{5,13},{9,1},{13,5},{2,10},{6,14},... | collective-permute-start | bytes 393224 | tf_op jit(solution)/shard_map/ppermute | solution.py:22
  8.1 14.3 %collective-permute-start.4 = (bf16[256,256]{1,0:T(8,128)(2,1)S(1)}, bf16[256,256]{1,0:T(8,128)(2,1)S(1)}, u32[]{:S(2)}, u32[]{:S(2)}) collective-permute-start(bf16[256,256]{1,0:T(8,128)(2,1)S(1)} %get-tuple-element.43), channel_id=1, source_target_pairs={{0,12},{4,8},{8,4},{12,0},{1,13},{5,9},{9,5},{13,1},{2,14},{6,10},... | collective-permute-start | bytes 393224 | tf_op jit(solution)/shard_map/ppermute | solution.py:22
  26.6 2.0 %collective-permute-start.5 = (bf16[256,256]{1,0:T(8,128)(2,1)S(1)}, bf16[256,256]{1,0:T(8,128)(2,1)S(1)}, u32[]{:S(2)}, u32[]{:S(2)}) collective-permute-start(bf16[256,256]{1,0:T(8,128)(2,1)S(1)} %get-tuple-element.45), channel_id=1, source_target_pairs={{0,4},{4,0},{8,12},{12,8},{1,5},{5,1},{9,13},{13,9},{2,6},{6,2},{1... | collective-permute-start | bytes 393224 | tf_op jit(solution)/shard_map/ppermute | solution.py:22
  28.7 4.3 %collective-permute-start.6 = (bf16[128,256]{1,0:T(8,128)(2,1)S(1)}, bf16[128,256]{1,0:T(8,128)(2,1)S(1)}, u32[]{:S(2)}, u32[]{:S(2)}) collective-permute-start(bf16[128,256]{1,0:T(8,128)(2,1)S(1)} %get-tuple-element.50), channel_id=1, source_target_pairs={{0,8},{4,12},{8,0},{12,4},{1,9},{5,13},{9,1},{13,5},{2,10},{6,14},... | collective-permute-start | bytes 196616 | tf_op jit(solution)/shard_map/ppermute | solution.py:22
  30.2 14.1 %collective-permute-start.11 = (bf16[2,256,512]{2,1,0:T(8,128)(2,1)S(1)}, bf16[2,256,512]{2,1,0:T(8,128)(2,1)S(1)}, u32[]{:S(2)}, u32[]{:S(2)}) collective-permute-start(bf16[2,256,512]{2,1,0:T(8,128)(2,1)S(1)} %place_rim.2), channel_id=1, source_target_pairs={{0,4},{4,8},{8,12},{12,0},{1,5},{5,9},{9,13},{13,1},{2,6},{6,10},{... | collective-permute-start | bytes 1572872 | tf_op jit(solution)/shard_map/ppermute | solution.py:27
  31.4 15.3 %collective-permute-start.13 = (bf16[2,256,512]{2,1,0:T(8,128)(2,1)S(1)}, bf16[2,256,512]{2,1,0:T(8,128)(2,1)S(1)}, u32[]{:S(2)}, u32[]{:S(2)}) collective-permute-start(bf16[2,256,512]{2,1,0:T(8,128)(2,1)S(1)} %place_rim.3), channel_id=1, source_target_pairs={{0,4},{4,8},{8,12},{12,0},{1,5},{5,9},{9,13},{13,1},{2,6},{6,10},{... | collective-permute-start | bytes 1572872 | tf_op jit(solution)/shard_map/ppermute | solution.py:27
  33.1 4.3 %copy-start = (f32[2,2,256,512]{3,2,1,0:T(8,128)S(1)}, f32[2,2,256,512]{3,2,1,0:T(8,128)}, u32[]{:S(2)}) copy-start(f32[2,2,256,512]{3,2,1,0:T(8,128)} %param.7) | copy-start | bytes 6291460
  33.1 6.2 %collective-permute-start.9 = (bf16[128,256]{1,0:T(8,128)(2,1)S(1)}, bf16[128,256]{1,0:T(8,128)(2,1)S(1)}, u32[]{:S(2)}, u32[]{:S(2)}) collective-permute-start(bf16[128,256]{1,0:T(8,128)(2,1)S(1)} %get-tuple-element.52), channel_id=1, source_target_pairs={{0,2},{1,3},{2,0},{3,1},{4,6},{5,7},{6,4},{7,5},{8,10},{9,11},{10,... | collective-permute-start | bytes 196616 | tf_op jit(solution)/shard_map/ppermute | solution.py:22
  35.7 6.2 %collective-permute-start.8 = (bf16[128,256]{1,0:T(8,128)(2,1)S(1)}, bf16[128,256]{1,0:T(8,128)(2,1)S(1)}, u32[]{:S(2)}, u32[]{:S(2)}) collective-permute-start(bf16[128,256]{1,0:T(8,128)(2,1)S(1)} %get-tuple-element.52), channel_id=1, source_target_pairs={{0,3},{1,2},{2,1},{3,0},{4,7},{5,6},{6,5},{7,4},{8,11},{9,10},{10,... | collective-permute-start | bytes 196616 | tf_op jit(solution)/shard_map/ppermute | solution.py:22
  37.1 5.0 %collective-permute-start.7 = (bf16[128,256]{1,0:T(8,128)(2,1)S(1)}, bf16[128,256]{1,0:T(8,128)(2,1)S(1)}, u32[]{:S(2)}, u32[]{:S(2)}) collective-permute-start(bf16[128,256]{1,0:T(8,128)(2,1)S(1)} %get-tuple-element.52), channel_id=1, source_target_pairs={{0,1},{1,0},{2,3},{3,2},{4,5},{5,4},{6,7},{7,6},{8,9},{9,8},{10,11... | collective-permute-start | bytes 196616 | tf_op jit(solution)/shard_map/ppermute | solution.py:22
  42.1 4.5 %collective-permute-start.10 = (bf16[128,256]{1,0:T(8,128)(2,1)S(1)}, bf16[128,256]{1,0:T(8,128)(2,1)S(1)}, u32[]{:S(2)}, u32[]{:S(2)}) collective-permute-start(bf16[128,256]{1,0:T(8,128)(2,1)S(1)} %full_sum.1.mine_ref), channel_id=1, source_target_pairs={{0,8},{4,12},{8,0},{12,4},{1,9},{5,13},{9,1},{13,5},{2,10},{6,14},... | collective-permute-start | bytes 196616 | tf_op jit(solution)/shard_map/ppermute | solution.py:22
  46.6 1.4 %collective-permute-start.12 = (bf16[256,256]{1,0:T(8,128)(2,1)S(1)}, bf16[256,256]{1,0:T(8,128)(2,1)S(1)}, u32[]{:S(2)}, u32[]{:S(2)}) collective-permute-start(bf16[256,256]{1,0:T(8,128)(2,1)S(1)} %gather_half.1.mine_ref), channel_id=1, source_target_pairs={{0,4},{4,0},{8,12},{12,8},{1,5},{5,1},{9,13},{13,9},{2,6},{6,2},{1... | collective-permute-start | bytes 393224 | tf_op jit(solution)/shard_map/ppermute | solution.py:22
